TPU v7x, 256 devices: a whole 4x4x8 slice. The times are simulated.
256 devices in a mesh: grp: 8 (over y, core), mem: 32 (over x, z).
Axes of the slice: x: 4, y: 4, z: 8, core: 2. Of those that a mesh axis runs over, the one named last changes fastest.
Arguments:
- old_rows: bfloat16 [65536, 1024], P(('grp', 'mem')), may hold values from -24 to 24
- new_rows: bfloat16 [65536, 1024], P(('grp', 'mem')), may hold values from -6 to 6
- list_ids: int32 [65536], P(('grp', 'mem')), may hold values from 0 to 65535, as said below
- owner_map: int32 [65536], replicated, may hold values from 0 to 31, as said below
Outputs:
- owner_rows: float32 [131072, 1024], P(('grp', 'mem'))
- rotation: bfloat16 [1024, 1024], P('mem')
Inputs may be any that keep to these rules, and one draw needn't show every extreme that they name: `list_ids`: in each device's block of 256 rows, at most 16 rows belong to lists of any one owner; in every group some owner receives exactly 16 rows from every device of the group. `owner_map`: every owner holds 65536 // 32 lists.
All inputs are finite; a program needn't handle non-finite values.
Results may differ from a plain program's by a relative error of at most 0.023.
Values may be sent and summed in bfloat16 or wider, within the bound.
No kernel may reach another device: no remote copies, remote signals or barrier semaphores. Data moves between devices by JAX's collectives and lax.ppermute only.
A program may use at most 64 MiB of HBM per device.

v0:
```python
import math

import jax
import jax.numpy as jnp
from jax import lax
from jax.sharding import PartitionSpec as P

ITERS = 2


EPSILON = 1e-06
COEFF_ONE = 3.4445
COEFF_THREE = -4.775
COEFF_FIVE = 2.0315


def combine_terms(iterate, first, second):
    return (
        COEFF_ONE * iterate.astype(jnp.float32)
        + COEFF_THREE * first.astype(jnp.float32)
        + COEFF_FIVE * second
    ).astype(jnp.bfloat16)


def local(old_rows, new_rows, list_ids, owner_map):
    features = old_rows.shape[1]
    row_total = old_rows.shape[0]
    members = lax.axis_size("mem")
    block_rows = features // members
    scaling = 0.25 * math.sqrt(features)
    partial_value = jnp.dot(old_rows.T, new_rows, preferred_element_type=jnp.float32)
    covariance = lax.psum(partial_value, ("grp", "mem"))
    squares = jnp.sum(covariance * covariance)
    iterate = (covariance * scaling / jnp.sqrt(squares + EPSILON)).astype(jnp.bfloat16)
    for sweep in range(ITERS):
        gram = jnp.dot(iterate, iterate.T, preferred_element_type=jnp.float32).astype(jnp.bfloat16)
        first = jnp.dot(gram, iterate, preferred_element_type=jnp.float32).astype(jnp.bfloat16)
        second = jnp.dot(gram, first, preferred_element_type=jnp.float32)
        iterate = combine_terms(iterate, first, second)
    own_rows = lax.dynamic_slice_in_dim(iterate, lax.axis_index("mem") * block_rows, block_rows, 0)
    capacity = 2 * row_total // members
    owner_of_row = owner_map[list_ids]
    onehot = (owner_of_row[:, None] == jnp.arange(members, dtype=jnp.int32)[None, :]).astype(
        jnp.int32
    )
    earlier = jnp.cumsum(onehot, axis=0) - onehot
    slot_index = owner_of_row * capacity + jnp.sum(earlier * onehot, axis=1)
    payload = jnp.dot(old_rows, iterate, preferred_element_type=jnp.float32)
    buffer = jnp.zeros((members * capacity, features), jnp.float32).at[slot_index].set(payload)
    buffer = buffer.reshape(members, capacity, features)
    arrived = lax.all_to_all(buffer, "mem", split_axis=0, concat_axis=0, tiled=True).reshape(
        members * capacity, features
    )
    return (arrived, own_rows)


def solution(mesh):
    in_specs = (P(("grp", "mem"), None), P(("grp", "mem"), None), P(("grp", "mem")), P())
    out_specs = (P(("grp", "mem"), None), P("mem", None))
    return jax.shard_map(local, mesh=mesh, in_specs=in_specs, out_specs=out_specs, check_vma=False)
```

profile of v0, /device:TPU:1, one launch (start us, length us, event | category | flops | bytes accessed | tf_op | source)
XLA Modules:
  0.0 378.4 jit_solution(7004765975214528384)
XLA Ops:
  7.2 0.0 copy-start
  7.2 0.0 all-reduce.2.cloned.1.call-start
  7.2 1.0 copy-done
  8.2 3.8 fusion.8
  12.0 0.0 copy-start.3
  12.0 0.0 copy-start.2
  12.0 0.0 all-reduce.2.cloned.1.call-update
  12.0 0.7 copy-done.3
  12.7 0.3 copy-done.2
  12.9 1.7 gather_fusion
  14.7 0.6 reduce-window.6
  15.3 0.2 slice_reduce_fusion
  15.5 0.1 fusion.6
  15.6 268.6 %all-reduce.2.cloned.1.call-done = f32[1024,1024]{1,0:T(8,128)} async-done(((f32[1024,1024]{1,0:T(8,128)}), f32[1024,1024]{1,0:T(8,128)}) %all-reduce.2.cloned.1.call-update) | async-done | bytes 4194320 | tf_op jit(solution)/shard_map/psum | solution.py:32
  284.2 3.9 %multiply_reduce_fusion = f32[]{:T(128)} fusion(f32[1024,1024]{1,0:T(8,128)} %all-reduce.2.cloned.1.call-done), kind=kLoop, calls=%fused_computation.5 | loop fusion | flops 2097151 | bytes 4194308 | tf_op jit(solution)/shard_map/reduce_sum | solution.py:33
  288.8 2.8 divide_convert_fusion
  291.6 2.4 convolution_convert_fusion.1
  294.0 2.3 fusion.9
  296.3 2.6 add_convert_fusion.1
  298.9 2.4 convolution_convert_fusion
  301.3 2.3 fusion.10
  303.6 2.8 add_convert_fusion
  306.5 0.0 copy-start.1
  306.5 1.3 copy-done.1
  307.8 0.8 convolution_bitcast_fusion
  308.6 0.3 copy.8
  308.9 2.8 scatter_custom_fusion
  311.8 9.7 %all-to-all-start = ((f32[32,16,1024]{2,1,0:T(8,128)}), f32[32,16,1024]{2,1,0:T(8,128)S(1)}, u32[]{:S(2)}, u32[]{:S(2)}) async-start(f32[32,16,1024]{2,1,0:T(8,128)} %bitcast.43), calls=%async_computation | async-start | bytes 4194304 | tf_op jit(solution)/shard_map/all_to_all | solution.py:51
  321.5 1.5 constant_dynamic-slice_fusion
  322.9 47.3 %all-to-all-done = f32[32,16,1024]{2,1,0:T(8,128)S(1)} async-done(((f32[32,16,1024]{2,1,0:T(8,128)}), f32[32,16,1024]{2,1,0:T(8,128)S(1)}, u32[]{:S(2)}, u32[]{:S(2)}) %all-to-all-start) | async-done | bytes 2097184 | tf_op jit(solution)/shard_map/all_to_all | solution.py:51
  370.3 1.3 copy.13
  (7 shorter events, 0.1 us)
Async XLA Ops:
  7.2 1.0 copy-start
  7.2 277.1 %all-reduce.2.cloned.1.call-start = ((), (), s32[]{:S(2)}) async-start(), calls=%async_computation.1 | async-start | bytes 8388608 | tf_op jit(solution)/shard_map/psum | solution.py:32
  12.0 0.7 copy-start.3
  12.0 1.0 copy-start.2
  306.5 1.4 copy-start.1
  311.8 58.5 %all-to-all-start = ((f32[32,16,1024]{2,1,0:T(8,128)}), f32[32,16,1024]{2,1,0:T(8,128)S(1)}, u32[]{:S(2)}, u32[]{:S(2)}) async-start(f32[32,16,1024]{2,1,0:T(8,128)} %bitcast.43), calls=%async_computation | async-start | bytes 4194304 | tf_op jit(solution)/shard_map/all_to_all | solution.py:51
Sparse Core Ops, SparseCore 0:
  13.5 270.7 all-reduce.1
where the time goes:
time: 379 us; the launch traced here: 378 us
  waiting for transfers between devices  316 us (83%)
  matrix products  19.4 us (5%)
  between operations  14.9 us (4%)
  local copies, waits for them, and re-layouts  11.1 us (3%)
  starting transfers between devices  9.72 us (3%)
  other arithmetic  7.41 us (2%)
    psum x1, waiting for transfers between devices, local(): covariance = lax.psum(partial_value, ('grp', 'mem'))  269 us
    all_to_all x1, waiting for transfers between devices, local(): lax.all_to_all(buffer, 'mem', split_axis=0, concat_axis=0, tiled=True)  47.3 us
    all_to_all x1, starting transfers between devices, local(): lax.all_to_all(buffer, 'mem', split_axis=0, concat_axis=0, tiled=True)  9.68 us
  transfers between devices with their start and end apart: 2, of which 2 were waited for; matrix products, arithmetic and copies ran while one was open for 1% of the time, Pallas kernels for 0%

commit v1 on v0

v1 whole, which is shorter than its diff:
```python
import math

import jax
import jax.numpy as jnp
from jax import lax
from jax.sharding import Mesh
from jax.sharding import PartitionSpec as P

ITERS = 2

EPSILON = 1e-06
COEFF_ONE = 3.4445
COEFF_THREE = -4.775
COEFF_FIVE = 2.0315

ALL = ("y", "core", "x", "z")
MEM = ("x", "z")
F32 = jnp.float32
BF16 = jnp.bfloat16


def dot(a, b):
    return jnp.dot(a, b, preferred_element_type=F32)


def swap_core(value):
    return lax.ppermute(value, "core", [(0, 1), (1, 0)])


def exchange(value, axes):
    return lax.all_to_all(value, axes, split_axis=0, concat_axis=0, tiled=True)


def outgoing_rows(old_rows, list_ids, owner_map, members):
    row_total = old_rows.shape[0]
    capacity = 2 * row_total // members
    owner = owner_map[list_ids]
    index = jnp.arange(row_total, dtype=jnp.int32)
    earlier = (owner[:, None] == owner[None, :]) & (index[None, :] < index[:, None])
    target = owner * capacity + jnp.sum(earlier.astype(jnp.int32), axis=1)
    slots = jnp.arange(members * capacity, dtype=jnp.int32)
    place = (slots[:, None] == target[None, :]).astype(BF16)
    return dot(place, old_rows).astype(BF16)


def covariance_of(old_rows, new_rows):
    features = old_rows.shape[1]
    half = features // 2
    core = lax.axis_index("core")
    mine = lax.dynamic_slice_in_dim(new_rows, core * half, half, 1)
    theirs = lax.dynamic_slice_in_dim(new_rows, (1 - core) * half, half, 1)
    old_pair = swap_core(old_rows)
    new_pair = swap_core(theirs)
    part = (dot(old_rows.T, mine) + dot(old_pair.T, new_pair)).astype(BF16)
    planes = lax.axis_size("y") * lax.axis_size("x")
    block = features // planes
    arrived = exchange(part, ("y", "x")).reshape(planes, block, half)
    part = jnp.sum(arrived.astype(F32), axis=0).astype(BF16)
    depth = lax.axis_size("z")
    copies = jnp.broadcast_to(part[None], (depth, block, half))
    arrived = exchange(copies, "z")
    total = jnp.sum(arrived.astype(F32), axis=0).astype(BF16)
    copies = jnp.broadcast_to(total[None], (planes, block, half))
    own_half = exchange(copies, ("y", "x")).reshape(features, half)
    other_half = swap_core(own_half)
    low = jnp.where(core == 0, own_half, other_half)
    high = jnp.where(core == 0, other_half, own_half)
    return jnp.concatenate([low, high], axis=1)


def local(old_rows, new_rows, list_ids, owner_map):
    features = old_rows.shape[1]
    members = lax.axis_size(MEM)
    block_rows = features // members
    scaling = 0.25 * math.sqrt(features)
    sent = outgoing_rows(old_rows, list_ids, owner_map, members)
    received = exchange(sent, MEM)
    covariance = covariance_of(old_rows, new_rows).astype(F32)
    squares = jnp.sum(covariance * covariance)
    iterate = (covariance * scaling / jnp.sqrt(squares + EPSILON)).astype(BF16)
    for sweep in range(ITERS):
        gram = dot(iterate, iterate.T).astype(BF16)
        first = dot(gram, iterate).astype(BF16)
        second = dot(gram, first)
        iterate = (
            COEFF_ONE * iterate.astype(F32) + COEFF_THREE * first.astype(F32) + COEFF_FIVE * second
        ).astype(BF16)
    own_rows = lax.dynamic_slice_in_dim(iterate, lax.axis_index(MEM) * block_rows, block_rows, 0)
    return (dot(received, iterate), own_rows)


def solution(mesh):
    shape = mesh.shape
    grid = mesh.devices.reshape(shape["grp"] // 2, 2, 4, shape["mem"] // 4)
    fine = Mesh(grid, ALL)
    in_specs = (P(ALL, None), P(ALL, None), P(ALL), P())
    out_specs = (P(ALL, None), P(MEM, None))
    return jax.shard_map(local, mesh=fine, in_specs=in_specs, out_specs=out_specs, check_vma=False)
```

time: 379 us -> 115 us (0.30)
  waiting for transfers between devices: 316 us -> 7.76 us
  blocking collectives: 0 us -> 62.9 us
  between operations: 14.9 us -> 1.51 us
  local copies, waits for them, and re-layouts: 11.1 us -> 3.08 us
    psum x1 -> x0, waiting for transfers between devices: 269 us -> none  [local(): covariance = lax.psum(partial_value, ('grp', 'mem'))]
    all_to_all x0 -> x3, blocking collectives: none -> 62.9 us  [exchange(): return lax.all_to_all(value, axes, split_axis=0, concat_axis=0, tiled=True)]
    all_to_all x1, waiting for transfers between devices: 47.3 us -> 7.75 us  [exchange(): return lax.all_to_all(value, axes, split_axis=0, concat_axis=0, tiled=True)]
    ppermute x0 -> x3, starting transfers between devices: none -> 8.34 us  [swap_core(): return lax.ppermute(value, 'core', [(0, 1), (1, 0)])]
    all_to_all x1, starting transfers between devices: 9.68 us -> 4.84 us  [exchange(): return lax.all_to_all(value, axes, split_axis=0, concat_axis=0, tiled=True)]
    unnamed x9 -> x10, local copies, waits for them, and re-layouts: 4.58 us -> 0.03 us
    dot_general x8 -> x10, matrix products: 19.4 us -> 22.1 us  [dot(): return jnp.dot(a, b, preferred_element_type=F32)]
  transfers between devices with their start and end apart: 2 -> 4, of which waited for: 2 -> 1; matrix products, arithmetic and copies ran while one was open for 1% -> 20% of each run, Pallas kernels for 0% -> 0%
where the time goes in v1:
time: 115 us; the launch traced here: 114 us
  blocking collectives  62.9 us (55%)
  matrix products  22.1 us (19%)
  starting transfers between devices  13.2 us (11%)
  waiting for transfers between devices  7.76 us (7%)
  other arithmetic  3.78 us (3%)
  local copies, waits for them, and re-layouts  3.08 us (3%)
  between operations  1.51 us (1%)
    all_to_all x3, blocking collectives, exchange(): return lax.all_to_all(value, axes, split_axis=0, concat_axis=0, tiled=True)  62.9 us
    dot_general x10, matrix products, dot(): return jnp.dot(a, b, preferred_element_type=F32)  22.1 us
    ppermute x3, starting transfers between devices, swap_core(): return lax.ppermute(value, 'core', [(0, 1), (1, 0)])  8.34 us
    all_to_all x1, waiting for transfers between devices, exchange(): return lax.all_to_all(value, axes, split_axis=0, concat_axis=0, tiled=True)  7.75 us
    all_to_all x1, starting transfers between devices, exchange(): return lax.all_to_all(value, axes, split_axis=0, concat_axis=0, tiled=True)  4.84 us
  transfers between devices with their start and end apart: 4, of which 1 were waited for; matrix products, arithmetic and copies ran while one was open for 20% of the time, Pallas kernels for 0%

profile of v1, /device:TPU:1, one launch (start us, length us, event | category | flops | bytes accessed | tf_op | source)
XLA Modules:
  0.0 114.3 jit_solution(16214290542284251208)
XLA Ops:
  0.6 0.0 copy-start
  0.6 3.3 %collective-permute-start.1 = (bf16[256,1024]{1,0:T(8,128)(2,1)}, bf16[256,1024]{1,0:T(8,128)(2,1)S(1)}, u32[]{:S(2)}, u32[]{:S(2)}) collective-permute-start(bf16[256,1024]{1,0:T(8,128)(2,1)} %param.4), channel_id=1, source_target_pairs={{0,32},{32,0},{1,33},{33,1},{2,34},{34,2},{3,35},{35,3},{4,36},{36... | collective-permute-start | bytes 1572872 | tf_op jit(solution)/shard_map/ppermute | solution.py:27
  4.0 0.0 copy-done
  4.0 1.0 collective-permute-start
  5.0 1.5 %fusion.6 = f32[512,1024]{1,0:T(8,128)S(1)} fusion(bf16[256,1024]{1,0:T(8,128)(2,1)} %param.4, bf16[256,1024]{1,0:T(8,128)(2,1)S(1)} %copy-done, s32[]{:T(128)S(6)} %select_n.26), kind=kOutput, calls=%fused_computation.19 | convolution fusion | flops 268435456 | bytes 2883588 | tf_op jit(solution)/shard_map/dot_general | solution.py:23
  6.5 0.0 collective-permute-done
  6.6 0.0 collective-permute-done.1
  6.6 0.5 fusion.5
  7.0 0.5 copy.7
  7.6 21.6 %all_to_all.31 = bf16[16,64,512]{2,1,0:T(8,128)(2,1)S(1)} all-to-all(bf16[16,64,512]{2,1,0:T(8,128)(2,1)S(1)} %bitcast.24), channel_id=1, replica_groups=mesh['y'=4,'core'=2,'x'=4,'z'=8] {'y','x'}, dimensions={0} | all-to-all | bytes 2097152 | tf_op jit(solution)/shard_map/all_to_all | solution.py:31
  29.1 0.1 reduce_sum.43
  29.3 23.0 %all_to_all.32 = bf16[8,64,512]{2,1,0:T(8,128)(2,1)S(1)} all-to-all(bf16[8,64,512]{2,1,0:T(8,128)(2,1)S(1)} %broadcast_in_dim.7), channel_id=1, replica_groups=mesh['y'=4,'core'=2,'x'=4,'z'=8] {'z'}, dimensions={0} | all-to-all | bytes 1048576 | tf_op jit(solution)/shard_map/all_to_all | solution.py:31
  52.4 0.0 copy-start.4
  52.4 0.0 copy-start.2
  52.4 0.1 reduce_sum.44
  52.5 0.0 copy-start.3
  52.5 0.1 broadcast_in_dim.8
  52.6 18.3 %all_to_all.33 = bf16[16,64,512]{2,1,0:T(8,128)(2,1)S(1)} all-to-all(bf16[16,64,512]{2,1,0:T(8,128)(2,1)S(1)} %broadcast_in_dim.8), channel_id=1, replica_groups=mesh['y'=4,'core'=2,'x'=4,'z'=8] {'y','x'}, dimensions={0} | all-to-all | bytes 2097152 | tf_op jit(solution)/shard_map/all_to_all | solution.py:31
  70.8 0.0 copy-start.1
  70.8 4.0 %collective-permute-start.2 = (bf16[1024,512]{1,0:T(8,128)(2,1)S(1)}, bf16[1024,512]{1,0:T(8,128)(2,1)}, u32[]{:S(2)}, u32[]{:S(2)}) collective-permute-start(bf16[1024,512]{1,0:T(8,128)(2,1)S(1)} %bitcast.23), channel_id=1, source_target_pairs={{0,32},{32,0},{1,33},{33,1},{2,34},{34,2},{3,35},{35,3},{4,36},{36... | collective-permute-start | bytes 3145736 | tf_op jit(solution)/shard_map/ppermute | solution.py:27
  74.8 0.0 copy-done.4
  74.8 0.0 copy-done.2
  74.9 1.7 %gather_fusion = s32[256]{0:T(256)S(1)} fusion(s32[65536]{0:T(1024)S(1)} %copy-done.2, s32[1024]{0:T(1024)S(1)} %pad_clamp_fusion), kind=kCustom, calls=%fused_computation | custom fusion | bytes 3072 | tf_op jit(solution)/shard_map/gather | solution.py:37
  76.6 0.2 convert_reduce_fusion
  76.8 0.0 copy-done.3
  76.8 1.4 %convolution_convert_fusion.2 = bf16[512,1024]{1,0:T(8,128)(2,1)} fusion(bf16[256,1024]{1,0:T(8,128)(2,1)S(1)} %copy-done.3, s32[256]{0:T(256)S(1)} %multiply_add_fusion), kind=kOutput, calls=%fused_computation.14 | convolution fusion | flops 269090816 | bytes 1573888 | tf_op jit(solution)/shard_map/dot_general | solution.py:23
  78.2 0.0 copy-done.1
  78.2 4.8 %all-to-all-start = ((bf16[32,16,1024]{2,1,0:T(8,128)(2,1)}), bf16[32,16,1024]{2,1,0:T(8,128)(2,1)}, u32[]{:S(2)}, u32[]{:S(2)}) async-start(bf16[32,16,1024]{2,1,0:T(8,128)(2,1)} %bitcast), calls=%async_computation | async-start | bytes 2097152 | tf_op jit(solution)/shard_map/all_to_all | solution.py:31
  83.1 0.0 collective-permute-done.2
  83.1 1.7 %broadcast_select_fusion.1 = (bf16[1024,512]{1,0:T(8,128)(2,1)S(1)}, bf16[1024,512]{1,0:T(8,128)(2,1)S(1)}) fusion(bf16[1024,512]{1,0:T(8,128)(2,1)} %collective-permute-done.2, pred[]{:T(512)S(6)} %eq.36, bf16[16,64,512]{2,1,0:T(8,128)(2,1)} %copy-done.1), kind=kLoop, calls=%fused_computation.17 | loop fusion | flops 1048576 | bytes 4194305 | tf_op jit(solution)/shard_map/jit(_where)/select_n | solution.py:66
  84.8 1.7 %fusion.2 = f32[]{:T(128)} fusion(bf16[1024,512]{1,0:T(8,128)(2,1)S(1)} %get-tuple-element.3, bf16[1024,512]{1,0:T(8,128)(2,1)S(1)} %get-tuple-element.2), kind=kLoop, calls=%fused_computation.5 | loop fusion | flops 6291455 | bytes 2097156 | tf_op jit(solution)/shard_map/reduce_sum | solution.py:79
  87.1 2.4 %convolution_convert_fusion.1 = bf16[1024,1024]{1,0:T(8,128)(2,1)S(1)} fusion(f32[]{:T(128)S(6)} %sqrt.3, bf16[1024,512]{1,0:T(8,128)(2,1)S(1)} %get-tuple-element.3, bf16[1024,512]{1,0:T(8,128)(2,1)S(1)} %get-tuple-element.2), kind=kOutput, calls=%fused_computation.13 | convolution fusion | flops 2155872256 | bytes 4194308 | tf_op jit(solution)/shard_map/dot_general | solution.py:23
  89.5 2.4 %fusion.11 = bf16[1024,1024]{1,0:T(8,128)(2,1)S(1)} fusion(bf16[1024,1024]{1,0:T(8,128)(2,1)S(1)} %convolution_convert_fusion.1, f32[]{:T(128)S(6)} %sqrt.3, bf16[1024,512]{1,0:T(8,128)(2,1)S(1)} %get-tuple-element.3, bf16[1024,512]{1,0:T(8,128)(2,1)S(1)} %get-tuple-element.2), kind=kOutput, calls=%fused_computation.31 | convolution fusion | flops 2154823680 | bytes 6291460 | tf_op jit(solution)/shard_map/dot_general | solution.py:23
  91.9 2.8 %add_convert_fusion.1 = bf16[1024,1024]{1,0:T(8,128)(2,1)S(1)} fusion(bf16[1024,1024]{1,0:T(8,128)(2,1)S(1)} %convolution_convert_fusion.1, bf16[1024,1024]{1,0:T(8,128)(2,1)S(1)} %fusion.11, f32[]{:T(128)S(6)} %sqrt.3, bf16[1024,512]{1,0:T(8,128)(2,1)S(1)} %get-tuple-element.3, bf16[1024,512]{1,0:T(8,128)(2,1)S(1)} %get-tuple-element.2), kind=kOutput, calls=%fused_computation.7 | convolution fusion | flops 2163212288 | bytes 8388612 | tf_op jit(solution)/shard_map/dot_general | solution.py:23
  94.7 2.4 %convolution_convert_fusion = bf16[1024,1024]{1,0:T(8,128)(2,1)S(1)} fusion(bf16[1024,1024]{1,0:T(8,128)(2,1)S(1)} %add_convert_fusion.1), kind=kOutput, calls=%fused_computation.12 | convolution fusion | flops 2148532224 | bytes 4194304 | tf_op jit(solution)/shard_map/dot_general | solution.py:23
  97.1 2.3 %fusion.14 = bf16[1024,1024]{1,0:T(8,128)(2,1)S(1)} fusion(bf16[1024,1024]{1,0:T(8,128)(2,1)S(1)} %convolution_convert_fusion, bf16[1024,1024]{1,0:T(8,128)(2,1)S(1)} %add_convert_fusion.1), kind=kOutput, calls=%fused_computation.32 | convolution fusion | flops 2147483648 | bytes 6291456 | tf_op jit(solution)/shard_map/dot_general | solution.py:23
  99.4 2.6 %add_convert_fusion = bf16[1024,1024]{1,0:T(8,128)(2,1)S(1)} fusion(bf16[1024,1024]{1,0:T(8,128)(2,1)S(1)} %add_convert_fusion.1, bf16[1024,1024]{1,0:T(8,128)(2,1)S(1)} %convolution_convert_fusion, bf16[1024,1024]{1,0:T(8,128)(2,1)S(1)} %fusion.14), kind=kOutput, calls=%fused_computation.6 | convolution fusion | flops 2155872256 | bytes 8388608 | tf_op jit(solution)/shard_map/dot_general | solution.py:23
  102.1 7.8 %all-to-all-done = bf16[32,16,1024]{2,1,0:T(8,128)(2,1)} async-done(((bf16[32,16,1024]{2,1,0:T(8,128)(2,1)}), bf16[32,16,1024]{2,1,0:T(8,128)(2,1)}, u32[]{:S(2)}, u32[]{:S(2)}) %all-to-all-start) | async-done | bytes 1048608 | tf_op jit(solution)/shard_map/all_to_all | solution.py:31
  109.8 3.8 %fusion.15 = f32[512,1024]{1,0:T(8,128)} fusion(bf16[512,1024]{1,0:T(8,128)(2,1)} %bitcast.1, bf16[1024,1024]{1,0:T(8,128)(2,1)S(1)} %add_convert_fusion), kind=kOutput, calls=%fused_computation.33 | convolution fusion | flops 1073741824 | bytes 5242880 | tf_op jit(solution)/shard_map/dot_general | solution.py:23
  113.6 0.6 constant_dynamic-slice_fusion
  (5 shorter events, 0.1 us)
Async XLA Ops:
  0.6 3.3 %copy-start = (bf16[256,1024]{1,0:T(8,128)(2,1)S(1)}, bf16[256,1024]{1,0:T(8,128)(2,1)}, u32[]{:S(2)}) copy-start(bf16[256,1024]{1,0:T(8,128)(2,1)} %param.5) | copy-start | bytes 1572868
  0.6 5.9 %collective-permute-start.1 = (bf16[256,1024]{1,0:T(8,128)(2,1)}, bf16[256,1024]{1,0:T(8,128)(2,1)S(1)}, u32[]{:S(2)}, u32[]{:S(2)}) collective-permute-start(bf16[256,1024]{1,0:T(8,128)(2,1)} %param.4), channel_id=1, source_target_pairs={{0,32},{32,0},{1,33},{33,1},{2,34},{34,2},{3,35},{35,3},{4,36},{36... | collective-permute-start | bytes 1572872 | tf_op jit(solution)/shard_map/ppermute | solution.py:27
  4.0 2.5 %collective-permute-start = (bf16[256,512]{1,0:T(8,128)(2,1)S(1)}, bf16[256,512]{1,0:T(8,128)(2,1)S(1)}, u32[]{:S(2)}, u32[]{:S(2)}) collective-permute-start(bf16[256,512]{1,0:T(8,128)(2,1)S(1)} %constant_dynamic-slice_fusion.1), channel_id=1, source_target_pairs={{0,32},{32,0},{1,33},{33,1},{2,34},{34,2},{3,35},{35,3},{4,36},{36... | collective-permute-start | bytes 786440 | tf_op jit(solution)/shard_map/ppermute | solution.py:27
  52.4 22.5 %copy-start.4 = (s32[256]{0:T(256)S(1)}, s32[256]{0:T(256)}, u32[]{:S(2)}) copy-start(s32[256]{0:T(256)} %param.6) | copy-start | bytes 3076
  52.4 22.5 %copy-start.2 = (s32[65536]{0:T(1024)S(1)}, s32[65536]{0:T(1024)}, u32[]{:S(2)}) copy-start(s32[65536]{0:T(1024)} %param.7) | copy-start | bytes 786436
  52.5 24.3 %copy-start.3 = (bf16[256,1024]{1,0:T(8,128)(2,1)S(1)}, bf16[256,1024]{1,0:T(8,128)(2,1)}, u32[]{:S(2)}) copy-start(bf16[256,1024]{1,0:T(8,128)(2,1)} %param.4) | copy-start | bytes 1572868
  70.8 7.4 %copy-start.1 = (bf16[16,64,512]{2,1,0:T(8,128)(2,1)}, bf16[16,64,512]{2,1,0:T(8,128)(2,1)S(1)}, u32[]{:S(2)}) copy-start(bf16[16,64,512]{2,1,0:T(8,128)(2,1)S(1)} %all_to_all.33) | copy-start | bytes 3145732
  70.8 12.2 %collective-permute-start.2 = (bf16[1024,512]{1,0:T(8,128)(2,1)S(1)}, bf16[1024,512]{1,0:T(8,128)(2,1)}, u32[]{:S(2)}, u32[]{:S(2)}) collective-permute-start(bf16[1024,512]{1,0:T(8,128)(2,1)S(1)} %bitcast.23), channel_id=1, source_target_pairs={{0,32},{32,0},{1,33},{33,1},{2,34},{34,2},{3,35},{35,3},{4,36},{36... | collective-permute-start | bytes 3145736 | tf_op jit(solution)/shard_map/ppermute | solution.py:27
  78.2 31.6 %all-to-all-start = ((bf16[32,16,1024]{2,1,0:T(8,128)(2,1)}), bf16[32,16,1024]{2,1,0:T(8,128)(2,1)}, u32[]{:S(2)}, u32[]{:S(2)}) async-start(bf16[32,16,1024]{2,1,0:T(8,128)(2,1)} %bitcast), calls=%async_computation | async-start | bytes 2097152 | tf_op jit(solution)/shard_map/all_to_all | solution.py:31

commit v2 on v1

--- a/solution.py
+++ b/solution.py
@@ -13,8 +13,9 @@
 COEFF_THREE = -4.775
 COEFF_FIVE = 2.0315
 
-ALL = ("y", "core", "x", "z")
-MEM = ("x", "z")
+ALL = ("y", "core", "x", "zh", "zl")
+MEM = ("x", "zh", "zl")
+SPREAD = ("y", "x", "zl")
 F32 = jnp.float32
 BF16 = jnp.bfloat16
 
@@ -52,20 +53,30 @@
     old_pair = swap_core(old_rows)
     new_pair = swap_core(theirs)
     part = (dot(old_rows.T, mine) + dot(old_pair.T, new_pair)).astype(BF16)
-    planes = lax.axis_size("y") * lax.axis_size("x")
+    planes = lax.axis_size(SPREAD)
     block = features // planes
-    arrived = exchange(part, ("y", "x")).reshape(planes, block, half)
+    arrived = exchange(part, SPREAD).reshape(planes, block, half)
     part = jnp.sum(arrived.astype(F32), axis=0).astype(BF16)
-    depth = lax.axis_size("z")
+    depth = lax.axis_size("zh")
     copies = jnp.broadcast_to(part[None], (depth, block, half))
-    arrived = exchange(copies, "z")
+    arrived = exchange(copies, "zh").reshape(depth, block, half)
     total = jnp.sum(arrived.astype(F32), axis=0).astype(BF16)
-    copies = jnp.broadcast_to(total[None], (planes, block, half))
-    own_half = exchange(copies, ("y", "x")).reshape(features, half)
-    other_half = swap_core(own_half)
-    low = jnp.where(core == 0, own_half, other_half)
-    high = jnp.where(core == 0, other_half, own_half)
-    return jnp.concatenate([low, high], axis=1)
+    width = lax.axis_size("y")
+    copies = jnp.broadcast_to(total[None], (planes // width, block, half))
+    slab = exchange(copies.reshape(features // width, half), ("x", "zl"))
+    rows = features // width
+    y = lax.axis_index("y")
+    covariance = jnp.zeros((features, features), BF16)
+    for shift in range(width):
+        perm = [(i, (i + shift) % width) for i in range(width)]
+        own = slab if shift == 0 else lax.ppermute(slab, "y", perm)
+        other = swap_core(own)
+        low = jnp.where(core == 0, own, other)
+        high = jnp.where(core == 0, other, own)
+        both = jnp.concatenate([low, high], axis=1)
+        start = ((y - shift) % width) * rows
+        covariance = lax.dynamic_update_slice_in_dim(covariance, both, start, 0)
+    return covariance
 
 
 def local(old_rows, new_rows, list_ids, owner_map):
@@ -91,7 +102,7 @@
 
 def solution(mesh):
     shape = mesh.shape
-    grid = mesh.devices.reshape(shape["grp"] // 2, 2, 4, shape["mem"] // 4)
+    grid = mesh.devices.reshape(shape["grp"] // 2, 2, 4, shape["mem"] // 8, 2)
     fine = Mesh(grid, ALL)
     in_specs = (P(ALL, None), P(ALL, None), P(ALL), P())
     out_specs = (P(ALL, None), P(MEM, None))

time: 115 us -> 102 us (0.89)
  blocking collectives: 62.9 us -> 38.4 us
  starting transfers between devices: 13.2 us -> 21.2 us
  waiting for transfers between devices: 7.76 us -> 10.3 us
    all_to_all x3 -> x2, blocking collectives: 62.9 us -> 38.4 us  [exchange(): return lax.all_to_all(value, axes, split_axis=0, concat_axis=0, tiled=True)]
    ppermute x0 -> x3, waiting for transfers between devices: none -> 5.69 us  [covariance_of(): own = slab if shift == 0 else lax.ppermute(slab, 'y', perm)]
    all_to_all x1 -> x2, waiting for transfers between devices: 7.75 us -> 4.11 us  [exchange(): return lax.all_to_all(value, axes, split_axis=0, concat_axis=0, tiled=True)]
    all_to_all x1 -> x2, starting transfers between devices: 4.84 us -> 8.08 us  [exchange(): return lax.all_to_all(value, axes, split_axis=0, concat_axis=0, tiled=True)]
    ppermute x0 -> x3, starting transfers between devices: none -> 3 us  [covariance_of(): own = slab if shift == 0 else lax.ppermute(slab, 'y', perm)]
    ppermute x3 -> x6, starting transfers between devices: 8.34 us -> 10.1 us  [swap_core(): return lax.ppermute(value, 'core', [(0, 1), (1, 0)])]
  transfers between devices with their start and end apart: 4 -> 11, of which waited for: 1 -> 3; matrix products, arithmetic and copies ran while one was open for 20% -> 23% of each run, Pallas kernels for 0% -> 0%
where the time goes in v2:
time: 102 us; the launch traced here: 101 us
  blocking collectives  38.4 us (38%)
  matrix products  22.2 us (22%)
  starting transfers between devices  21.2 us (21%)
  waiting for transfers between devices  10.3 us (10%)
  local copies, waits for them, and re-layouts  3.93 us (4%)
  other arithmetic  3.44 us (3%)
  between operations  1.69 us (2%)
    all_to_all x2, blocking collectives, exchange(): return lax.all_to_all(value, axes, split_axis=0, concat_axis=0, tiled=True)  38.4 us
    dot_general x10, matrix products, dot(): return jnp.dot(a, b, preferred_element_type=F32)  22.2 us
    ppermute x6, starting transfers between devices, swap_core(): return lax.ppermute(value, 'core', [(0, 1), (1, 0)])  10.1 us
    all_to_all x2, starting transfers between devices, exchange(): return lax.all_to_all(value, axes, split_axis=0, concat_axis=0, tiled=True)  8.08 us
    ppermute x3, waiting for transfers between devices, covariance_of(): own = slab if shift == 0 else lax.ppermute(slab, 'y', perm)  5.69 us
    all_to_all x2, waiting for transfers between devices, exchange(): return lax.all_to_all(value, axes, split_axis=0, concat_axis=0, tiled=True)  4.11 us
    ppermute x3, starting transfers between devices, covariance_of(): own = slab if shift == 0 else lax.ppermute(slab, 'y', perm)  3 us
  transfers between devices with their start and end apart: 11, of which 3 were waited for; matrix products, arithmetic and copies ran while one was open for 23% of the time, Pallas kernels for 0%

profile of v2, /device:TPU:1, one launch (start us, length us, event | category | flops | bytes accessed | tf_op | source)
XLA Modules:
  0.0 101.2 jit_solution(5983790179571488000)
XLA Ops:
  0.6 0.0 copy-start
  0.6 3.3 %collective-permute-start.1 = (bf16[256,1024]{1,0:T(8,128)(2,1)}, bf16[256,1024]{1,0:T(8,128)(2,1)S(1)}, u32[]{:S(2)}, u32[]{:S(2)}) collective-permute-start(bf16[256,1024]{1,0:T(8,128)(2,1)} %param.4), channel_id=1, source_target_pairs={{0,32},{32,0},{1,33},{33,1},{2,34},{34,2},{3,35},{35,3},{4,36},{36... | collective-permute-start | bytes 1572872 | tf_op jit(solution)/shard_map/ppermute | solution.py:28
  4.0 0.0 copy-done
  4.0 1.0 %collective-permute-start = (bf16[256,512]{1,0:T(8,128)(2,1)S(1)}, bf16[256,512]{1,0:T(8,128)(2,1)S(1)}, u32[]{:S(2)}, u32[]{:S(2)}) collective-permute-start(bf16[256,512]{1,0:T(8,128)(2,1)S(1)} %constant_dynamic-slice_fusion.1), channel_id=1, source_target_pairs={{0,32},{32,0},{1,33},{33,1},{2,34},{34,2},{3,35},{35,3},{4,36},{36... | collective-permute-start | bytes 786440 | tf_op jit(solution)/shard_map/ppermute | solution.py:28
  5.0 1.5 %fusion.6 = f32[512,1024]{1,0:T(8,128)S(1)} fusion(bf16[256,1024]{1,0:T(8,128)(2,1)} %param.4, bf16[256,1024]{1,0:T(8,128)(2,1)S(1)} %copy-done, s32[]{:T(128)S(6)} %select_n.81), kind=kOutput, calls=%fused_computation.20 | convolution fusion | flops 268435456 | bytes 2883588 | tf_op jit(solution)/shard_map/dot_general | solution.py:24
  6.5 0.0 collective-permute-done
  6.6 0.0 collective-permute-done.1
  6.6 0.5 fusion.5
  7.0 0.5 copy.7
  7.6 0.0 copy-start.3
  7.6 0.0 copy-start.1
  7.6 24.0 %all_to_all.35 = bf16[32,32,512]{2,1,0:T(8,128)(2,1)S(1)} all-to-all(bf16[32,32,512]{2,1,0:T(8,128)(2,1)S(1)} %bitcast.23), channel_id=1, replica_groups=mesh['y'=4,'core'=2,'x'=4,'zh'=4,'zl'=2] {'y','x','zl'}, dimensions={0} | all-to-all | bytes 2097152 | tf_op jit(solution)/shard_map/all_to_all | solution.py:32
  31.6 0.0 copy-start.2
  31.6 0.2 reduce_sum.43
  31.8 14.4 %all_to_all.36 = bf16[4,32,512]{2,1,0:T(8,128)(2,1)S(1)} all-to-all(bf16[4,32,512]{2,1,0:T(8,128)(2,1)S(1)} %broadcast_in_dim.10), channel_id=1, replica_groups=mesh['y'=4,'core'=2,'x'=4,'zh'=4,'zl'=2] {'zh'}, dimensions={0} | all-to-all | bytes 262144 | tf_op jit(solution)/shard_map/all_to_all | solution.py:32
  46.2 0.7 broadcast_in_dim.11
  46.9 3.4 %all-to-all-start.3 = ((bf16[8,32,512]{2,1,0:T(8,128)(2,1)}), bf16[8,32,512]{2,1,0:T(8,128)(2,1)S(1)}, u32[]{:S(2)}, u32[]{:S(2)}) async-start(bf16[8,32,512]{2,1,0:T(8,128)(2,1)} %broadcast_in_dim.11), calls=%async_computation.3 | async-start | bytes 524288 | tf_op jit(solution)/shard_map/all_to_all | solution.py:32
  50.3 0.0 copy-done.3
  50.4 0.0 copy-done.1
  50.4 1.7 %gather_fusion = s32[256]{0:T(256)S(1)} fusion(s32[65536]{0:T(1024)S(1)} %copy-done.1, s32[1024]{0:T(1024)S(1)} %pad_clamp_fusion), kind=kCustom, calls=%fused_computation | custom fusion | bytes 3072 | tf_op jit(solution)/shard_map/gather | solution.py:38
  52.1 0.2 convert_reduce_fusion
  52.3 4.1 %all-to-all-done.3 = bf16[8,32,512]{2,1,0:T(8,128)(2,1)S(1)} async-done(((bf16[8,32,512]{2,1,0:T(8,128)(2,1)}), bf16[8,32,512]{2,1,0:T(8,128)(2,1)S(1)}, u32[]{:S(2)}, u32[]{:S(2)}) %all-to-all-start.3) | async-done | bytes 262176 | tf_op jit(solution)/shard_map/all_to_all | solution.py:32
  56.4 4.2 %collective-permute-start.2 = (bf16[256,512]{1,0:T(8,128)(2,1)S(1)}, bf16[256,512]{1,0:T(8,128)(2,1)S(1)}, u32[]{:S(2)}, u32[]{:S(2)}) collective-permute-start(bf16[256,512]{1,0:T(8,128)(2,1)S(1)} %bitcast.24), channel_id=1, source_target_pairs={{0,32},{32,0},{1,33},{33,1},{2,34},{34,2},{3,35},{35,3},{4,36},{36... | collective-permute-start | bytes 786440 | tf_op jit(solution)/shard_map/ppermute | solution.py:28
  60.6 0.0 collective-permute-start.3
  60.6 1.7 %collective-permute-start.5 = (bf16[256,512]{1,0:T(8,128)(2,1)S(1)}, bf16[256,512]{1,0:T(8,128)(2,1)S(1)}, u32[]{:S(2)}, u32[]{:S(2)}) collective-permute-start(bf16[256,512]{1,0:T(8,128)(2,1)S(1)} %bitcast.26), channel_id=1, source_target_pairs={{0,128},{64,192},{128,0},{192,64},{1,129},{65,193},{129,1},{193,65... | collective-permute-start | bytes 786440 | tf_op jit(solution)/shard_map/ppermute | solution.py:72
  62.4 0.0 copy-done.2
  62.4 1.4 %convolution_convert_fusion.2 = bf16[512,1024]{1,0:T(8,128)(2,1)} fusion(bf16[256,1024]{1,0:T(8,128)(2,1)S(1)} %copy-done.2, s32[256]{0:T(256)S(1)} %multiply_add_fusion), kind=kOutput, calls=%fused_computation.13 | convolution fusion | flops 269090816 | bytes 1573888 | tf_op jit(solution)/shard_map/dot_general | solution.py:24
  63.8 4.7 %all-to-all-start = ((bf16[32,16,1024]{2,1,0:T(8,128)(2,1)}), bf16[32,16,1024]{2,1,0:T(8,128)(2,1)}, u32[]{:S(2)}, u32[]{:S(2)}) async-start(bf16[32,16,1024]{2,1,0:T(8,128)(2,1)} %bitcast), calls=%async_computation | async-start | bytes 2097152 | tf_op jit(solution)/shard_map/all_to_all | solution.py:32
  68.5 1.3 %collective-permute-start.7 = (bf16[256,512]{1,0:T(8,128)(2,1)S(1)}, bf16[256,512]{1,0:T(8,128)(2,1)S(1)}, u32[]{:S(2)}, u32[]{:S(2)}) collective-permute-start(bf16[256,512]{1,0:T(8,128)(2,1)S(1)} %bitcast.27), channel_id=1, source_target_pairs={{0,192},{64,0},{128,64},{192,128},{1,193},{65,1},{129,65},{193,129... | collective-permute-start | bytes 786440 | tf_op jit(solution)/shard_map/ppermute | solution.py:72
  69.8 5.7 %collective-permute-done.3 = bf16[256,512]{1,0:T(8,128)(2,1)} collective-permute-done((bf16[256,512]{1,0:T(8,128)(2,1)S(1)}, bf16[256,512]{1,0:T(8,128)(2,1)}, u32[]{:S(2)}, u32[]{:S(2)}) %collective-permute-start.3) | collective-permute-done | bytes 262176 | tf_op jit(solution)/shard_map/ppermute | solution.py:72
  75.5 0.8 collective-permute-start.4
  76.3 0.0 collective-permute-done.5
  76.3 0.0 collective-permute-start.6
  76.3 0.0 collective-permute-done.2
  76.3 0.1 broadcast_select_fusion.7
  76.4 0.3 broadcast_in_dim.9
  76.6 0.1 maximum_dynamic-update-slice_fusion
  76.7 0.0 collective-permute-done.7
  76.7 0.8 collective-permute-start.8
  77.5 0.5 collective-permute-done.4
  78.0 1.0 broadcast_select_fusion.5
  79.0 0.0 collective-permute-done.6
  79.0 0.1 maximum_dynamic-update-slice_fusion.1
  79.1 0.1 maximum_dynamic-update-slice_fusion.2
  79.2 0.0 collective-permute-done.8
  79.2 0.1 broadcast_select_fusion.1
  79.2 0.1 maximum_dynamic-update-slice_fusion.3
  79.3 1.7 %fusion.2 = f32[]{:T(128)} fusion(bf16[1024,1024]{1,0:T(8,128)(2,1)S(1)} %maximum_dynamic-update-slice_fusion.3), kind=kLoop, calls=%fused_computation.5 | loop fusion | flops 3145727 | bytes 2097156 | tf_op jit(solution)/shard_map/reduce_sum | solution.py:90
  81.7 2.4 %convolution_convert_fusion.1 = bf16[1024,1024]{1,0:T(8,128)(2,1)S(1)} fusion(bf16[1024,1024]{1,0:T(8,128)(2,1)S(1)} %maximum_dynamic-update-slice_fusion.3, f32[]{:T(128)S(6)} %sqrt.3), kind=kOutput, calls=%fused_computation.12 | convolution fusion | flops 2152726528 | bytes 4194308 | tf_op jit(solution)/shard_map/dot_general | solution.py:24
  84.0 2.4 %fusion.11 = bf16[1024,1024]{1,0:T(8,128)(2,1)S(1)} fusion(bf16[1024,1024]{1,0:T(8,128)(2,1)S(1)} %convolution_convert_fusion.1, bf16[1024,1024]{1,0:T(8,128)(2,1)S(1)} %maximum_dynamic-update-slice_fusion.3, f32[]{:T(128)S(6)} %sqrt.3), kind=kOutput, calls=%fused_computation.40 | convolution fusion | flops 2151677952 | bytes 6291460 | tf_op jit(solution)/shard_map/dot_general | solution.py:24
  86.4 2.9 %add_convert_fusion.1 = bf16[1024,1024]{1,0:T(8,128)(2,1)S(1)} fusion(bf16[1024,1024]{1,0:T(8,128)(2,1)S(1)} %convolution_convert_fusion.1, bf16[1024,1024]{1,0:T(8,128)(2,1)S(1)} %fusion.11, f32[]{:T(128)S(6)} %sqrt.3, bf16[1024,1024]{1,0:T(8,128)(2,1)S(1)} %maximum_dynamic-update-slice_fusion.3), kind=kOutput, calls=%fused_computation.7 | convolution fusion | flops 2160066560 | bytes 8388612 | tf_op jit(solution)/shard_map/dot_general | solution.py:24
  89.3 2.4 %convolution_convert_fusion = bf16[1024,1024]{1,0:T(8,128)(2,1)S(1)} fusion(bf16[1024,1024]{1,0:T(8,128)(2,1)S(1)} %add_convert_fusion.1), kind=kOutput, calls=%fused_computation.11 | convolution fusion | flops 2148532224 | bytes 4194304 | tf_op jit(solution)/shard_map/dot_general | solution.py:24
  91.7 2.3 %fusion.14 = bf16[1024,1024]{1,0:T(8,128)(2,1)S(1)} fusion(bf16[1024,1024]{1,0:T(8,128)(2,1)S(1)} %convolution_convert_fusion, bf16[1024,1024]{1,0:T(8,128)(2,1)S(1)} %add_convert_fusion.1), kind=kOutput, calls=%fused_computation.41 | convolution fusion | flops 2147483648 | bytes 6291456 | tf_op jit(solution)/shard_map/dot_general | solution.py:24
  94.1 2.7 %add_convert_fusion = bf16[1024,1024]{1,0:T(8,128)(2,1)S(1)} fusion(bf16[1024,1024]{1,0:T(8,128)(2,1)S(1)} %add_convert_fusion.1, bf16[1024,1024]{1,0:T(8,128)(2,1)S(1)} %convolution_convert_fusion, bf16[1024,1024]{1,0:T(8,128)(2,1)S(1)} %fusion.14), kind=kOutput, calls=%fused_computation.6 | convolution fusion | flops 2155872256 | bytes 8388608 | tf_op jit(solution)/shard_map/dot_general | solution.py:24
  96.7 0.0 all-to-all-done
  96.7 3.8 %fusion.15 = f32[512,1024]{1,0:T(8,128)} fusion(bf16[512,1024]{1,0:T(8,128)(2,1)} %bitcast.1, bf16[1024,1024]{1,0:T(8,128)(2,1)S(1)} %add_convert_fusion), kind=kOutput, calls=%fused_computation.42 | convolution fusion | flops 1073741824 | bytes 5242880 | tf_op jit(solution)/shard_map/dot_general | solution.py:24
  100.5 0.6 constant_dynamic-slice_fusion
  (7 shorter events, 0.1 us)
Async XLA Ops:
  0.6 3.3 %copy-start = (bf16[256,1024]{1,0:T(8,128)(2,1)S(1)}, bf16[256,1024]{1,0:T(8,128)(2,1)}, u32[]{:S(2)}) copy-start(bf16[256,1024]{1,0:T(8,128)(2,1)} %param.5) | copy-start | bytes 1572868
  0.6 5.9 %collective-permute-start.1 = (bf16[256,1024]{1,0:T(8,128)(2,1)}, bf16[256,1024]{1,0:T(8,128)(2,1)S(1)}, u32[]{:S(2)}, u32[]{:S(2)}) collective-permute-start(bf16[256,1024]{1,0:T(8,128)(2,1)} %param.4), channel_id=1, source_target_pairs={{0,32},{32,0},{1,33},{33,1},{2,34},{34,2},{3,35},{35,3},{4,36},{36... | collective-permute-start | bytes 1572872 | tf_op jit(solution)/shard_map/ppermute | solution.py:28
  4.0 2.5 %collective-permute-start = (bf16[256,512]{1,0:T(8,128)(2,1)S(1)}, bf16[256,512]{1,0:T(8,128)(2,1)S(1)}, u32[]{:S(2)}, u32[]{:S(2)}) collective-permute-start(bf16[256,512]{1,0:T(8,128)(2,1)S(1)} %constant_dynamic-slice_fusion.1), channel_id=1, source_target_pairs={{0,32},{32,0},{1,33},{33,1},{2,34},{34,2},{3,35},{35,3},{4,36},{36... | collective-permute-start | bytes 786440 | tf_op jit(solution)/shard_map/ppermute | solution.py:28
  7.6 42.8 %copy-start.3 = (s32[256]{0:T(256)S(1)}, s32[256]{0:T(256)}, u32[]{:S(2)}) copy-start(s32[256]{0:T(256)} %param.6) | copy-start | bytes 3076
  7.6 42.8 %copy-start.1 = (s32[65536]{0:T(1024)S(1)}, s32[65536]{0:T(1024)}, u32[]{:S(2)}) copy-start(s32[65536]{0:T(1024)} %param.7) | copy-start | bytes 786436
  31.6 30.8 %copy-start.2 = (bf16[256,1024]{1,0:T(8,128)(2,1)S(1)}, bf16[256,1024]{1,0:T(8,128)(2,1)}, u32[]{:S(2)}) copy-start(bf16[256,1024]{1,0:T(8,128)(2,1)} %param.4) | copy-start | bytes 1572868
  46.9 9.5 %all-to-all-start.3 = ((bf16[8,32,512]{2,1,0:T(8,128)(2,1)}), bf16[8,32,512]{2,1,0:T(8,128)(2,1)S(1)}, u32[]{:S(2)}, u32[]{:S(2)}) async-start(bf16[8,32,512]{2,1,0:T(8,128)(2,1)} %broadcast_in_dim.11), calls=%async_computation.3 | async-start | bytes 524288 | tf_op jit(solution)/shard_map/all_to_all | solution.py:32
  56.4 19.9 %collective-permute-start.2 = (bf16[256,512]{1,0:T(8,128)(2,1)S(1)}, bf16[256,512]{1,0:T(8,128)(2,1)S(1)}, u32[]{:S(2)}, u32[]{:S(2)}) collective-permute-start(bf16[256,512]{1,0:T(8,128)(2,1)S(1)} %bitcast.24), channel_id=1, source_target_pairs={{0,32},{32,0},{1,33},{33,1},{2,34},{34,2},{3,35},{35,3},{4,36},{36... | collective-permute-start | bytes 786440 | tf_op jit(solution)/shard_map/ppermute | solution.py:28
  60.6 14.9 %collective-permute-start.3 = (bf16[256,512]{1,0:T(8,128)(2,1)S(1)}, bf16[256,512]{1,0:T(8,128)(2,1)}, u32[]{:S(2)}, u32[]{:S(2)}) collective-permute-start(bf16[256,512]{1,0:T(8,128)(2,1)S(1)} %bitcast.25), channel_id=1, source_target_pairs={{0,64},{64,128},{128,192},{192,0},{1,65},{65,129},{129,193},{193,1... | collective-permute-start | bytes 786440 | tf_op jit(solution)/shard_map/ppermute | solution.py:72
  60.6 15.7 %collective-permute-start.5 = (bf16[256,512]{1,0:T(8,128)(2,1)S(1)}, bf16[256,512]{1,0:T(8,128)(2,1)S(1)}, u32[]{:S(2)}, u32[]{:S(2)}) collective-permute-start(bf16[256,512]{1,0:T(8,128)(2,1)S(1)} %bitcast.26), channel_id=1, source_target_pairs={{0,128},{64,192},{128,0},{192,64},{1,129},{65,193},{129,1},{193,65... | collective-permute-start | bytes 786440 | tf_op jit(solution)/shard_map/ppermute | solution.py:72
  63.8 33.0 %all-to-all-start = ((bf16[32,16,1024]{2,1,0:T(8,128)(2,1)}), bf16[32,16,1024]{2,1,0:T(8,128)(2,1)}, u32[]{:S(2)}, u32[]{:S(2)}) async-start(bf16[32,16,1024]{2,1,0:T(8,128)(2,1)} %bitcast), calls=%async_computation | async-start | bytes 2097152 | tf_op jit(solution)/shard_map/all_to_all | solution.py:32
  68.5 8.2 %collective-permute-start.7 = (bf16[256,512]{1,0:T(8,128)(2,1)S(1)}, bf16[256,512]{1,0:T(8,128)(2,1)S(1)}, u32[]{:S(2)}, u32[]{:S(2)}) collective-permute-start(bf16[256,512]{1,0:T(8,128)(2,1)S(1)} %bitcast.27), channel_id=1, source_target_pairs={{0,192},{64,0},{128,64},{192,128},{1,193},{65,1},{129,65},{193,129... | collective-permute-start | bytes 786440 | tf_op jit(solution)/shard_map/ppermute | solution.py:72
  75.5 2.5 %collective-permute-start.4 = (bf16[256,512]{1,0:T(8,128)(2,1)}, bf16[256,512]{1,0:T(8,128)(2,1)S(1)}, u32[]{:S(2)}, u32[]{:S(2)}) collective-permute-start(bf16[256,512]{1,0:T(8,128)(2,1)} %collective-permute-done.3), channel_id=1, source_target_pairs={{0,32},{32,0},{1,33},{33,1},{2,34},{34,2},{3,35},{35,3},{4,36},{36... | collective-permute-start | bytes 786440 | tf_op jit(solution)/shard_map/ppermute | solution.py:28
  76.3 2.7 %collective-permute-start.6 = (bf16[256,512]{1,0:T(8,128)(2,1)S(1)}, bf16[256,512]{1,0:T(8,128)(2,1)S(1)}, u32[]{:S(2)}, u32[]{:S(2)}) collective-permute-start(bf16[256,512]{1,0:T(8,128)(2,1)S(1)} %collective-permute-done.5), channel_id=1, source_target_pairs={{0,32},{32,0},{1,33},{33,1},{2,34},{34,2},{3,35},{35,3},{4,36},{36... | collective-permute-start | bytes 786440 | tf_op jit(solution)/shard_map/ppermute | solution.py:28
  76.7 2.4 %collective-permute-start.8 = (bf16[256,512]{1,0:T(8,128)(2,1)S(1)}, bf16[256,512]{1,0:T(8,128)(2,1)S(1)}, u32[]{:S(2)}, u32[]{:S(2)}) collective-permute-start(bf16[256,512]{1,0:T(8,128)(2,1)S(1)} %collective-permute-done.7), channel_id=1, source_target_pairs={{0,32},{32,0},{1,33},{33,1},{2,34},{34,2},{3,35},{35,3},{4,36},{36... | collective-permute-start | bytes 786440 | tf_op jit(solution)/shard_map/ppermute | solution.py:28

commit v3 on v2

v3 whole, which is shorter than its diff:
```python
import math

import jax
import jax.numpy as jnp
from jax import lax
from jax.experimental import pallas as pl
from jax.experimental.pallas import tpu as pltpu
from jax.sharding import Mesh
from jax.sharding import PartitionSpec as P

WIDTH = 4

EPSILON = 1e-06
COEFF_ONE = 3.4445
COEFF_THREE = -4.775
COEFF_FIVE = 2.0315

ALL = ("y", "core", "x", "zh", "zl")
MEM = ("x", "zh", "zl")
SPREAD = ("y", "x", "zl")
F32 = jnp.float32
BF16 = jnp.bfloat16


def dot(a, b):
    return jnp.dot(a, b, preferred_element_type=F32)


def swap_core(value):
    return lax.ppermute(value, "core", [(0, 1), (1, 0)])


def exchange(value, axes):
    return lax.all_to_all(value, axes, split_axis=0, concat_axis=0, tiled=True)


def outgoing_rows(old_rows, list_ids, owner_map, members):
    row_total = old_rows.shape[0]
    capacity = 2 * row_total // members
    owner = owner_map[list_ids]
    index = jnp.arange(row_total, dtype=jnp.int32)
    earlier = (owner[:, None] == owner[None, :]) & (index[None, :] < index[:, None])
    target = owner * capacity + jnp.sum(earlier.astype(jnp.int32), axis=1)
    slots = jnp.arange(members * capacity, dtype=jnp.int32)
    place = (slots[:, None] == target[None, :]).astype(BF16)
    return dot(place, old_rows).astype(BF16)


def covariance_of(old_rows, new_rows):
    features = old_rows.shape[1]
    half = features // 2
    core = lax.axis_index("core")
    mine = lax.dynamic_slice_in_dim(new_rows, core * half, half, 1)
    theirs = lax.dynamic_slice_in_dim(new_rows, (1 - core) * half, half, 1)
    old_pair = swap_core(old_rows)
    new_pair = swap_core(theirs)
    part = (dot(old_rows.T, mine) + dot(old_pair.T, new_pair)).astype(BF16)
    planes = lax.axis_size(SPREAD)
    block = features // planes
    arrived = exchange(part, SPREAD).reshape(planes, block, half)
    part = jnp.sum(arrived.astype(F32), axis=0).astype(BF16)
    depth = lax.axis_size("zh")
    copies = jnp.broadcast_to(part[None], (depth, block, half))
    arrived = exchange(copies, "zh").reshape(depth, block, half)
    total = jnp.sum(arrived.astype(F32), axis=0).astype(BF16)
    copies = jnp.broadcast_to(total[None], (planes // WIDTH, block, half))
    slab = exchange(copies.reshape(features // WIDTH, half), ("x", "zl"))
    return slab


def polar_kernel(place, *refs):
    owns, others = refs[0:WIDTH], refs[WIDTH : 2 * WIDTH]
    result, rotation = refs[2 * WIDTH : 2 * WIDTH + 2]
    start, middle, gram32, gram, poly = refs[2 * WIDTH + 2 :]
    rows, half = owns[0].shape
    features = 2 * half
    span = [slice(s * rows, (s + 1) * rows) for s in range(WIDTH)]
    pairs = [(s, t) for s in range(WIDTH) for t in range(s, WIDTH)]

    def product(a, b):
        return lax.dot_general(a, b, (((1,), (1,)), ((), ())), preferred_element_type=F32)

    def mirrored(target, s, t, value):
        target[span[s], span[t]] = value.astype(BF16)
        if s != t:
            target[span[t], span[s]] = value.T.astype(BF16)

    for s in range(WIDTH):
        start[span[s], :half] = owns[s][...]
        start[span[s], half:] = others[s][...]
    squares = jnp.zeros((1, 1), F32)
    diagonal = lax.broadcasted_iota(jnp.int32, (rows, rows), 0) == lax.broadcasted_iota(
        jnp.int32, (rows, rows), 1
    )
    for k, (s, t) in enumerate(pairs):
        value = product(start[span[s], :], start[span[t], :])
        gram32[k] = value
        if s == t:
            squares += jnp.sum(jnp.where(diagonal, value, 0.0), keepdims=True)
    scale = 0.25 * math.sqrt(features) / jnp.sqrt(squares + EPSILON)
    for k, (s, t) in enumerate(pairs):
        mirrored(gram, s, t, gram32[k] * (scale * scale))

    def polynomial():
        for s, t in pairs:
            square = product(gram[span[s], :], gram[span[t], :])
            mirrored(poly, s, t, COEFF_THREE * gram[span[s], span[t]].astype(F32) + COEFF_FIVE * square)

    def advance(source, s):
        moved = jnp.dot(poly[span[s], :], source[...], preferred_element_type=F32)
        return COEFF_ONE * source[span[s], :].astype(F32) + moved

    polynomial()
    for s in range(WIDTH):
        middle[span[s], :] = (advance(start, s) * scale).astype(BF16)
    for s, t in pairs:
        mirrored(gram, s, t, product(middle[span[s], :], middle[span[t], :]))
    polynomial()
    y, core, member = place[0], place[1], place[2]
    for s in range(WIDTH):
        first = pl.multiple_of(lax.rem(y - s + WIDTH, WIDTH) * rows, rows)
        value = advance(middle, s).astype(BF16)
        result[pl.ds(first, rows), pl.ds(pl.multiple_of(core * half, half), half)] = value[:, :half]
        result[pl.ds(first, rows), pl.ds(pl.multiple_of((1 - core) * half, half), half)] = value[:, half:]
    kept = rotation.shape[0]
    rotation[...] = result[pl.ds(pl.multiple_of(member * kept, kept), kept), :]


def polar(place, owns, others, block_rows):
    rows, half = owns[0].shape
    features = 2 * half
    whole = (features, features)

    vmem = pl.BlockSpec(memory_space=pltpu.VMEM)
    return pl.pallas_call(
        polar_kernel,
        out_shape=(
            jax.ShapeDtypeStruct(whole, BF16),
            jax.ShapeDtypeStruct((block_rows, features), BF16),
        ),
        in_specs=[pl.BlockSpec(memory_space=pltpu.SMEM)] + [vmem] * (2 * WIDTH),
        out_specs=(vmem, vmem),
        scratch_shapes=[
            pltpu.VMEM(whole, BF16),
            pltpu.VMEM(whole, BF16),
            pltpu.VMEM((WIDTH * (WIDTH + 1) // 2, rows, rows), F32),
            pltpu.VMEM(whole, BF16),
            pltpu.VMEM(whole, BF16),
        ],
        compiler_params=pltpu.CompilerParams(vmem_limit_bytes=24 * 1024 * 1024),
        cost_estimate=pl.CostEstimate(flops=9 * features**3, bytes_accessed=2**22, transcendentals=0),
        name="polar",
    )(place.astype(jnp.int32), *owns, *others)


def rotate_kernel(rows, factor, out):
    out[...] = jnp.dot(rows[...], factor[...], preferred_element_type=F32)


def rotate(rows, factor):
    count, features = rows.shape
    block = 128
    return pl.pallas_call(
        rotate_kernel,
        grid=(count // block,),
        out_shape=jax.ShapeDtypeStruct((count, features), F32),
        in_specs=[
            pl.BlockSpec((block, features), lambda i: (i, 0)),
            pl.BlockSpec((features, features), lambda i: (0, 0)),
        ],
        out_specs=pl.BlockSpec((block, features), lambda i: (i, 0)),
        compiler_params=pltpu.CompilerParams(vmem_limit_bytes=12 * 1024 * 1024),
        cost_estimate=pl.CostEstimate(
            flops=2 * count * features**2, bytes_accessed=5 * 2**20, transcendentals=0
        ),
        name="rotate",
    )(rows, factor)


def local(old_rows, new_rows, list_ids, owner_map):
    features = old_rows.shape[1]
    members = lax.axis_size(MEM)
    sent = outgoing_rows(old_rows, list_ids, owner_map, members)
    slab = covariance_of(old_rows, new_rows)
    slab, sent = lax.optimization_barrier((slab, sent))
    received = exchange(sent, MEM)
    owns = [slab]
    for shift in range(1, WIDTH):
        owns.append(lax.ppermute(slab, "y", [(i, (i + shift) % WIDTH) for i in range(WIDTH)]))
    others = [swap_core(own) for own in owns]
    place = jnp.stack([lax.axis_index("y"), lax.axis_index("core"), lax.axis_index(MEM)])
    factor, own_rows = polar(place, owns, others, features // members)
    return (rotate(received, factor), own_rows)


def solution(mesh):
    shape = mesh.shape
    grid = mesh.devices.reshape(WIDTH, 2, 4, shape["mem"] // 8, 2)
    fine = Mesh(grid, ALL)
    in_specs = (P(ALL, None), P(ALL, None), P(ALL), P())
    out_specs = (P(ALL, None), P(MEM, None))
    return jax.shard_map(local, mesh=fine, in_specs=in_specs, out_specs=out_specs, check_vma=False)
```

time: 102 us -> 98.7 us (0.968)
  blocking collectives: 38.4 us -> 0 us
  starting transfers between devices: 21.2 us -> 42.2 us
  matrix products: 22.2 us -> 3.4 us
  waiting for transfers between devices: 10.3 us -> 28.6 us
  Pallas kernels: 0 us -> 15.2 us
  local copies, waits for them, and re-layouts: 3.93 us -> 7.39 us
  other arithmetic: 3.44 us -> 0.45 us
    all_to_all x2 -> x0, blocking collectives: 38.4 us -> none  [exchange(): return lax.all_to_all(value, axes, split_axis=0, concat_axis=0, tiled=True)]
    all_to_all x2 -> x4, waiting for transfers between devices: 4.11 us -> 27.4 us  [exchange(): return lax.all_to_all(value, axes, split_axis=0, concat_axis=0, tiled=True)]
    dot_general x10 -> x3, matrix products: 22.2 us -> 3.4 us  [dot(): return jnp.dot(a, b, preferred_element_type=F32)]
    pallas_call x0 -> x2, Pallas kernels: none -> 15.2 us  [the longest x1 12.3 us: polar(): pl.pallas_call(polar_kernel, out_shape=(jax.ShapeDtypeStruct(whole, BF16)...]
    all_to_all x2 -> x4, starting transfers between devices: 8.08 us -> 21.4 us  [exchange(): return lax.all_to_all(value, axes, split_axis=0, concat_axis=0, tiled=True)]
    ppermute x6, starting transfers between devices: 10.1 us -> 19.2 us  [swap_core(): return lax.ppermute(value, 'core', [(0, 1), (1, 0)])]
    ppermute x3, waiting for transfers between devices: 5.69 us -> 0.01 us  [local(): lax.ppermute(slab, 'y', [(i, (i + shift) % WIDTH) for i in range(WIDTH)])]
    unnamed x8 -> x12, local copies, waits for them, and re-layouts: 0.03 us -> 2.94 us
  transfers between devices with their start and end apart: 11 -> 13, of which waited for: 3 -> 4; matrix products, arithmetic and copies ran while one was open for 23% -> 5% of each run, Pallas kernels for 0% -> 13%
where the time goes in v3:
time: 98.7 us; the launch traced here: 98.1 us
  starting transfers between devices  42.2 us (43%)
  waiting for transfers between devices  28.6 us (29%)
  Pallas kernels  15.2 us (15%)
  local copies, waits for them, and re-layouts  7.39 us (7%)
  matrix products  3.4 us (3%)
    all_to_all x4, waiting for transfers between devices, exchange(): return lax.all_to_all(value, axes, split_axis=0, concat_axis=0, tiled=True)  27.4 us
    all_to_all x4, starting transfers between devices, exchange(): return lax.all_to_all(value, axes, split_axis=0, concat_axis=0, tiled=True)  21.4 us
    ppermute x6, starting transfers between devices, swap_core(): return lax.ppermute(value, 'core', [(0, 1), (1, 0)])  19.2 us
    pallas_call x1, Pallas kernels, polar(): pl.pallas_call(polar_kernel, out_shape=(jax.ShapeDtypeStruct(whole, BF16)...  12.3 us
    dot_general x3, matrix products, dot(): return jnp.dot(a, b, preferred_element_type=F32)  3.4 us
    pallas_call x1, Pallas kernels, rotate(): pl.pallas_call(rotate_kernel, grid=(count // block,), out_shape=jax.Shape...  2.95 us
    unnamed x12, local copies, waits for them, and re-layouts  2.94 us
  transfers between devices with their start and end apart: 13, of which 4 were waited for; matrix products, arithmetic and copies ran while one was open for 5% of the time, Pallas kernels for 13%

profile of v3, /device:TPU:1, one launch (start us, length us, event | category | flops | bytes accessed | tf_op | source)
XLA Modules:
  0.0 98.1 jit_solution(254933861212929978)
XLA Ops:
  0.6 0.0 copy-start
  0.6 3.3 %collective-permute-start.1 = (bf16[256,1024]{1,0:T(8,128)(2,1)}, bf16[256,1024]{1,0:T(8,128)(2,1)S(1)}, u32[]{:S(2)}, u32[]{:S(2)}) collective-permute-start(bf16[256,1024]{1,0:T(8,128)(2,1)} %param.4), channel_id=1, source_target_pairs={{0,32},{32,0},{1,33},{33,1},{2,34},{34,2},{3,35},{35,3},{4,36},{36... | collective-permute-start | bytes 1572872 | tf_op jit(solution)/shard_map/ppermute | solution.py:30
  4.0 0.0 copy-done
  4.0 1.0 %collective-permute-start = (bf16[256,512]{1,0:T(8,128)(2,1)S(1)}, bf16[256,512]{1,0:T(8,128)(2,1)S(1)}, u32[]{:S(2)}, u32[]{:S(2)}) collective-permute-start(bf16[256,512]{1,0:T(8,128)(2,1)S(1)} %constant_dynamic-slice_fusion), channel_id=1, source_target_pairs={{0,32},{32,0},{1,33},{33,1},{2,34},{34,2},{3,35},{35,3},{4,36},{36... | collective-permute-start | bytes 786440 | tf_op jit(solution)/shard_map/ppermute | solution.py:30
  5.0 1.5 %fusion.2 = f32[512,1024]{1,0:T(8,128)S(1)} fusion(bf16[256,1024]{1,0:T(8,128)(2,1)} %param.4, bf16[256,1024]{1,0:T(8,128)(2,1)S(1)} %copy-done, s32[]{:T(128)S(6)} %select_n.9), kind=kOutput, calls=%fused_computation.8 | convolution fusion | flops 268435456 | bytes 2883588 | tf_op jit(solution)/shard_map/dot_general | solution.py:26
  6.5 0.0 collective-permute-done
  6.6 0.0 collective-permute-done.1
  6.6 0.5 fusion
  7.0 0.0 copy-start.5
  7.0 1.3 %copy.7 = bf16[1024,512]{1,0:T(8,128)(2,1)} copy(bf16[1024,512]{0,1:T(8,128)(2,1)S(1)} %fusion) | data formatting | bytes 2097152 | tf_op jit(solution)/shard_map/convert_element_type | solution.py:57
  8.4 0.0 copy-start.3
  8.4 6.8 %all-to-all-start = ((bf16[32,32,512]{2,1,0:T(8,128)(2,1)}), bf16[32,32,512]{2,1,0:T(8,128)(2,1)S(1)}, u32[]{:S(2)}, u32[]{:S(2)}) async-start(bf16[32,32,512]{2,1,0:T(8,128)(2,1)} %bitcast.1), calls=%async_computation | async-start | bytes 2097152 | tf_op jit(solution)/shard_map/all_to_all | solution.py:34
  15.2 0.0 copy-done.5
  15.2 0.0 copy-start.4
  15.2 17.4 %all-to-all-done = bf16[32,32,512]{2,1,0:T(8,128)(2,1)S(1)} async-done(((bf16[32,32,512]{2,1,0:T(8,128)(2,1)}), bf16[32,32,512]{2,1,0:T(8,128)(2,1)S(1)}, u32[]{:S(2)}, u32[]{:S(2)}) %all-to-all-start) | async-done | bytes 1048608 | tf_op jit(solution)/shard_map/all_to_all | solution.py:34
  32.6 0.2 reduce_sum.33
  32.7 0.7 broadcast_in_dim.6
  33.4 7.3 %all-to-all-start.1 = ((bf16[4,32,512]{2,1,0:T(8,128)(2,1)}), bf16[4,32,512]{2,1,0:T(8,128)(2,1)S(1)}, u32[]{:S(2)}, u32[]{:S(2)}) async-start(bf16[4,32,512]{2,1,0:T(8,128)(2,1)} %broadcast_in_dim.6), calls=%async_computation.1 | async-start | bytes 262144 | tf_op jit(solution)/shard_map/all_to_all | solution.py:34
  40.7 0.0 copy-done.3
  40.7 1.7 %gather_fusion = s32[256]{0:T(256)S(1)} fusion(s32[65536]{0:T(1024)S(1)} %copy-done.3, s32[1024]{0:T(1024)S(1)} %pad_clamp_fusion), kind=kCustom, calls=%fused_computation | custom fusion | bytes 3072 | tf_op jit(solution)/shard_map/gather | solution.py:40
  42.4 0.2 convert_reduce_fusion
  42.6 5.4 %all-to-all-done.1 = bf16[4,32,512]{2,1,0:T(8,128)(2,1)S(1)} async-done(((bf16[4,32,512]{2,1,0:T(8,128)(2,1)}), bf16[4,32,512]{2,1,0:T(8,128)(2,1)S(1)}, u32[]{:S(2)}, u32[]{:S(2)}) %all-to-all-start.1) | async-done | bytes 131104 | tf_op jit(solution)/shard_map/all_to_all | solution.py:34
  48.0 0.7 broadcast_in_dim.7
  48.7 3.4 %all-to-all-start.2 = ((bf16[8,32,512]{2,1,0:T(8,128)(2,1)}), bf16[8,32,512]{2,1,0:T(8,128)(2,1)S(1)}, u32[]{:S(2)}, u32[]{:S(2)}) async-start(bf16[8,32,512]{2,1,0:T(8,128)(2,1)} %broadcast_in_dim.7), calls=%async_computation.2 | async-start | bytes 524288 | tf_op jit(solution)/shard_map/all_to_all | solution.py:34
  52.2 0.0 copy-done.4
  52.2 1.4 %convolution_convert_fusion = bf16[512,1024]{1,0:T(8,128)(2,1)} fusion(bf16[256,1024]{1,0:T(8,128)(2,1)S(1)} %copy-done.4, s32[256]{0:T(256)S(1)} %multiply_add_fusion), kind=kOutput, calls=%fused_computation.2 | convolution fusion | flops 269090816 | bytes 1573888 | tf_op jit(solution)/shard_map/dot_general | solution.py:26
  53.6 4.6 %all-to-all-done.2 = bf16[8,32,512]{2,1,0:T(8,128)(2,1)S(1)} async-done(((bf16[8,32,512]{2,1,0:T(8,128)(2,1)}), bf16[8,32,512]{2,1,0:T(8,128)(2,1)S(1)}, u32[]{:S(2)}, u32[]{:S(2)}) %all-to-all-start.2) | async-done | bytes 262176 | tf_op jit(solution)/shard_map/all_to_all | solution.py:34
  58.2 3.9 %all-to-all-start.3 = ((bf16[32,16,1024]{2,1,0:T(8,128)(2,1)}), bf16[32,16,1024]{2,1,0:T(8,128)(2,1)S(1)}, u32[]{:S(2)}, u32[]{:S(2)}) async-start(bf16[32,16,1024]{2,1,0:T(8,128)(2,1)} %bitcast.3), calls=%async_computation.3 | async-start | bytes 2097152 | tf_op jit(solution)/shard_map/all_to_all | solution.py:34
  62.2 0.6 collective-permute-start.4
  62.8 0.3 collective-permute-start.3
  63.1 0.7 collective-permute-start.2
  63.7 5.3 %collective-permute-start.5 = (bf16[256,512]{1,0:T(8,128)(2,1)S(1)}, bf16[256,512]{1,0:T(8,128)(2,1)S(1)}, u32[]{:S(2)}, u32[]{:S(2)}) collective-permute-start(bf16[256,512]{1,0:T(8,128)(2,1)S(1)} %bitcast.17), channel_id=1, source_target_pairs={{0,32},{32,0},{1,33},{33,1},{2,34},{34,2},{3,35},{35,3},{4,36},{36... | collective-permute-start | bytes 786440 | tf_op jit(solution)/shard_map/ppermute | solution.py:30
  69.0 0.0 collective-permute-done.4.refs_3_
  69.0 4.7 %collective-permute-start.8 = (bf16[256,512]{1,0:T(8,128)(2,1)S(1)}, bf16[256,512]{1,0:T(8,128)(2,1)S(1)}, u32[]{:S(2)}, u32[]{:S(2)}) collective-permute-start(bf16[256,512]{1,0:T(8,128)(2,1)S(1)} %collective-permute-done.4.refs_3_), channel_id=1, source_target_pairs={{0,32},{32,0},{1,33},{33,1},{2,34},{34,2},{3,35},{35,3},{4,36},{36... | collective-permute-start | bytes 786440 | tf_op jit(solution)/shard_map/ppermute | solution.py:30
  73.8 0.0 collective-permute-done.3.refs_2_
  73.8 2.2 %collective-permute-start.7 = (bf16[256,512]{1,0:T(8,128)(2,1)S(1)}, bf16[256,512]{1,0:T(8,128)(2,1)S(1)}, u32[]{:S(2)}, u32[]{:S(2)}) collective-permute-start(bf16[256,512]{1,0:T(8,128)(2,1)S(1)} %collective-permute-done.3.refs_2_), channel_id=1, source_target_pairs={{0,32},{32,0},{1,33},{33,1},{2,34},{34,2},{3,35},{35,3},{4,36},{36... | collective-permute-start | bytes 786440 | tf_op jit(solution)/shard_map/ppermute | solution.py:30
  76.0 0.0 collective-permute-done.2.refs_1_
  76.0 2.7 %collective-permute-start.6 = (bf16[256,512]{1,0:T(8,128)(2,1)S(1)}, bf16[256,512]{1,0:T(8,128)(2,1)}, u32[]{:S(2)}, u32[]{:S(2)}) collective-permute-start(bf16[256,512]{1,0:T(8,128)(2,1)S(1)} %collective-permute-done.2.refs_1_), channel_id=1, source_target_pairs={{0,32},{32,0},{1,33},{33,1},{2,34},{34,2},{3,35},{35,3},{4,36},{36... | collective-permute-start | bytes 786440 | tf_op jit(solution)/shard_map/ppermute | solution.py:30
  78.6 0.1 pad_add_fusion.place
  78.7 0.0 collective-permute-done.5.refs_4_
  78.7 0.0 collective-permute-done.8.refs_7_
  78.7 0.0 collective-permute-done.7.refs_6_
  78.7 1.2 %collective-permute-done.6.refs_5_ = bf16[256,512]{1,0:T(8,128)(2,1)} collective-permute-done((bf16[256,512]{1,0:T(8,128)(2,1)S(1)}, bf16[256,512]{1,0:T(8,128)(2,1)}, u32[]{:S(2)}, u32[]{:S(2)}) %collective-permute-start.6) | collective-permute-done | bytes 262176 | tf_op jit(solution)/shard_map/ppermute | solution.py:30
  79.9 12.3 %polar.1 = (bf16[1024,1024]{1,0:T(8,128)(2,1)S(1)}, bf16[32,1024]{1,0:T(8,128)(2,1)}) custom-call(s32[3]{0:T(128)S(1)} %pad_add_fusion.place, bf16[256,512]{1,0:T(8,128)(2,1)S(1)} %bitcast.18, bf16[256,512]{1,0:T(8,128)(2,1)S(1)} %collective-permute-done.2.refs_1_, bf16[256,512]{1,0:T(8,128)(2,1)S(1)} %collective-permute-done.3.refs_2_, ...), custom_call_target="tpu_custom_call" | custom-call | flops 9663676416 | bytes 4194304 | tf_op jit(solution)/shard_map/polar/pallas_call | solution.py:135
  92.2 0.0 copy-start.1
  92.2 1.3 %copy-done.1 = bf16[1024,1024]{1,0:T(8,128)(2,1)} copy-done((bf16[1024,1024]{1,0:T(8,128)(2,1)}, bf16[1024,1024]{1,0:T(8,128)(2,1)S(1)}, u32[]{:S(2)}) %copy-start.1) | copy-done | bytes 2097176
  93.5 0.0 all-to-all-done.3
  93.5 0.0 copy-start.2
  93.5 1.6 %copy-done.2 = bf16[1024,1024]{1,0:T(8,128)(2,1)S(1)} copy-done((bf16[1024,1024]{1,0:T(8,128)(2,1)S(1)}, bf16[1024,1024]{1,0:T(8,128)(2,1)}, u32[]{:S(2)}) %copy-start.2) | copy-done | bytes 2097176
  95.1 3.0 %rotate.1 = f32[512,1024]{1,0:T(8,128)} custom-call(bf16[512,1024]{1,0:T(8,128)(2,1)S(1)} %bitcast.13, bf16[1024,1024]{1,0:T(8,128)(2,1)S(1)} %copy-done.2), custom_call_target="tpu_custom_call" | custom-call | flops 1073741824 | bytes 5242880 | tf_op jit(solution)/shard_map/rotate/pallas_call | solution.py:163
  (5 shorter events, 0.1 us)
Async XLA Ops:
  0.6 3.3 %copy-start = (bf16[256,1024]{1,0:T(8,128)(2,1)S(1)}, bf16[256,1024]{1,0:T(8,128)(2,1)}, u32[]{:S(2)}) copy-start(bf16[256,1024]{1,0:T(8,128)(2,1)} %param.5) | copy-start | bytes 1572868
  0.6 5.9 %collective-permute-start.1 = (bf16[256,1024]{1,0:T(8,128)(2,1)}, bf16[256,1024]{1,0:T(8,128)(2,1)S(1)}, u32[]{:S(2)}, u32[]{:S(2)}) collective-permute-start(bf16[256,1024]{1,0:T(8,128)(2,1)} %param.4), channel_id=1, source_target_pairs={{0,32},{32,0},{1,33},{33,1},{2,34},{34,2},{3,35},{35,3},{4,36},{36... | collective-permute-start | bytes 1572872 | tf_op jit(solution)/shard_map/ppermute | solution.py:30
  4.0 2.5 %collective-permute-start = (bf16[256,512]{1,0:T(8,128)(2,1)S(1)}, bf16[256,512]{1,0:T(8,128)(2,1)S(1)}, u32[]{:S(2)}, u32[]{:S(2)}) collective-permute-start(bf16[256,512]{1,0:T(8,128)(2,1)S(1)} %constant_dynamic-slice_fusion), channel_id=1, source_target_pairs={{0,32},{32,0},{1,33},{33,1},{2,34},{34,2},{3,35},{35,3},{4,36},{36... | collective-permute-start | bytes 786440 | tf_op jit(solution)/shard_map/ppermute | solution.py:30
  7.0 8.1 %copy-start.5 = (s32[256]{0:T(256)S(1)}, s32[256]{0:T(256)}, u32[]{:S(2)}) copy-start(s32[256]{0:T(256)} %param.6) | copy-start | bytes 3076
  8.4 32.3 %copy-start.3 = (s32[65536]{0:T(1024)S(1)}, s32[65536]{0:T(1024)}, u32[]{:S(2)}) copy-start(s32[65536]{0:T(1024)} %param.7) | copy-start | bytes 786436
  8.4 24.2 %all-to-all-start = ((bf16[32,32,512]{2,1,0:T(8,128)(2,1)}), bf16[32,32,512]{2,1,0:T(8,128)(2,1)S(1)}, u32[]{:S(2)}, u32[]{:S(2)}) async-start(bf16[32,32,512]{2,1,0:T(8,128)(2,1)} %bitcast.1), calls=%async_computation | async-start | bytes 2097152 | tf_op jit(solution)/shard_map/all_to_all | solution.py:34
  15.2 37.0 %copy-start.4 = (bf16[256,1024]{1,0:T(8,128)(2,1)S(1)}, bf16[256,1024]{1,0:T(8,128)(2,1)}, u32[]{:S(2)}) copy-start(bf16[256,1024]{1,0:T(8,128)(2,1)} %param.4) | copy-start | bytes 1572868
  33.4 14.6 %all-to-all-start.1 = ((bf16[4,32,512]{2,1,0:T(8,128)(2,1)}), bf16[4,32,512]{2,1,0:T(8,128)(2,1)S(1)}, u32[]{:S(2)}, u32[]{:S(2)}) async-start(bf16[4,32,512]{2,1,0:T(8,128)(2,1)} %broadcast_in_dim.6), calls=%async_computation.1 | async-start | bytes 262144 | tf_op jit(solution)/shard_map/all_to_all | solution.py:34
  48.7 9.5 %all-to-all-start.2 = ((bf16[8,32,512]{2,1,0:T(8,128)(2,1)}), bf16[8,32,512]{2,1,0:T(8,128)(2,1)S(1)}, u32[]{:S(2)}, u32[]{:S(2)}) async-start(bf16[8,32,512]{2,1,0:T(8,128)(2,1)} %broadcast_in_dim.7), calls=%async_computation.2 | async-start | bytes 524288 | tf_op jit(solution)/shard_map/all_to_all | solution.py:34
  58.2 35.3 %all-to-all-start.3 = ((bf16[32,16,1024]{2,1,0:T(8,128)(2,1)}), bf16[32,16,1024]{2,1,0:T(8,128)(2,1)S(1)}, u32[]{:S(2)}, u32[]{:S(2)}) async-start(bf16[32,16,1024]{2,1,0:T(8,128)(2,1)} %bitcast.3), calls=%async_computation.3 | async-start | bytes 2097152 | tf_op jit(solution)/shard_map/all_to_all | solution.py:34
  62.2 6.9 %collective-permute-start.4 = (bf16[256,512]{1,0:T(8,128)(2,1)S(1)}, bf16[256,512]{1,0:T(8,128)(2,1)S(1)}, u32[]{:S(2)}, u32[]{:S(2)}) collective-permute-start(bf16[256,512]{1,0:T(8,128)(2,1)S(1)} %bitcast.14), channel_id=1, source_target_pairs={{0,192},{64,0},{128,64},{192,128},{1,193},{65,1},{129,65},{193,129... | collective-permute-start | bytes 786440 | tf_op jit(solution)/shard_map/ppermute | solution.py:189
  62.8 11.0 %collective-permute-start.3 = (bf16[256,512]{1,0:T(8,128)(2,1)S(1)}, bf16[256,512]{1,0:T(8,128)(2,1)S(1)}, u32[]{:S(2)}, u32[]{:S(2)}) collective-permute-start(bf16[256,512]{1,0:T(8,128)(2,1)S(1)} %bitcast.15), channel_id=1, source_target_pairs={{0,128},{64,192},{128,0},{192,64},{1,129},{65,193},{129,1},{193,65... | collective-permute-start | bytes 786440 | tf_op jit(solution)/shard_map/ppermute | solution.py:189
  63.1 12.9 %collective-permute-start.2 = (bf16[256,512]{1,0:T(8,128)(2,1)S(1)}, bf16[256,512]{1,0:T(8,128)(2,1)S(1)}, u32[]{:S(2)}, u32[]{:S(2)}) collective-permute-start(bf16[256,512]{1,0:T(8,128)(2,1)S(1)} %bitcast.16), channel_id=1, source_target_pairs={{0,64},{64,128},{128,192},{192,0},{1,65},{65,129},{129,193},{193,1... | collective-permute-start | bytes 786440 | tf_op jit(solution)/shard_map/ppermute | solution.py:189
  63.7 15.0 %collective-permute-start.5 = (bf16[256,512]{1,0:T(8,128)(2,1)S(1)}, bf16[256,512]{1,0:T(8,128)(2,1)S(1)}, u32[]{:S(2)}, u32[]{:S(2)}) collective-permute-start(bf16[256,512]{1,0:T(8,128)(2,1)S(1)} %bitcast.17), channel_id=1, source_target_pairs={{0,32},{32,0},{1,33},{33,1},{2,34},{34,2},{3,35},{35,3},{4,36},{36... | collective-permute-start | bytes 786440 | tf_op jit(solution)/shard_map/ppermute | solution.py:30
  69.0 9.7 %collective-permute-start.8 = (bf16[256,512]{1,0:T(8,128)(2,1)S(1)}, bf16[256,512]{1,0:T(8,128)(2,1)S(1)}, u32[]{:S(2)}, u32[]{:S(2)}) collective-permute-start(bf16[256,512]{1,0:T(8,128)(2,1)S(1)} %collective-permute-done.4.refs_3_), channel_id=1, source_target_pairs={{0,32},{32,0},{1,33},{33,1},{2,34},{34,2},{3,35},{35,3},{4,36},{36... | collective-permute-start | bytes 786440 | tf_op jit(solution)/shard_map/ppermute | solution.py:30
  73.8 4.9 %collective-permute-start.7 = (bf16[256,512]{1,0:T(8,128)(2,1)S(1)}, bf16[256,512]{1,0:T(8,128)(2,1)S(1)}, u32[]{:S(2)}, u32[]{:S(2)}) collective-permute-start(bf16[256,512]{1,0:T(8,128)(2,1)S(1)} %collective-permute-done.3.refs_2_), channel_id=1, source_target_pairs={{0,32},{32,0},{1,33},{33,1},{2,34},{34,2},{3,35},{35,3},{4,36},{36... | collective-permute-start | bytes 786440 | tf_op jit(solution)/shard_map/ppermute | solution.py:30
  76.0 4.0 %collective-permute-start.6 = (bf16[256,512]{1,0:T(8,128)(2,1)S(1)}, bf16[256,512]{1,0:T(8,128)(2,1)}, u32[]{:S(2)}, u32[]{:S(2)}) collective-permute-start(bf16[256,512]{1,0:T(8,128)(2,1)S(1)} %collective-permute-done.2.refs_1_), channel_id=1, source_target_pairs={{0,32},{32,0},{1,33},{33,1},{2,34},{34,2},{3,35},{35,3},{4,36},{36... | collective-permute-start | bytes 786440 | tf_op jit(solution)/shard_map/ppermute | solution.py:30
  92.2 1.3 %copy-start.1 = (bf16[1024,1024]{1,0:T(8,128)(2,1)}, bf16[1024,1024]{1,0:T(8,128)(2,1)S(1)}, u32[]{:S(2)}) copy-start(bf16[1024,1024]{1,0:T(8,128)(2,1)S(1)} %get-tuple-element.8.factor) | copy-start | bytes 6291460
  93.5 1.6 %copy-start.2 = (bf16[1024,1024]{1,0:T(8,128)(2,1)S(1)}, bf16[1024,1024]{1,0:T(8,128)(2,1)}, u32[]{:S(2)}) copy-start(bf16[1024,1024]{1,0:T(8,128)(2,1)} %copy-done.1) | copy-start | bytes 6291460

commit v4 on v3

--- a/solution.py
+++ b/solution.py
@@ -46,32 +46,80 @@
     return dot(place, old_rows).astype(BF16)
 
 
-def covariance_of(old_rows, new_rows):
+def product_kernel(place, old_own, new_own, old_pair, new_pair, out):
+    features, half = out.shape
+    block = features // 4
+    mine = new_own[:, pl.ds(pl.multiple_of(place[1] * half, half), half)]
+    for k in range(4):
+        columns = slice(k * block, (k + 1) * block)
+        total = None
+        for old, new in ((old_own, mine), (old_pair, new_pair[...])):
+            term = lax.dot_general(
+                old[:, columns], new, (((0,), (0,)), ((), ())), preferred_element_type=F32
+            )
+            total = term if total is None else total + term
+        out[columns, :] = total.astype(BF16)
+
+
+def pair_product(place, old_own, new_own, old_pair, new_pair):
+    rows, features = old_own.shape
+    half = features // 2
+    vmem = pl.BlockSpec(memory_space=pltpu.VMEM)
+    return pl.pallas_call(
+        product_kernel,
+        out_shape=jax.ShapeDtypeStruct((features, half), BF16),
+        in_specs=[pl.BlockSpec(memory_space=pltpu.SMEM)] + [vmem] * 4,
+        out_specs=vmem,
+        compiler_params=pltpu.CompilerParams(vmem_limit_bytes=12 * 1024 * 1024),
+        cost_estimate=pl.CostEstimate(
+            flops=4 * rows * features * half, bytes_accessed=3 * 2**20, transcendentals=0
+        ),
+        name="pair_product",
+    )(place, old_own, new_own, old_pair, new_pair)
+
+
+def sum_kernel(terms, out):
+    total = terms[0].astype(F32)
+    for k in range(1, terms.shape[0]):
+        total += terms[k].astype(F32)
+    for k in range(out.shape[0]):
+        out[k] = total.astype(BF16)
+
+
+def sum_and_copy(terms, copies):
+    _, rows, columns = terms.shape
+    vmem = pl.BlockSpec(memory_space=pltpu.VMEM)
+    return pl.pallas_call(
+        sum_kernel,
+        out_shape=jax.ShapeDtypeStruct((copies, rows, columns), BF16),
+        in_specs=[vmem],
+        out_specs=vmem,
+        compiler_params=pltpu.CompilerParams(vmem_limit_bytes=8 * 1024 * 1024),
+        cost_estimate=pl.CostEstimate(flops=terms.size, bytes_accessed=2**20, transcendentals=0),
+        name="sum_and_copy",
+    )(terms)
+
+
+def covariance_slab(place, old_rows, new_rows):
     features = old_rows.shape[1]
     half = features // 2
     core = lax.axis_index("core")
-    mine = lax.dynamic_slice_in_dim(new_rows, core * half, half, 1)
     theirs = lax.dynamic_slice_in_dim(new_rows, (1 - core) * half, half, 1)
-    old_pair = swap_core(old_rows)
-    new_pair = swap_core(theirs)
-    part = (dot(old_rows.T, mine) + dot(old_pair.T, new_pair)).astype(BF16)
+    part = pair_product(place, old_rows, new_rows, swap_core(old_rows), swap_core(theirs))
     planes = lax.axis_size(SPREAD)
+    depth = lax.axis_size("zh")
     block = features // planes
     arrived = exchange(part, SPREAD).reshape(planes, block, half)
-    part = jnp.sum(arrived.astype(F32), axis=0).astype(BF16)
-    depth = lax.axis_size("zh")
-    copies = jnp.broadcast_to(part[None], (depth, block, half))
+    copies = sum_and_copy(arrived, depth)
     arrived = exchange(copies, "zh").reshape(depth, block, half)
-    total = jnp.sum(arrived.astype(F32), axis=0).astype(BF16)
-    copies = jnp.broadcast_to(total[None], (planes // WIDTH, block, half))
-    slab = exchange(copies.reshape(features // WIDTH, half), ("x", "zl"))
-    return slab
+    copies = sum_and_copy(arrived, planes // WIDTH)
+    return exchange(copies.reshape(features // WIDTH, half), ("x", "zl"))
 
 
 def polar_kernel(place, *refs):
     owns, others = refs[0:WIDTH], refs[WIDTH : 2 * WIDTH]
     result, rotation = refs[2 * WIDTH : 2 * WIDTH + 2]
-    start, middle, gram32, gram, poly = refs[2 * WIDTH + 2 :]
+    start, middle, gram32, gram, poly, slab_sem = refs[2 * WIDTH + 2 :]
     rows, half = owns[0].shape
     features = 2 * half
     span = [slice(s * rows, (s + 1) * rows) for s in range(WIDTH)]
@@ -85,9 +133,13 @@
         if s != t:
             target[span[t], span[s]] = value.T.astype(BF16)
 
+    own_slab = pltpu.make_async_copy(owns[0], start.at[span[0], pl.ds(0, half)], slab_sem)
+    own_slab.start()
     for s in range(WIDTH):
-        start[span[s], :half] = owns[s][...]
+        if s:
+            start[span[s], :half] = owns[s][...]
         start[span[s], half:] = others[s][...]
+    own_slab.wait()
     squares = jnp.zeros((1, 1), F32)
     diagonal = lax.broadcasted_iota(jnp.int32, (rows, rows), 0) == lax.broadcasted_iota(
         jnp.int32, (rows, rows), 1
@@ -138,7 +190,8 @@
             jax.ShapeDtypeStruct(whole, BF16),
             jax.ShapeDtypeStruct((block_rows, features), BF16),
         ),
-        in_specs=[pl.BlockSpec(memory_space=pltpu.SMEM)] + [vmem] * (2 * WIDTH),
+        in_specs=[pl.BlockSpec(memory_space=pltpu.SMEM), pl.BlockSpec(memory_space=pl.ANY)]
+        + [vmem] * (2 * WIDTH - 1),
         out_specs=(vmem, vmem),
         scratch_shapes=[
             pltpu.VMEM(whole, BF16),
@@ -146,29 +199,49 @@
             pltpu.VMEM((WIDTH * (WIDTH + 1) // 2, rows, rows), F32),
             pltpu.VMEM(whole, BF16),
             pltpu.VMEM(whole, BF16),
+            pltpu.SemaphoreType.DMA,
         ],
         compiler_params=pltpu.CompilerParams(vmem_limit_bytes=24 * 1024 * 1024),
         cost_estimate=pl.CostEstimate(flops=9 * features**3, bytes_accessed=2**22, transcendentals=0),
         name="polar",
-    )(place.astype(jnp.int32), *owns, *others)
-
-
-def rotate_kernel(rows, factor, out):
-    out[...] = jnp.dot(rows[...], factor[...], preferred_element_type=F32)
+    )(place, *owns, *others)
+
+
+def rotate_kernel(rows, factor, out, held, product, in_sems, out_sems):
+    block = held.shape[1]
+    parts = range(held.shape[0])
+
+    def fetch(k):
+        return pltpu.make_async_copy(rows.at[pl.ds(k * block, block), :], held.at[k], in_sems.at[k])
+
+    def store(k):
+        return pltpu.make_async_copy(product.at[k], out.at[pl.ds(k * block, block), :], out_sems.at[k])
+
+    for k in parts:
+        fetch(k).start()
+    for k in parts:
+        fetch(k).wait()
+        product[k] = jnp.dot(held[k], factor[...], preferred_element_type=F32)
+        store(k).start()
+    for k in parts:
+        store(k).wait()
 
 
 def rotate(rows, factor):
     count, features = rows.shape
-    block = 128
+    parts = 4
+    block = count // parts
     return pl.pallas_call(
         rotate_kernel,
-        grid=(count // block,),
         out_shape=jax.ShapeDtypeStruct((count, features), F32),
-        in_specs=[
-            pl.BlockSpec((block, features), lambda i: (i, 0)),
-            pl.BlockSpec((features, features), lambda i: (0, 0)),
+        in_specs=[pl.BlockSpec(memory_space=pltpu.HBM), pl.BlockSpec(memory_space=pltpu.VMEM)],
+        out_specs=pl.BlockSpec(memory_space=pltpu.HBM),
+        scratch_shapes=[
+            pltpu.VMEM((parts, block, features), BF16),
+            pltpu.VMEM((parts, block, features), F32),
+            pltpu.SemaphoreType.DMA((parts,)),
+            pltpu.SemaphoreType.DMA((parts,)),
         ],
-        out_specs=pl.BlockSpec((block, features), lambda i: (i, 0)),
         compiler_params=pltpu.CompilerParams(vmem_limit_bytes=12 * 1024 * 1024),
         cost_estimate=pl.CostEstimate(
             flops=2 * count * features**2, bytes_accessed=5 * 2**20, transcendentals=0
@@ -180,15 +253,16 @@
 def local(old_rows, new_rows, list_ids, owner_map):
     features = old_rows.shape[1]
     members = lax.axis_size(MEM)
+    place = jnp.stack([lax.axis_index("y"), lax.axis_index("core"), lax.axis_index(MEM)])
+    place = place.astype(jnp.int32)
     sent = outgoing_rows(old_rows, list_ids, owner_map, members)
-    slab = covariance_of(old_rows, new_rows)
+    slab = covariance_slab(place, old_rows, new_rows)
     slab, sent = lax.optimization_barrier((slab, sent))
     received = exchange(sent, MEM)
     owns = [slab]
     for shift in range(1, WIDTH):
         owns.append(lax.ppermute(slab, "y", [(i, (i + shift) % WIDTH) for i in range(WIDTH)]))
     others = [swap_core(own) for own in owns]
-    place = jnp.stack([lax.axis_index("y"), lax.axis_index("core"), lax.axis_index(MEM)])
     factor, own_rows = polar(place, owns, others, features // members)
     return (rotate(received, factor), own_rows)
 

time: 98.7 us -> 98.4 us (level)
  Pallas kernels: 15.2 us -> 18.5 us
  matrix products: 3.4 us -> 1.42 us
  local copies, waits for them, and re-layouts: 7.39 us -> 5.75 us
  waiting for transfers between devices: 28.6 us -> 29.7 us
  starting transfers between devices: 42.2 us -> 41.2 us
    pallas_call x1 -> x4, Pallas kernels: 2.95 us -> 6.55 us  [the longest x1 2.76 us: rotate(): pl.pallas_call(rotate_kernel, out_shape=jax.ShapeDtypeStruct((count, feat...]
    dot_general x3 -> x1, matrix products: 3.4 us -> 1.42 us  [dot(): return jnp.dot(a, b, preferred_element_type=F32)]
    broadcast_in_dim x2 -> x0, local copies, waits for them, and re-layouts: 1.39 us -> none  [the longest x1 0.72 us: covariance_of(): copies = jnp.broadcast_to(total[None], (planes // WIDTH, block, half))]
    ppermute x6, waiting for transfers between devices: 1.22 us -> 2.58 us  [swap_core(): return lax.ppermute(value, 'core', [(0, 1), (1, 0)])]
    convert_element_type x1 -> x0, local copies, waits for them, and re-layouts: 1.32 us -> none  [covariance_of(): part = (dot(old_rows.T, mine) + dot(old_pair.T, new_pair)).astype(BF16)]
    unnamed x12 -> x14, local copies, waits for them, and re-layouts: 2.94 us -> 3.06 us
  transfers between devices with their start and end apart: 13 -> 13, of which waited for: 4 -> 5; matrix products, arithmetic and copies ran while one was open for 5% -> 4% of each run, Pallas kernels for 13% -> 12%
where the time goes in v4:
time: 98.4 us; the launch traced here: 97.8 us
  starting transfers between devices  41.2 us (42%)
  waiting for transfers between devices  29.7 us (30%)
  Pallas kernels  18.5 us (19%)
  local copies, waits for them, and re-layouts  5.75 us (6%)
  matrix products  1.42 us (1%)
    all_to_all x4, waiting for transfers between devices, exchange(): return lax.all_to_all(value, axes, split_axis=0, concat_axis=0, tiled=True)  27.1 us
    all_to_all x4, starting transfers between devices, exchange(): return lax.all_to_all(value, axes, split_axis=0, concat_axis=0, tiled=True)  21.3 us
    ppermute x6, starting transfers between devices, swap_core(): return lax.ppermute(value, 'core', [(0, 1), (1, 0)])  18.3 us
    pallas_call x1, Pallas kernels, polar(): pl.pallas_call(polar_kernel, out_shape=(jax.ShapeDtypeStruct(whole, BF16)...  12 us
    unnamed x14, local copies, waits for them, and re-layouts  3.06 us
    pallas_call x1, Pallas kernels, rotate(): pl.pallas_call(rotate_kernel, out_shape=jax.ShapeDtypeStruct((count, feat...  2.76 us
    ppermute x6, waiting for transfers between devices, swap_core(): return lax.ppermute(value, 'core', [(0, 1), (1, 0)])  2.58 us
    pallas_call x1, Pallas kernels, pair_product(): pl.pallas_call(product_kernel, out_shape=jax.ShapeDtypeStruct((features,...  2.27 us
  transfers between devices with their start and end apart: 13, of which 5 were waited for; matrix products, arithmetic and copies ran while one was open for 4% of the time, Pallas kernels for 12%

profile of v4, /device:TPU:1, one launch (start us, length us, event | category | flops | bytes accessed | tf_op | source)
XLA Modules:
  0.0 97.8 jit_solution(9311013294906627032)
XLA Ops:
  0.6 0.0 copy-start
  0.6 3.3 %collective-permute-start = (bf16[256,1024]{1,0:T(8,128)(2,1)}, bf16[256,1024]{1,0:T(8,128)(2,1)S(1)}, u32[]{:S(2)}, u32[]{:S(2)}) collective-permute-start(bf16[256,1024]{1,0:T(8,128)(2,1)} %old_own.1), channel_id=1, source_target_pairs={{0,32},{32,0},{1,33},{33,1},{2,34},{34,2},{3,35},{35,3},{4,36},{36... | collective-permute-start | bytes 1572872 | tf_op jit(solution)/shard_map/ppermute | solution.py:30
  4.0 1.0 constant_dynamic-slice_fusion
  4.9 0.1 collective-permute-start.1
  5.1 0.0 copy-start.6
  5.1 0.1 pad_add_fusion.place
  5.1 1.4 %collective-permute-done.1.new_pair = bf16[256,512]{1,0:T(8,128)(2,1)S(1)} collective-permute-done((bf16[256,512]{1,0:T(8,128)(2,1)S(1)}, bf16[256,512]{1,0:T(8,128)(2,1)S(1)}, u32[]{:S(2)}, u32[]{:S(2)}) %collective-permute-start.1) | collective-permute-done | bytes 262176 | tf_op jit(solution)/shard_map/ppermute | solution.py:30
  6.6 0.0 collective-permute-done.old_pair
  6.6 0.0 copy-start.1
  6.6 1.0 %copy-done.1 = bf16[256,1024]{1,0:T(8,128)(2,1)S(1)} copy-done((bf16[256,1024]{1,0:T(8,128)(2,1)S(1)}, bf16[256,1024]{1,0:T(8,128)(2,1)}, u32[]{:S(2)}) %copy-start.1) | copy-done | bytes 524312
  7.6 0.0 copy-start.3
  7.6 1.0 %copy-done.3 = bf16[256,1024]{1,0:T(8,128)(2,1)S(1)} copy-done((bf16[256,1024]{1,0:T(8,128)(2,1)S(1)}, bf16[256,1024]{1,0:T(8,128)(2,1)}, u32[]{:S(2)}) %copy-start.3) | copy-done | bytes 524312
  8.7 2.3 %pair_product.1 = bf16[1024,512]{1,0:T(8,128)(2,1)} custom-call(s32[3]{0:T(128)S(1)} %pad_add_fusion.place, bf16[256,1024]{1,0:T(8,128)(2,1)S(1)} %copy-done.1, bf16[256,1024]{1,0:T(8,128)(2,1)S(1)} %copy-done.3, bf16[256,1024]{1,0:T(8,128)(2,1)S(1)} %collective-permute-done.old_pair, bf16[256,512]{1,0:T(8,128)(2,1)S(1)} %collective-permute-done.1.new_pair), custom_call_target="tpu_custom_call" | custom-call | flops 536870912 | bytes 3145728 | tf_op jit(solution)/shard_map/pair_product/pallas_call | solution.py:68
  10.9 6.7 %all-to-all-start = ((bf16[32,32,512]{2,1,0:T(8,128)(2,1)}), bf16[32,32,512]{2,1,0:T(8,128)(2,1)S(1)}, u32[]{:S(2)}, u32[]{:S(2)}) async-start(bf16[32,32,512]{2,1,0:T(8,128)(2,1)} %bitcast.3), calls=%async_computation | async-start | bytes 2097152 | tf_op jit(solution)/shard_map/all_to_all | solution.py:34
  17.6 0.0 copy-done.6
  17.6 0.0 copy-start.2
  17.6 17.2 %all-to-all-done.terms = bf16[32,32,512]{2,1,0:T(8,128)(2,1)S(1)} async-done(((bf16[32,32,512]{2,1,0:T(8,128)(2,1)}), bf16[32,32,512]{2,1,0:T(8,128)(2,1)S(1)}, u32[]{:S(2)}, u32[]{:S(2)}) %all-to-all-start) | async-done | bytes 1048608 | tf_op jit(solution)/shard_map/all_to_all | solution.py:34
  34.8 0.8 sum_and_copy.2
  35.6 7.3 %all-to-all-start.1 = ((bf16[4,32,512]{2,1,0:T(8,128)(2,1)}), bf16[4,32,512]{2,1,0:T(8,128)(2,1)S(1)}, u32[]{:S(2)}, u32[]{:S(2)}) async-start(bf16[4,32,512]{2,1,0:T(8,128)(2,1)} %sum_and_copy.2), calls=%async_computation.1 | async-start | bytes 262144 | tf_op jit(solution)/shard_map/all_to_all | solution.py:34
  42.9 0.0 copy-done
  42.9 1.7 %gather_fusion = s32[256]{0:T(256)S(1)} fusion(s32[65536]{0:T(1024)S(1)} %copy-done, s32[1024]{0:T(1024)S(1)} %pad_clamp_fusion), kind=kCustom, calls=%fused_computation | custom fusion | bytes 3072 | tf_op jit(solution)/shard_map/gather | solution.py:40
  44.7 0.2 convert_reduce_fusion
  44.8 5.3 %all-to-all-done.1.terms = bf16[4,32,512]{2,1,0:T(8,128)(2,1)S(1)} async-done(((bf16[4,32,512]{2,1,0:T(8,128)(2,1)}), bf16[4,32,512]{2,1,0:T(8,128)(2,1)S(1)}, u32[]{:S(2)}, u32[]{:S(2)}) %all-to-all-start.1) | async-done | bytes 131104 | tf_op jit(solution)/shard_map/all_to_all | solution.py:34
  50.1 0.7 sum_and_copy.3
  50.9 3.4 %all-to-all-start.2 = ((bf16[8,32,512]{2,1,0:T(8,128)(2,1)}), bf16[8,32,512]{2,1,0:T(8,128)(2,1)S(1)}, u32[]{:S(2)}, u32[]{:S(2)}) async-start(bf16[8,32,512]{2,1,0:T(8,128)(2,1)} %sum_and_copy.3), calls=%async_computation.2 | async-start | bytes 524288 | tf_op jit(solution)/shard_map/all_to_all | solution.py:34
  54.3 0.0 copy-done.2
  54.3 1.4 %convolution_convert_fusion = bf16[512,1024]{1,0:T(8,128)(2,1)} fusion(bf16[256,1024]{1,0:T(8,128)(2,1)S(1)} %copy-done.2, s32[256]{0:T(256)S(1)} %multiply_add_fusion), kind=kOutput, calls=%fused_computation.1 | convolution fusion | flops 269090816 | bytes 1573888 | tf_op jit(solution)/shard_map/dot_general | solution.py:26
  55.7 4.6 %all-to-all-done.2 = bf16[8,32,512]{2,1,0:T(8,128)(2,1)S(1)} async-done(((bf16[8,32,512]{2,1,0:T(8,128)(2,1)}), bf16[8,32,512]{2,1,0:T(8,128)(2,1)S(1)}, u32[]{:S(2)}, u32[]{:S(2)}) %all-to-all-start.2) | async-done | bytes 262176 | tf_op jit(solution)/shard_map/all_to_all | solution.py:34
  60.4 0.0 copy-start.4
  60.4 3.9 %all-to-all-start.3 = ((bf16[32,16,1024]{2,1,0:T(8,128)(2,1)}), bf16[32,16,1024]{2,1,0:T(8,128)(2,1)S(1)}, u32[]{:S(2)}, u32[]{:S(2)}) async-start(bf16[32,16,1024]{2,1,0:T(8,128)(2,1)} %bitcast.5), calls=%async_computation.3 | async-start | bytes 2097152 | tf_op jit(solution)/shard_map/all_to_all | solution.py:34
  64.3 0.6 collective-permute-start.4
  64.9 0.4 collective-permute-start.3
  65.3 0.6 collective-permute-start.2
  65.8 5.0 %collective-permute-start.5 = (bf16[256,512]{1,0:T(8,128)(2,1)S(1)}, bf16[256,512]{1,0:T(8,128)(2,1)S(1)}, u32[]{:S(2)}, u32[]{:S(2)}) collective-permute-start(bf16[256,512]{1,0:T(8,128)(2,1)S(1)} %bitcast.12), channel_id=1, source_target_pairs={{0,32},{32,0},{1,33},{33,1},{2,34},{34,2},{3,35},{35,3},{4,36},{36... | collective-permute-start | bytes 786440 | tf_op jit(solution)/shard_map/ppermute | solution.py:30
  70.9 0.0 collective-permute-done.4.refs_3_
  70.9 5.0 %collective-permute-start.8 = (bf16[256,512]{1,0:T(8,128)(2,1)S(1)}, bf16[256,512]{1,0:T(8,128)(2,1)S(1)}, u32[]{:S(2)}, u32[]{:S(2)}) collective-permute-start(bf16[256,512]{1,0:T(8,128)(2,1)S(1)} %collective-permute-done.4.refs_3_), channel_id=1, source_target_pairs={{0,32},{32,0},{1,33},{33,1},{2,34},{34,2},{3,35},{35,3},{4,36},{36... | collective-permute-start | bytes 786440 | tf_op jit(solution)/shard_map/ppermute | solution.py:30
  75.9 0.0 collective-permute-done.3.refs_2_
  75.9 2.2 %collective-permute-start.7 = (bf16[256,512]{1,0:T(8,128)(2,1)S(1)}, bf16[256,512]{1,0:T(8,128)(2,1)S(1)}, u32[]{:S(2)}, u32[]{:S(2)}) collective-permute-start(bf16[256,512]{1,0:T(8,128)(2,1)S(1)} %collective-permute-done.3.refs_2_), channel_id=1, source_target_pairs={{0,32},{32,0},{1,33},{33,1},{2,34},{34,2},{3,35},{35,3},{4,36},{36... | collective-permute-start | bytes 786440 | tf_op jit(solution)/shard_map/ppermute | solution.py:30
  78.1 0.0 collective-permute-done.2.refs_1_
  78.1 2.7 %collective-permute-start.6 = (bf16[256,512]{1,0:T(8,128)(2,1)S(1)}, bf16[256,512]{1,0:T(8,128)(2,1)S(1)}, u32[]{:S(2)}, u32[]{:S(2)}) collective-permute-start(bf16[256,512]{1,0:T(8,128)(2,1)S(1)} %collective-permute-done.2.refs_1_), channel_id=1, source_target_pairs={{0,32},{32,0},{1,33},{33,1},{2,34},{34,2},{3,35},{35,3},{4,36},{36... | collective-permute-start | bytes 786440 | tf_op jit(solution)/shard_map/ppermute | solution.py:30
  80.7 0.0 collective-permute-done.5.refs_4_
  80.8 0.0 collective-permute-done.8.refs_7_
  80.8 0.0 collective-permute-done.7.refs_6_
  80.8 0.0 copy-done.4
  80.8 1.1 %collective-permute-done.6.refs_5_ = bf16[256,512]{1,0:T(8,128)(2,1)S(1)} collective-permute-done((bf16[256,512]{1,0:T(8,128)(2,1)S(1)}, bf16[256,512]{1,0:T(8,128)(2,1)S(1)}, u32[]{:S(2)}, u32[]{:S(2)}) %collective-permute-start.6) | collective-permute-done | bytes 262176 | tf_op jit(solution)/shard_map/ppermute | solution.py:30
  81.9 0.0 copy-start.5
  81.9 0.9 copy-done.5
  82.9 12.0 %polar.1 = (bf16[1024,1024]{1,0:T(8,128)(2,1)S(1)}, bf16[32,1024]{1,0:T(8,128)(2,1)}) custom-call(s32[3]{0:T(128)S(1)} %pad_add_fusion.place, bf16[256,512]{1,0:T(8,128)(2,1)S(1)} %bitcast.13, bf16[256,512]{1,0:T(8,128)(2,1)S(1)} %collective-permute-done.2.refs_1_, bf16[256,512]{1,0:T(8,128)(2,1)S(1)} %collective-permute-done.3.refs_2_, ...), custom_call_target="tpu_custom_call" | custom-call | flops 9663676416 | bytes 4194304 | tf_op jit(solution)/shard_map/polar/pallas_call | solution.py:187
  94.8 0.0 all-to-all-done.3
  94.8 2.8 %rotate.1 = f32[512,1024]{1,0:T(8,128)} custom-call(bf16[512,1024]{1,0:T(8,128)(2,1)S(1)} %bitcast.8, bf16[1024,1024]{1,0:T(8,128)(2,1)S(1)} %get-tuple-element.8.factor), custom_call_target="tpu_custom_call" | custom-call | flops 1073741824 | bytes 5242880 | tf_op jit(solution)/shard_map/rotate/pallas_call | solution.py:234
  (3 shorter events, 0.0 us)
Async XLA Ops:
  0.6 42.3 %copy-start = (s32[65536]{0:T(1024)S(1)}, s32[65536]{0:T(1024)}, u32[]{:S(2)}) copy-start(s32[65536]{0:T(1024)} %param.7) | copy-start | bytes 786436
  0.6 5.9 %collective-permute-start = (bf16[256,1024]{1,0:T(8,128)(2,1)}, bf16[256,1024]{1,0:T(8,128)(2,1)S(1)}, u32[]{:S(2)}, u32[]{:S(2)}) collective-permute-start(bf16[256,1024]{1,0:T(8,128)(2,1)} %old_own.1), channel_id=1, source_target_pairs={{0,32},{32,0},{1,33},{33,1},{2,34},{34,2},{3,35},{35,3},{4,36},{36... | collective-permute-start | bytes 1572872 | tf_op jit(solution)/shard_map/ppermute | solution.py:30
  4.9 1.6 %collective-permute-start.1 = (bf16[256,512]{1,0:T(8,128)(2,1)S(1)}, bf16[256,512]{1,0:T(8,128)(2,1)S(1)}, u32[]{:S(2)}, u32[]{:S(2)}) collective-permute-start(bf16[256,512]{1,0:T(8,128)(2,1)S(1)} %constant_dynamic-slice_fusion), channel_id=1, source_target_pairs={{0,32},{32,0},{1,33},{33,1},{2,34},{34,2},{3,35},{35,3},{4,36},{36... | collective-permute-start | bytes 786440 | tf_op jit(solution)/shard_map/ppermute | solution.py:30
  5.1 12.5 %copy-start.6 = (s32[256]{0:T(256)S(1)}, s32[256]{0:T(256)}, u32[]{:S(2)}) copy-start(s32[256]{0:T(256)} %param.6) | copy-start | bytes 3076
  6.6 1.0 %copy-start.1 = (bf16[256,1024]{1,0:T(8,128)(2,1)S(1)}, bf16[256,1024]{1,0:T(8,128)(2,1)}, u32[]{:S(2)}) copy-start(bf16[256,1024]{1,0:T(8,128)(2,1)} %old_own.1) | copy-start | bytes 1572868
  7.6 1.0 %copy-start.3 = (bf16[256,1024]{1,0:T(8,128)(2,1)S(1)}, bf16[256,1024]{1,0:T(8,128)(2,1)}, u32[]{:S(2)}) copy-start(bf16[256,1024]{1,0:T(8,128)(2,1)} %new_own.1) | copy-start | bytes 1572868
  10.9 23.9 %all-to-all-start = ((bf16[32,32,512]{2,1,0:T(8,128)(2,1)}), bf16[32,32,512]{2,1,0:T(8,128)(2,1)S(1)}, u32[]{:S(2)}, u32[]{:S(2)}) async-start(bf16[32,32,512]{2,1,0:T(8,128)(2,1)} %bitcast.3), calls=%async_computation | async-start | bytes 2097152 | tf_op jit(solution)/shard_map/all_to_all | solution.py:34
  17.6 36.7 %copy-start.2 = (bf16[256,1024]{1,0:T(8,128)(2,1)S(1)}, bf16[256,1024]{1,0:T(8,128)(2,1)}, u32[]{:S(2)}) copy-start(bf16[256,1024]{1,0:T(8,128)(2,1)} %old_own.1) | copy-start | bytes 1572868
  35.6 14.5 %all-to-all-start.1 = ((bf16[4,32,512]{2,1,0:T(8,128)(2,1)}), bf16[4,32,512]{2,1,0:T(8,128)(2,1)S(1)}, u32[]{:S(2)}, u32[]{:S(2)}) async-start(bf16[4,32,512]{2,1,0:T(8,128)(2,1)} %sum_and_copy.2), calls=%async_computation.1 | async-start | bytes 262144 | tf_op jit(solution)/shard_map/all_to_all | solution.py:34
  50.9 9.5 %all-to-all-start.2 = ((bf16[8,32,512]{2,1,0:T(8,128)(2,1)}), bf16[8,32,512]{2,1,0:T(8,128)(2,1)S(1)}, u32[]{:S(2)}, u32[]{:S(2)}) async-start(bf16[8,32,512]{2,1,0:T(8,128)(2,1)} %sum_and_copy.3), calls=%async_computation.2 | async-start | bytes 524288 | tf_op jit(solution)/shard_map/all_to_all | solution.py:34
  60.4 20.4 %copy-start.4 = (bf16[8,32,512]{2,1,0:T(8,128)(2,1)}, bf16[8,32,512]{2,1,0:T(8,128)(2,1)S(1)}, u32[]{:S(2)}) copy-start(bf16[8,32,512]{2,1,0:T(8,128)(2,1)S(1)} %all-to-all-done.2) | copy-start | bytes 786436
  60.4 34.5 %all-to-all-start.3 = ((bf16[32,16,1024]{2,1,0:T(8,128)(2,1)}), bf16[32,16,1024]{2,1,0:T(8,128)(2,1)S(1)}, u32[]{:S(2)}, u32[]{:S(2)}) async-start(bf16[32,16,1024]{2,1,0:T(8,128)(2,1)} %bitcast.5), calls=%async_computation.3 | async-start | bytes 2097152 | tf_op jit(solution)/shard_map/all_to_all | solution.py:34
  64.3 6.6 %collective-permute-start.4 = (bf16[256,512]{1,0:T(8,128)(2,1)S(1)}, bf16[256,512]{1,0:T(8,128)(2,1)S(1)}, u32[]{:S(2)}, u32[]{:S(2)}) collective-permute-start(bf16[256,512]{1,0:T(8,128)(2,1)S(1)} %bitcast.9), channel_id=1, source_target_pairs={{0,192},{64,0},{128,64},{192,128},{1,193},{65,1},{129,65},{193,129... | collective-permute-start | bytes 786440 | tf_op jit(solution)/shard_map/ppermute | solution.py:264
  64.9 11.0 %collective-permute-start.3 = (bf16[256,512]{1,0:T(8,128)(2,1)S(1)}, bf16[256,512]{1,0:T(8,128)(2,1)S(1)}, u32[]{:S(2)}, u32[]{:S(2)}) collective-permute-start(bf16[256,512]{1,0:T(8,128)(2,1)S(1)} %bitcast.10), channel_id=1, source_target_pairs={{0,128},{64,192},{128,0},{192,64},{1,129},{65,193},{129,1},{193,65... | collective-permute-start | bytes 786440 | tf_op jit(solution)/shard_map/ppermute | solution.py:264
  65.3 12.8 %collective-permute-start.2 = (bf16[256,512]{1,0:T(8,128)(2,1)S(1)}, bf16[256,512]{1,0:T(8,128)(2,1)S(1)}, u32[]{:S(2)}, u32[]{:S(2)}) collective-permute-start(bf16[256,512]{1,0:T(8,128)(2,1)S(1)} %bitcast.11), channel_id=1, source_target_pairs={{0,64},{64,128},{128,192},{192,0},{1,65},{65,129},{129,193},{193,1... | collective-permute-start | bytes 786440 | tf_op jit(solution)/shard_map/ppermute | solution.py:264
  65.8 14.9 %collective-permute-start.5 = (bf16[256,512]{1,0:T(8,128)(2,1)S(1)}, bf16[256,512]{1,0:T(8,128)(2,1)S(1)}, u32[]{:S(2)}, u32[]{:S(2)}) collective-permute-start(bf16[256,512]{1,0:T(8,128)(2,1)S(1)} %bitcast.12), channel_id=1, source_target_pairs={{0,32},{32,0},{1,33},{33,1},{2,34},{34,2},{3,35},{35,3},{4,36},{36... | collective-permute-start | bytes 786440 | tf_op jit(solution)/shard_map/ppermute | solution.py:30
  70.9 9.9 %collective-permute-start.8 = (bf16[256,512]{1,0:T(8,128)(2,1)S(1)}, bf16[256,512]{1,0:T(8,128)(2,1)S(1)}, u32[]{:S(2)}, u32[]{:S(2)}) collective-permute-start(bf16[256,512]{1,0:T(8,128)(2,1)S(1)} %collective-permute-done.4.refs_3_), channel_id=1, source_target_pairs={{0,32},{32,0},{1,33},{33,1},{2,34},{34,2},{3,35},{35,3},{4,36},{36... | collective-permute-start | bytes 786440 | tf_op jit(solution)/shard_map/ppermute | solution.py:30
  75.9 4.8 %collective-permute-start.7 = (bf16[256,512]{1,0:T(8,128)(2,1)S(1)}, bf16[256,512]{1,0:T(8,128)(2,1)S(1)}, u32[]{:S(2)}, u32[]{:S(2)}) collective-permute-start(bf16[256,512]{1,0:T(8,128)(2,1)S(1)} %collective-permute-done.3.refs_2_), channel_id=1, source_target_pairs={{0,32},{32,0},{1,33},{33,1},{2,34},{34,2},{3,35},{35,3},{4,36},{36... | collective-permute-start | bytes 786440 | tf_op jit(solution)/shard_map/ppermute | solution.py:30
  78.1 3.8 %collective-permute-start.6 = (bf16[256,512]{1,0:T(8,128)(2,1)S(1)}, bf16[256,512]{1,0:T(8,128)(2,1)S(1)}, u32[]{:S(2)}, u32[]{:S(2)}) collective-permute-start(bf16[256,512]{1,0:T(8,128)(2,1)S(1)} %collective-permute-done.2.refs_1_), channel_id=1, source_target_pairs={{0,32},{32,0},{1,33},{33,1},{2,34},{34,2},{3,35},{35,3},{4,36},{36... | collective-permute-start | bytes 786440 | tf_op jit(solution)/shard_map/ppermute | solution.py:30
  81.9 0.9 copy-start.5

commit v5 on v3

v5 whole, which is shorter than its diff:
```python
import math

import jax
import jax.numpy as jnp
from jax import lax
from jax.experimental import pallas as pl
from jax.experimental.pallas import tpu as pltpu
from jax.sharding import Mesh
from jax.sharding import PartitionSpec as P

WIDTH = 4

EPSILON = 1e-06
COEFF_ONE = 3.4445
COEFF_THREE = -4.775
COEFF_FIVE = 2.0315

Y = ("yh", "yl")
ALL = ("yh", "yl", "core", "x", "zh", "zl")
MEM = ("x", "zh", "zl")
SPREAD = ("yh", "yl", "x", "zl")
GATHER = ("yh", "x", "zl")
F32 = jnp.float32
BF16 = jnp.bfloat16


def dot(a, b):
    return jnp.dot(a, b, preferred_element_type=F32)


def swap_core(value):
    return lax.ppermute(value, "core", [(0, 1), (1, 0)])


def exchange(value, axes):
    return lax.all_to_all(value, axes, split_axis=0, concat_axis=0, tiled=True)


def outgoing_rows(old_rows, list_ids, owner_map, members):
    row_total = old_rows.shape[0]
    capacity = 2 * row_total // members
    owner = owner_map[list_ids]
    index = jnp.arange(row_total, dtype=jnp.int32)
    earlier = (owner[:, None] == owner[None, :]) & (index[None, :] < index[:, None])
    target = owner * capacity + jnp.sum(earlier.astype(jnp.int32), axis=1)
    slots = jnp.arange(members * capacity, dtype=jnp.int32)
    place = (slots[:, None] == target[None, :]).astype(BF16)
    return dot(place, old_rows).astype(BF16)


def sum_kernel(terms, out):
    total = terms[0].astype(F32)
    for k in range(1, terms.shape[0]):
        total += terms[k].astype(F32)
    for k in range(out.shape[0]):
        out[k] = total.astype(BF16)


def sum_and_copy(terms, copies):
    _, rows, columns = terms.shape
    vmem = pl.BlockSpec(memory_space=pltpu.VMEM)
    return pl.pallas_call(
        sum_kernel,
        out_shape=jax.ShapeDtypeStruct((copies, rows, columns), BF16),
        in_specs=[vmem],
        out_specs=vmem,
        compiler_params=pltpu.CompilerParams(vmem_limit_bytes=8 * 1024 * 1024),
        cost_estimate=pl.CostEstimate(flops=terms.size, bytes_accessed=2**20, transcendentals=0),
        name="sum_and_copy",
    )(terms)


def covariance_slabs(old_rows, new_rows):
    features = old_rows.shape[1]
    half = features // 2
    core = lax.axis_index("core")
    mine = lax.dynamic_slice_in_dim(new_rows, core * half, half, 1)
    theirs = lax.dynamic_slice_in_dim(new_rows, (1 - core) * half, half, 1)
    old_pair = swap_core(old_rows)
    new_pair = swap_core(theirs)
    part = (dot(old_rows.T, mine) + dot(old_pair.T, new_pair)).astype(BF16)
    planes = lax.axis_size(SPREAD)
    depth = lax.axis_size("zh")
    gathered = lax.axis_size(GATHER)
    block = features // planes
    arrived = exchange(part, SPREAD).reshape(planes, block, half)
    copies = sum_and_copy(arrived, depth)
    arrived = exchange(copies, "zh").reshape(depth, block, half)
    copies = sum_and_copy(arrived, gathered)
    return exchange(copies.reshape(gathered * block, half), GATHER)


def polar_kernel(place, mine, got_low, got_high, mine_other, low_other, high_other, *refs):
    result, rotation, start, middle, gram32, gram, poly, sems, out_sems = refs
    rows, half = got_low.shape
    features = 2 * half
    span = [slice(s * rows, (s + 1) * rows) for s in range(WIDTH)]
    pairs = [(s, t) for s in range(WIDTH) for t in range(s, WIDTH)]

    def product(a, b):
        return lax.dot_general(a, b, (((1,), (1,)), ((), ())), preferred_element_type=F32)

    def mirrored(target, s, t, value):
        target[span[s], span[t]] = value.astype(BF16)
        if s != t:
            target[span[t], span[s]] = value.T.astype(BF16)

    arrivals = [
        pltpu.make_async_copy(
            part, start.at[pl.ds(first * rows, part.shape[0]), pl.ds(side * half, half)], sems.at[k]
        )
        for k, (part, first, side) in enumerate(
            (
                (mine, 0, 0),
                (mine_other, 0, 1),
                (got_low, 2, 0),
                (low_other, 2, 1),
                (got_high, 3, 0),
                (high_other, 3, 1),
            )
        )
    ]
    for arrival in arrivals:
        arrival.start()
    for arrival in arrivals:
        arrival.wait()
    squares = jnp.zeros((1, 1), F32)
    diagonal = lax.broadcasted_iota(jnp.int32, (rows, rows), 0) == lax.broadcasted_iota(
        jnp.int32, (rows, rows), 1
    )
    for k, (s, t) in enumerate(pairs):
        value = product(start[span[s], :], start[span[t], :])
        gram32[k] = value
        if s == t:
            squares += jnp.sum(jnp.where(diagonal, value, 0.0), keepdims=True)
    scale = 0.25 * math.sqrt(features) / jnp.sqrt(squares + EPSILON)
    for k, (s, t) in enumerate(pairs):
        mirrored(gram, s, t, gram32[k] * (scale * scale))

    def polynomial():
        for s, t in pairs:
            square = product(gram[span[s], :], gram[span[t], :])
            mirrored(poly, s, t, COEFF_THREE * gram[span[s], span[t]].astype(F32) + COEFF_FIVE * square)

    def advance(source, s):
        moved = jnp.dot(poly[span[s], :], source[...], preferred_element_type=F32)
        return COEFF_ONE * source[span[s], :].astype(F32) + moved

    polynomial()
    for s in range(WIDTH):
        middle[span[s], :] = (advance(start, s) * scale).astype(BF16)
    for s, t in pairs:
        mirrored(gram, s, t, product(middle[span[s], :], middle[span[t], :]))
    polynomial()
    low, core, member = place[0], place[1], place[2]
    order = (low, low + 2, 1 - low, 3 - low)
    stores = []
    for s in range(WIDTH):
        first = pl.multiple_of(order[s] * rows, rows)
        value = advance(middle, s).astype(BF16)
        start[pl.ds(first, rows), pl.ds(pl.multiple_of(core * half, half), half)] = value[:, :half]
        start[pl.ds(first, rows), pl.ds(pl.multiple_of((1 - core) * half, half), half)] = value[:, half:]
        slab = pl.ds(first, rows)
        stores.append(pltpu.make_async_copy(start.at[slab, :], result.at[slab, :], out_sems.at[s]))
        stores[s].start()
    kept = rotation.shape[0]
    rotation[...] = start[pl.ds(pl.multiple_of(member * kept, kept), kept), :]
    for store in stores:
        store.wait()


def polar(place, parts, block_rows):
    rows, half = parts[1].shape
    features = 2 * half
    whole = (features, features)
    vmem = pl.BlockSpec(memory_space=pltpu.VMEM)
    return pl.pallas_call(
        polar_kernel,
        out_shape=(
            pltpu.HBM(whole, BF16),
            jax.ShapeDtypeStruct((block_rows, features), BF16),
        ),
        in_specs=[pl.BlockSpec(memory_space=pltpu.SMEM)]
        + [pl.BlockSpec(memory_space=pl.ANY)] * len(parts),
        out_specs=(pl.BlockSpec(memory_space=pl.ANY), vmem),
        scratch_shapes=[
            pltpu.VMEM(whole, BF16),
            pltpu.VMEM(whole, BF16),
            pltpu.VMEM((WIDTH * (WIDTH + 1) // 2, rows, rows), F32),
            pltpu.VMEM(whole, BF16),
            pltpu.VMEM(whole, BF16),
            pltpu.SemaphoreType.DMA((len(parts),)),
            pltpu.SemaphoreType.DMA((WIDTH,)),
        ],
        compiler_params=pltpu.CompilerParams(vmem_limit_bytes=24 * 1024 * 1024),
        cost_estimate=pl.CostEstimate(flops=9 * features**3, bytes_accessed=2**22, transcendentals=0),
        name="polar",
    )(place, *parts)


def rotate_kernel(rows, factor, out, held, weights, product, row_sem, in_sems, out_sems):
    block = held.shape[1] // in_sems.shape[0]
    parts = range(in_sems.shape[0])
    columns = [pl.ds(k * block, block) for k in parts]

    def fetch(k):
        return pltpu.make_async_copy(factor.at[:, columns[k]], weights.at[:, columns[k]], in_sems.at[k])

    def store(k):
        return pltpu.make_async_copy(product.at[:, columns[k]], out.at[:, columns[k]], out_sems.at[k])

    row_copy = pltpu.make_async_copy(rows, held, row_sem)
    fetch(0).start()
    row_copy.start()
    for k in parts[1:]:
        fetch(k).start()
    row_copy.wait()
    for k in parts:
        fetch(k).wait()
        product[:, columns[k]] = jnp.dot(held[...], weights[:, columns[k]], preferred_element_type=F32)
        store(k).start()
    for k in parts:
        store(k).wait()


def rotate(rows, factor):
    count, features = rows.shape
    parts = 4
    anywhere = pl.BlockSpec(memory_space=pl.ANY)
    return pl.pallas_call(
        rotate_kernel,
        out_shape=jax.ShapeDtypeStruct((count, features), F32),
        in_specs=[anywhere, anywhere],
        out_specs=anywhere,
        scratch_shapes=[
            pltpu.VMEM((count, features), BF16),
            pltpu.VMEM((features, features), BF16),
            pltpu.VMEM((count, features), F32),
            pltpu.SemaphoreType.DMA,
            pltpu.SemaphoreType.DMA((parts,)),
            pltpu.SemaphoreType.DMA((parts,)),
        ],
        compiler_params=pltpu.CompilerParams(vmem_limit_bytes=12 * 1024 * 1024),
        cost_estimate=pl.CostEstimate(
            flops=2 * count * features**2, bytes_accessed=5 * 2**20, transcendentals=0
        ),
        name="rotate",
    )(rows, factor)


def local(old_rows, new_rows, list_ids, owner_map):
    features = old_rows.shape[1]
    members = lax.axis_size(MEM)
    place = jnp.stack([lax.axis_index("yl"), lax.axis_index("core"), lax.axis_index(MEM)])
    sent = outgoing_rows(old_rows, list_ids, owner_map, members)
    mine = covariance_slabs(old_rows, new_rows)
    mine, sent = lax.optimization_barrier((mine, sent))
    received = exchange(sent, MEM)
    rows = mine.shape[0] // 2
    up = [(i, (i + 1) % WIDTH) for i in range(WIDTH)]
    down = [(i, (i - 1) % WIDTH) for i in range(WIDTH)]
    parts = [mine, lax.ppermute(mine[:rows], Y, up), lax.ppermute(mine[rows:], Y, down)]
    parts += [swap_core(part) for part in parts]
    factor, own_rows = polar(place.astype(jnp.int32), parts, features // members)
    factor = pltpu.with_memory_space_constraint(factor, pltpu.HBM)
    return (rotate(received, factor), own_rows)


def solution(mesh):
    shape = mesh.shape
    grid = mesh.devices.reshape(2, WIDTH // 2, 2, 4, shape["mem"] // 8, 2)
    fine = Mesh(grid, ALL)
    in_specs = (P(ALL, None), P(ALL, None), P(ALL), P())
    out_specs = (P(ALL, None), P(MEM, None))
    return jax.shard_map(local, mesh=fine, in_specs=in_specs, out_specs=out_specs, check_vma=False)
```

time: 98.7 us -> 98.7 us (level)
  blocking collectives: 0 us -> 38.4 us
  starting transfers between devices: 42.2 us -> 20.5 us
  waiting for transfers between devices: 28.6 us -> 12.9 us
  local copies, waits for them, and re-layouts: 7.39 us -> 2.34 us
  Pallas kernels: 15.2 us -> 19.5 us
    all_to_all x0 -> x2, blocking collectives: none -> 38.4 us  [exchange(): return lax.all_to_all(value, axes, split_axis=0, concat_axis=0, tiled=True)]
    all_to_all x4 -> x2, waiting for transfers between devices: 27.4 us -> 4.89 us  [exchange(): return lax.all_to_all(value, axes, split_axis=0, concat_axis=0, tiled=True)]
    all_to_all x4 -> x2, starting transfers between devices: 21.4 us -> 8.45 us  [exchange(): return lax.all_to_all(value, axes, split_axis=0, concat_axis=0, tiled=True)]
    ppermute x6 -> x5, starting transfers between devices: 19.2 us -> 10.5 us  [swap_core(): return lax.ppermute(value, 'core', [(0, 1), (1, 0)])]
    ppermute x3 -> x2, waiting for transfers between devices: 0.01 us -> 6.78 us  [the longest x1 6.45 us: local(): lax.ppermute(mine[rows:], Y, down)]
    pallas_call x2 -> x4, Pallas kernels: 15.2 us -> 19.5 us  [the longest x1 13.8 us: polar(): pl.pallas_call(polar_kernel, out_shape=(pltpu.HBM(whole, BF16), jax.Shape...]
    unnamed x12 -> x8, local copies, waits for them, and re-layouts: 2.94 us -> 0.02 us
    broadcast_in_dim x2 -> x0, local copies, waits for them, and re-layouts: 1.39 us -> none  [the longest x1 0.72 us: covariance_of(): copies = jnp.broadcast_to(total[None], (planes // WIDTH, block, half))]
  transfers between devices with their start and end apart: 13 -> 9, of which waited for: 4 -> 4; matrix products, arithmetic and copies ran while one was open for 5% -> 5% of each run, Pallas kernels for 13% -> 14%
where the time goes in v5:
time: 98.7 us; the launch traced here: 98.2 us
  blocking collectives  38.4 us (39%)
  starting transfers between devices  20.5 us (21%)
  Pallas kernels  19.5 us (20%)
  waiting for transfers between devices  12.9 us (13%)
  matrix products  3.39 us (3%)
  local copies, waits for them, and re-layouts  2.34 us (2%)
    all_to_all x2, blocking collectives, exchange(): return lax.all_to_all(value, axes, split_axis=0, concat_axis=0, tiled=True)  38.4 us
    pallas_call x1, Pallas kernels, polar(): pl.pallas_call(polar_kernel, out_shape=(pltpu.HBM(whole, BF16), jax.Shape...  13.8 us
    ppermute x5, starting transfers between devices, swap_core(): return lax.ppermute(value, 'core', [(0, 1), (1, 0)])  10.5 us
    all_to_all x2, starting transfers between devices, exchange(): return lax.all_to_all(value, axes, split_axis=0, concat_axis=0, tiled=True)  8.45 us
    ppermute x1, waiting for transfers between devices, local(): lax.ppermute(mine[rows:], Y, down)  6.45 us
    all_to_all x2, waiting for transfers between devices, exchange(): return lax.all_to_all(value, axes, split_axis=0, concat_axis=0, tiled=True)  4.89 us
    pallas_call x1, Pallas kernels, rotate(): pl.pallas_call(rotate_kernel, out_shape=jax.ShapeDtypeStruct((count, feat...  4.68 us
    dot_general x3, matrix products, dot(): return jnp.dot(a, b, preferred_element_type=F32)  3.39 us
  transfers between devices with their start and end apart: 9, of which 4 were waited for; matrix products, arithmetic and copies ran while one was open for 5% of the time, Pallas kernels for 14%

profile of v5, /device:TPU:1, one launch (start us, length us, event | category | flops | bytes accessed | tf_op | source)
XLA Modules:
  0.0 98.2 jit_solution(7929277102623009079)
XLA Ops:
  0.6 0.0 copy-start
  0.6 3.3 %collective-permute-start.1 = (bf16[256,1024]{1,0:T(8,128)(2,1)}, bf16[256,1024]{1,0:T(8,128)(2,1)S(1)}, u32[]{:S(2)}, u32[]{:S(2)}) collective-permute-start(bf16[256,1024]{1,0:T(8,128)(2,1)} %param.4), channel_id=1, source_target_pairs={{0,32},{32,0},{1,33},{33,1},{2,34},{34,2},{3,35},{35,3},{4,36},{36... | collective-permute-start | bytes 1572872 | tf_op jit(solution)/shard_map/ppermute | solution.py:32
  4.0 0.0 copy-done
  4.0 1.0 %collective-permute-start = (bf16[256,512]{1,0:T(8,128)(2,1)S(1)}, bf16[256,512]{1,0:T(8,128)(2,1)S(1)}, u32[]{:S(2)}, u32[]{:S(2)}) collective-permute-start(bf16[256,512]{1,0:T(8,128)(2,1)S(1)} %constant_dynamic-slice_fusion), channel_id=1, source_target_pairs={{0,32},{32,0},{1,33},{33,1},{2,34},{34,2},{3,35},{35,3},{4,36},{36... | collective-permute-start | bytes 786440 | tf_op jit(solution)/shard_map/ppermute | solution.py:32
  5.0 1.5 %fusion.2 = f32[512,1024]{1,0:T(8,128)S(1)} fusion(bf16[256,1024]{1,0:T(8,128)(2,1)} %param.4, bf16[256,1024]{1,0:T(8,128)(2,1)S(1)} %copy-done, s32[]{:T(128)S(6)} %select_n.9), kind=kOutput, calls=%fused_computation.8 | convolution fusion | flops 268435456 | bytes 2883588 | tf_op jit(solution)/shard_map/dot_general | solution.py:28
  6.5 0.0 collective-permute-done
  6.6 0.0 collective-permute-done.1
  6.6 0.5 fusion
  7.0 0.5 copy.8
  7.6 0.0 copy-start.3
  7.6 23.8 %all_to_all.34.terms = bf16[32,32,512]{2,1,0:T(8,128)(2,1)S(1)} all-to-all(bf16[32,32,512]{2,1,0:T(8,128)(2,1)S(1)} %bitcast.17), channel_id=1, replica_groups=mesh['yh'=2,'yl'=2,'core'=2,'x'=4,'zh'=4,'zl'=2] {'yh','yl','x','zl'}, dimensions={0} | all-to-all | bytes 2097152 | tf_op jit(solution)/shard_map/all_to_all | solution.py:36
  31.4 0.0 copy-start.1
  31.4 0.0 copy-start.2
  31.4 0.1 sum_and_copy.2
  31.6 14.5 %all_to_all.35.terms = bf16[4,32,512]{2,1,0:T(8,128)(2,1)S(1)} all-to-all(bf16[4,32,512]{2,1,0:T(8,128)(2,1)S(1)} %sum_and_copy.2), channel_id=1, replica_groups=mesh['yh'=2,'yl'=2,'core'=2,'x'=4,'zh'=4,'zl'=2] {'zh'}, dimensions={0} | all-to-all | bytes 262144 | tf_op jit(solution)/shard_map/all_to_all | solution.py:36
  46.1 0.8 sum_and_copy.3
  47.0 3.6 %all-to-all-start.2 = ((bf16[16,32,512]{2,1,0:T(8,128)(2,1)}), bf16[16,32,512]{2,1,0:T(8,128)(2,1)S(1)}, u32[]{:S(2)}, u32[]{:S(2)}) async-start(bf16[16,32,512]{2,1,0:T(8,128)(2,1)} %sum_and_copy.3), calls=%async_computation.2 | async-start | bytes 1048576 | tf_op jit(solution)/shard_map/all_to_all | solution.py:36
  50.6 0.0 copy-done.3
  50.6 0.0 copy-done.1
  50.6 1.7 %gather_fusion = s32[256]{0:T(256)S(1)} fusion(s32[65536]{0:T(1024)S(1)} %copy-done.1, s32[1024]{0:T(1024)S(1)} %pad_clamp_fusion), kind=kCustom, calls=%fused_computation | custom fusion | bytes 3072 | tf_op jit(solution)/shard_map/gather | solution.py:42
  52.3 0.2 convert_reduce_fusion
  52.5 0.0 copy-done.2
  52.5 1.4 %convolution_convert_fusion = bf16[512,1024]{1,0:T(8,128)(2,1)} fusion(bf16[256,1024]{1,0:T(8,128)(2,1)S(1)} %copy-done.2, s32[256]{0:T(256)S(1)} %multiply_add_fusion), kind=kOutput, calls=%fused_computation.2 | convolution fusion | flops 269090816 | bytes 1573888 | tf_op jit(solution)/shard_map/dot_general | solution.py:28
  54.0 4.9 %all-to-all-done.2 = bf16[16,32,512]{2,1,0:T(8,128)(2,1)S(1)} async-done(((bf16[16,32,512]{2,1,0:T(8,128)(2,1)}), bf16[16,32,512]{2,1,0:T(8,128)(2,1)S(1)}, u32[]{:S(2)}, u32[]{:S(2)}) %all-to-all-start.2) | async-done | bytes 524320 | tf_op jit(solution)/shard_map/all_to_all | solution.py:36
  58.8 4.9 %all-to-all-start.3 = ((bf16[32,16,1024]{2,1,0:T(8,128)(2,1)}), bf16[32,16,1024]{2,1,0:T(8,128)(2,1)S(1)}, u32[]{:S(2)}, u32[]{:S(2)}) async-start(bf16[32,16,1024]{2,1,0:T(8,128)(2,1)} %bitcast.3), calls=%async_computation.3 | async-start | bytes 2097152 | tf_op jit(solution)/shard_map/all_to_all | solution.py:36
  63.7 4.3 %collective-permute-start.4 = (bf16[512,512]{1,0:T(8,128)(2,1)S(1)}, bf16[512,512]{1,0:T(8,128)(2,1)S(1)}, u32[]{:S(2)}, u32[]{:S(2)}) collective-permute-start(bf16[512,512]{1,0:T(8,128)(2,1)S(1)} %bitcast.14), channel_id=1, source_target_pairs={{0,32},{32,0},{1,33},{33,1},{2,34},{34,2},{3,35},{35,3},{4,36},{36... | collective-permute-start | bytes 1572872 | tf_op jit(solution)/shard_map/ppermute | solution.py:32
  68.1 0.1 collective-permute-start.3
  68.2 1.5 %collective-permute-start.2 = (bf16[256,512]{1,0:T(8,128)(2,1)S(1)}, bf16[256,512]{1,0:T(8,128)(2,1)S(1)}, u32[]{:S(2)}, u32[]{:S(2)}) collective-permute-start(bf16[256,512]{1,0:T(8,128)(2,1)S(1)} %get-tuple-element.11), channel_id=1, source_target_pairs={{0,64},{64,128},{128,192},{192,0},{1,65},{65,129},{129,193},{193,1... | collective-permute-start | bytes 786440 | tf_op jit(solution)/shard_map/ppermute | solution.py:262
  69.7 6.5 %collective-permute-done.3.got_high = bf16[256,512]{1,0:T(8,128)(2,1)S(1)} collective-permute-done((bf16[256,512]{1,0:T(8,128)(2,1)S(1)}, bf16[256,512]{1,0:T(8,128)(2,1)S(1)}, u32[]{:S(2)}, u32[]{:S(2)}) %collective-permute-start.3) | collective-permute-done | bytes 262176 | tf_op jit(solution)/shard_map/ppermute | solution.py:262
  76.1 0.8 collective-permute-start.6
  76.9 0.3 collective-permute-done.2.got_low
  77.2 1.0 collective-permute-start.5
  78.2 0.1 pad_add_fusion.place
  78.3 0.0 collective-permute-done.4.mine_other
  78.3 0.0 collective-permute-done.6.high_other
  78.3 1.2 %collective-permute-done.5.low_other = bf16[256,512]{1,0:T(8,128)(2,1)} collective-permute-done((bf16[256,512]{1,0:T(8,128)(2,1)S(1)}, bf16[256,512]{1,0:T(8,128)(2,1)}, u32[]{:S(2)}, u32[]{:S(2)}) %collective-permute-start.5) | collective-permute-done | bytes 262176 | tf_op jit(solution)/shard_map/ppermute | solution.py:32
  79.5 13.8 %polar.1 = (bf16[1024,1024]{1,0:T(8,128)(2,1)}, bf16[32,1024]{1,0:T(8,128)(2,1)}) custom-call(s32[3]{0:T(128)S(1)} %pad_add_fusion.place, bf16[512,512]{1,0:T(8,128)(2,1)S(1)} %bitcast.16, bf16[256,512]{1,0:T(8,128)(2,1)S(1)} %collective-permute-done.2.got_low, bf16[256,512]{1,0:T(8,128)(2,1)S(1)} %collective-permute-done.3.got_high, ...), custom_call_target="tpu_custom_call" | custom-call | flops 9663676416 | bytes 4194304 | tf_op jit(solution)/shard_map/polar/pallas_call | solution.py:177
  93.3 0.0 all-to-all-done.3
  93.3 4.7 %rotate.1 = f32[512,1024]{1,0:T(8,128)} custom-call(bf16[512,1024]{1,0:T(8,128)(2,1)S(1)} %bitcast.13, bf16[1024,1024]{1,0:T(8,128)(2,1)} %get-tuple-element.8.factor), custom_call_target="tpu_custom_call" | custom-call | flops 1073741824 | bytes 5242880 | tf_op jit(solution)/shard_map/rotate/pallas_call | solution.py:230
  (5 shorter events, 0.1 us)
Async XLA Ops:
  0.6 3.3 %copy-start = (bf16[256,1024]{1,0:T(8,128)(2,1)S(1)}, bf16[256,1024]{1,0:T(8,128)(2,1)}, u32[]{:S(2)}) copy-start(bf16[256,1024]{1,0:T(8,128)(2,1)} %param.5) | copy-start | bytes 1572868
  0.6 5.9 %collective-permute-start.1 = (bf16[256,1024]{1,0:T(8,128)(2,1)}, bf16[256,1024]{1,0:T(8,128)(2,1)S(1)}, u32[]{:S(2)}, u32[]{:S(2)}) collective-permute-start(bf16[256,1024]{1,0:T(8,128)(2,1)} %param.4), channel_id=1, source_target_pairs={{0,32},{32,0},{1,33},{33,1},{2,34},{34,2},{3,35},{35,3},{4,36},{36... | collective-permute-start | bytes 1572872 | tf_op jit(solution)/shard_map/ppermute | solution.py:32
  4.0 2.5 %collective-permute-start = (bf16[256,512]{1,0:T(8,128)(2,1)S(1)}, bf16[256,512]{1,0:T(8,128)(2,1)S(1)}, u32[]{:S(2)}, u32[]{:S(2)}) collective-permute-start(bf16[256,512]{1,0:T(8,128)(2,1)S(1)} %constant_dynamic-slice_fusion), channel_id=1, source_target_pairs={{0,32},{32,0},{1,33},{33,1},{2,34},{34,2},{3,35},{35,3},{4,36},{36... | collective-permute-start | bytes 786440 | tf_op jit(solution)/shard_map/ppermute | solution.py:32
  7.6 43.0 %copy-start.3 = (s32[256]{0:T(256)S(1)}, s32[256]{0:T(256)}, u32[]{:S(2)}) copy-start(s32[256]{0:T(256)} %param.6) | copy-start | bytes 3076
  31.4 19.2 %copy-start.1 = (s32[65536]{0:T(1024)S(1)}, s32[65536]{0:T(1024)}, u32[]{:S(2)}) copy-start(s32[65536]{0:T(1024)} %param.7) | copy-start | bytes 786436
  31.4 21.1 %copy-start.2 = (bf16[256,1024]{1,0:T(8,128)(2,1)S(1)}, bf16[256,1024]{1,0:T(8,128)(2,1)}, u32[]{:S(2)}) copy-start(bf16[256,1024]{1,0:T(8,128)(2,1)} %param.4) | copy-start | bytes 1572868
  47.0 11.9 %all-to-all-start.2 = ((bf16[16,32,512]{2,1,0:T(8,128)(2,1)}), bf16[16,32,512]{2,1,0:T(8,128)(2,1)S(1)}, u32[]{:S(2)}, u32[]{:S(2)}) async-start(bf16[16,32,512]{2,1,0:T(8,128)(2,1)} %sum_and_copy.3), calls=%async_computation.2 | async-start | bytes 1048576 | tf_op jit(solution)/shard_map/all_to_all | solution.py:36
  58.8 34.5 %all-to-all-start.3 = ((bf16[32,16,1024]{2,1,0:T(8,128)(2,1)}), bf16[32,16,1024]{2,1,0:T(8,128)(2,1)S(1)}, u32[]{:S(2)}, u32[]{:S(2)}) async-start(bf16[32,16,1024]{2,1,0:T(8,128)(2,1)} %bitcast.3), calls=%async_computation.3 | async-start | bytes 2097152 | tf_op jit(solution)/shard_map/all_to_all | solution.py:36
  63.7 14.6 %collective-permute-start.4 = (bf16[512,512]{1,0:T(8,128)(2,1)S(1)}, bf16[512,512]{1,0:T(8,128)(2,1)S(1)}, u32[]{:S(2)}, u32[]{:S(2)}) collective-permute-start(bf16[512,512]{1,0:T(8,128)(2,1)S(1)} %bitcast.14), channel_id=1, source_target_pairs={{0,32},{32,0},{1,33},{33,1},{2,34},{34,2},{3,35},{35,3},{4,36},{36... | collective-permute-start | bytes 1572872 | tf_op jit(solution)/shard_map/ppermute | solution.py:32
  68.1 8.0 %collective-permute-start.3 = (bf16[256,512]{1,0:T(8,128)(2,1)S(1)}, bf16[256,512]{1,0:T(8,128)(2,1)S(1)}, u32[]{:S(2)}, u32[]{:S(2)}) collective-permute-start(bf16[256,512]{1,0:T(8,128)(2,1)S(1)} %get-tuple-element.10), channel_id=1, source_target_pairs={{0,192},{64,0},{128,64},{192,128},{1,193},{65,1},{129,65},{193,129... | collective-permute-start | bytes 786440 | tf_op jit(solution)/shard_map/ppermute | solution.py:262
  68.2 9.0 %collective-permute-start.2 = (bf16[256,512]{1,0:T(8,128)(2,1)S(1)}, bf16[256,512]{1,0:T(8,128)(2,1)S(1)}, u32[]{:S(2)}, u32[]{:S(2)}) collective-permute-start(bf16[256,512]{1,0:T(8,128)(2,1)S(1)} %get-tuple-element.11), channel_id=1, source_target_pairs={{0,64},{64,128},{128,192},{192,0},{1,65},{65,129},{129,193},{193,1... | collective-permute-start | bytes 786440 | tf_op jit(solution)/shard_map/ppermute | solution.py:262
  76.1 2.2 %collective-permute-start.6 = (bf16[256,512]{1,0:T(8,128)(2,1)S(1)}, bf16[256,512]{1,0:T(8,128)(2,1)S(1)}, u32[]{:S(2)}, u32[]{:S(2)}) collective-permute-start(bf16[256,512]{1,0:T(8,128)(2,1)S(1)} %collective-permute-done.3.got_high), channel_id=1, source_target_pairs={{0,32},{32,0},{1,33},{33,1},{2,34},{34,2},{3,35},{35,3},{4,36},{36... | collective-permute-start | bytes 786440 | tf_op jit(solution)/shard_map/ppermute | solution.py:32
  77.2 2.3 %collective-permute-start.5 = (bf16[256,512]{1,0:T(8,128)(2,1)S(1)}, bf16[256,512]{1,0:T(8,128)(2,1)}, u32[]{:S(2)}, u32[]{:S(2)}) collective-permute-start(bf16[256,512]{1,0:T(8,128)(2,1)S(1)} %collective-permute-done.2.got_low), channel_id=1, source_target_pairs={{0,32},{32,0},{1,33},{33,1},{2,34},{34,2},{3,35},{35,3},{4,36},{36... | collective-permute-start | bytes 786440 | tf_op jit(solution)/shard_map/ppermute | solution.py:32

commit v6 on v5

--- a/solution.py
+++ b/solution.py
@@ -91,11 +91,11 @@
 
 
 def polar_kernel(place, mine, got_low, got_high, mine_other, low_other, high_other, *refs):
-    result, rotation, start, middle, gram32, gram, poly, sems, out_sems = refs
+    result, rotation, start, middle, gram32, gram, poly, sems = refs
     rows, half = got_low.shape
     features = 2 * half
     span = [slice(s * rows, (s + 1) * rows) for s in range(WIDTH)]
-    pairs = [(s, t) for s in range(WIDTH) for t in range(s, WIDTH)]
+    pairs = [(s, t) for t in range(WIDTH) for s in range(t + 1)]
 
     def product(a, b):
         return lax.dot_general(a, b, (((1,), (1,)), ((), ())), preferred_element_type=F32)
@@ -122,13 +122,14 @@
     ]
     for arrival in arrivals:
         arrival.start()
-    for arrival in arrivals:
-        arrival.wait()
     squares = jnp.zeros((1, 1), F32)
     diagonal = lax.broadcasted_iota(jnp.int32, (rows, rows), 0) == lax.broadcasted_iota(
         jnp.int32, (rows, rows), 1
     )
     for k, (s, t) in enumerate(pairs):
+        if s == 0 and t != 1:
+            for arrival in arrivals[2 * max(t - 1, 0) : 2 * max(t - 1, 0) + 2]:
+                arrival.wait()
         value = product(start[span[s], :], start[span[t], :])
         gram32[k] = value
         if s == t:
@@ -154,19 +155,13 @@
     polynomial()
     low, core, member = place[0], place[1], place[2]
     order = (low, low + 2, 1 - low, 3 - low)
-    stores = []
     for s in range(WIDTH):
         first = pl.multiple_of(order[s] * rows, rows)
         value = advance(middle, s).astype(BF16)
-        start[pl.ds(first, rows), pl.ds(pl.multiple_of(core * half, half), half)] = value[:, :half]
-        start[pl.ds(first, rows), pl.ds(pl.multiple_of((1 - core) * half, half), half)] = value[:, half:]
-        slab = pl.ds(first, rows)
-        stores.append(pltpu.make_async_copy(start.at[slab, :], result.at[slab, :], out_sems.at[s]))
-        stores[s].start()
+        result[pl.ds(first, rows), pl.ds(pl.multiple_of(core * half, half), half)] = value[:, :half]
+        result[pl.ds(first, rows), pl.ds(pl.multiple_of((1 - core) * half, half), half)] = value[:, half:]
     kept = rotation.shape[0]
-    rotation[...] = start[pl.ds(pl.multiple_of(member * kept, kept), kept), :]
-    for store in stores:
-        store.wait()
+    rotation[...] = result[pl.ds(pl.multiple_of(member * kept, kept), kept), :]
 
 
 def polar(place, parts, block_rows):
@@ -177,12 +172,12 @@
     return pl.pallas_call(
         polar_kernel,
         out_shape=(
-            pltpu.HBM(whole, BF16),
+            jax.ShapeDtypeStruct(whole, BF16),
             jax.ShapeDtypeStruct((block_rows, features), BF16),
         ),
         in_specs=[pl.BlockSpec(memory_space=pltpu.SMEM)]
         + [pl.BlockSpec(memory_space=pl.ANY)] * len(parts),
-        out_specs=(pl.BlockSpec(memory_space=pl.ANY), vmem),
+        out_specs=(vmem, vmem),
         scratch_shapes=[
             pltpu.VMEM(whole, BF16),
             pltpu.VMEM(whole, BF16),
@@ -190,7 +185,6 @@
             pltpu.VMEM(whole, BF16),
             pltpu.VMEM(whole, BF16),
             pltpu.SemaphoreType.DMA((len(parts),)),
-            pltpu.SemaphoreType.DMA((WIDTH,)),
         ],
         compiler_params=pltpu.CompilerParams(vmem_limit_bytes=24 * 1024 * 1024),
         cost_estimate=pl.CostEstimate(flops=9 * features**3, bytes_accessed=2**22, transcendentals=0),
@@ -198,26 +192,21 @@
     )(place, *parts)
 
 
-def rotate_kernel(rows, factor, out, held, weights, product, row_sem, in_sems, out_sems):
-    block = held.shape[1] // in_sems.shape[0]
-    parts = range(in_sems.shape[0])
-    columns = [pl.ds(k * block, block) for k in parts]
+def rotate_kernel(rows, factor, out, held, product, in_sems, out_sems):
+    block = held.shape[1]
+    parts = range(held.shape[0])
 
     def fetch(k):
-        return pltpu.make_async_copy(factor.at[:, columns[k]], weights.at[:, columns[k]], in_sems.at[k])
+        return pltpu.make_async_copy(rows.at[pl.ds(k * block, block), :], held.at[k], in_sems.at[k])
 
     def store(k):
-        return pltpu.make_async_copy(product.at[:, columns[k]], out.at[:, columns[k]], out_sems.at[k])
-
-    row_copy = pltpu.make_async_copy(rows, held, row_sem)
-    fetch(0).start()
-    row_copy.start()
-    for k in parts[1:]:
+        return pltpu.make_async_copy(product.at[k], out.at[pl.ds(k * block, block), :], out_sems.at[k])
+
+    for k in parts:
         fetch(k).start()
-    row_copy.wait()
     for k in parts:
         fetch(k).wait()
-        product[:, columns[k]] = jnp.dot(held[...], weights[:, columns[k]], preferred_element_type=F32)
+        product[k] = jnp.dot(held[k], factor[...], preferred_element_type=F32)
         store(k).start()
     for k in parts:
         store(k).wait()
@@ -226,17 +215,15 @@
 def rotate(rows, factor):
     count, features = rows.shape
     parts = 4
-    anywhere = pl.BlockSpec(memory_space=pl.ANY)
+    block = count // parts
     return pl.pallas_call(
         rotate_kernel,
         out_shape=jax.ShapeDtypeStruct((count, features), F32),
-        in_specs=[anywhere, anywhere],
-        out_specs=anywhere,
+        in_specs=[pl.BlockSpec(memory_space=pltpu.HBM), pl.BlockSpec(memory_space=pltpu.VMEM)],
+        out_specs=pl.BlockSpec(memory_space=pltpu.HBM),
         scratch_shapes=[
-            pltpu.VMEM((count, features), BF16),
-            pltpu.VMEM((features, features), BF16),
-            pltpu.VMEM((count, features), F32),
-            pltpu.SemaphoreType.DMA,
+            pltpu.VMEM((parts, block, features), BF16),
+            pltpu.VMEM((parts, block, features), F32),
             pltpu.SemaphoreType.DMA((parts,)),
             pltpu.SemaphoreType.DMA((parts,)),
         ],
@@ -261,8 +248,9 @@
     down = [(i, (i - 1) % WIDTH) for i in range(WIDTH)]
     parts = [mine, lax.ppermute(mine[:rows], Y, up), lax.ppermute(mine[rows:], Y, down)]
     parts += [swap_core(part) for part in parts]
+    parts = [pltpu.with_memory_space_constraint(part, pltpu.HBM) for part in parts]
     factor, own_rows = polar(place.astype(jnp.int32), parts, features // members)
-    factor = pltpu.with_memory_space_constraint(factor, pltpu.HBM)
+    received = pltpu.with_memory_space_constraint(received, pltpu.HBM)
     return (rotate(received, factor), own_rows)
 
 

time: 98.7 us -> 98.7 us (level)
  local copies, waits for them, and re-layouts: 2.34 us -> 3.85 us
  Pallas kernels: 19.5 us -> 18.5 us
    unnamed x8 -> x18, local copies, waits for them, and re-layouts: 0.02 us -> 1.54 us
    ppermute x5, waiting for transfers between devices: 1.22 us -> 0.01 us  [swap_core(): return lax.ppermute(value, 'core', [(0, 1), (1, 0)])]
    pallas_call x1, Pallas kernels: 4.68 us -> 3.63 us  [rotate(): pl.pallas_call(rotate_kernel, out_shape=jax.ShapeDtypeStruct((count, feat...]
  transfers between devices with their start and end apart: 9 -> 9, of which waited for: 4 -> 3; matrix products, arithmetic and copies ran while one was open for 5% -> 5% of each run, Pallas kernels for 14% -> 14%
where the time goes in v6:
time: 98.7 us; the launch traced here: 98.1 us
  blocking collectives  38.4 us (39%)
  starting transfers between devices  20.5 us (21%)
  Pallas kernels  18.5 us (19%)
  waiting for transfers between devices  12.2 us (12%)
  local copies, waits for them, and re-layouts  3.85 us (4%)
  matrix products  3.39 us (3%)
    all_to_all x2, blocking collectives, exchange(): return lax.all_to_all(value, axes, split_axis=0, concat_axis=0, tiled=True)  38.4 us
    pallas_call x1, Pallas kernels, polar(): pl.pallas_call(polar_kernel, out_shape=(jax.ShapeDtypeStruct(whole, BF16)...  13.9 us
    ppermute x5, starting transfers between devices, swap_core(): return lax.ppermute(value, 'core', [(0, 1), (1, 0)])  10.4 us
    all_to_all x2, starting transfers between devices, exchange(): return lax.all_to_all(value, axes, split_axis=0, concat_axis=0, tiled=True)  8.58 us
    ppermute x1, waiting for transfers between devices, local(): lax.ppermute(mine[rows:], Y, down)  6.56 us
    all_to_all x2, waiting for transfers between devices, exchange(): return lax.all_to_all(value, axes, split_axis=0, concat_axis=0, tiled=True)  4.89 us
    pallas_call x1, Pallas kernels, rotate(): pl.pallas_call(rotate_kernel, out_shape=jax.ShapeDtypeStruct((count, feat...  3.63 us
    dot_general x3, matrix products, dot(): return jnp.dot(a, b, preferred_element_type=F32)  3.39 us
  transfers between devices with their start and end apart: 9, of which 3 were waited for; matrix products, arithmetic and copies ran while one was open for 5% of the time, Pallas kernels for 14%

profile of v6, /device:TPU:1, one launch (start us, length us, event | category | flops | bytes accessed | tf_op | source)
XLA Modules:
  0.0 98.1 jit_solution(8855712852042128237)
XLA Ops:
  0.6 0.0 copy-start
  0.6 3.3 %collective-permute-start.1 = (bf16[256,1024]{1,0:T(8,128)(2,1)}, bf16[256,1024]{1,0:T(8,128)(2,1)S(1)}, u32[]{:S(2)}, u32[]{:S(2)}) collective-permute-start(bf16[256,1024]{1,0:T(8,128)(2,1)} %param.4), channel_id=1, source_target_pairs={{0,32},{32,0},{1,33},{33,1},{2,34},{34,2},{3,35},{35,3},{4,36},{36... | collective-permute-start | bytes 1572872 | tf_op jit(solution)/shard_map/ppermute | solution.py:32
  4.0 0.0 copy-done
  4.0 1.0 %collective-permute-start = (bf16[256,512]{1,0:T(8,128)(2,1)S(1)}, bf16[256,512]{1,0:T(8,128)(2,1)S(1)}, u32[]{:S(2)}, u32[]{:S(2)}) collective-permute-start(bf16[256,512]{1,0:T(8,128)(2,1)S(1)} %constant_dynamic-slice_fusion), channel_id=1, source_target_pairs={{0,32},{32,0},{1,33},{33,1},{2,34},{34,2},{3,35},{35,3},{4,36},{36... | collective-permute-start | bytes 786440 | tf_op jit(solution)/shard_map/ppermute | solution.py:32
  5.0 1.5 %fusion.2 = f32[512,1024]{1,0:T(8,128)S(1)} fusion(bf16[256,1024]{1,0:T(8,128)(2,1)} %param.4, bf16[256,1024]{1,0:T(8,128)(2,1)S(1)} %copy-done, s32[]{:T(128)S(6)} %select_n.9), kind=kOutput, calls=%fused_computation.8 | convolution fusion | flops 268435456 | bytes 2883588 | tf_op jit(solution)/shard_map/dot_general | solution.py:28
  6.5 0.0 collective-permute-done
  6.6 0.0 collective-permute-done.1
  6.6 0.5 fusion
  7.0 0.5 copy.8
  7.6 0.0 copy-start.4
  7.6 23.8 %all_to_all.34.terms = bf16[32,32,512]{2,1,0:T(8,128)(2,1)S(1)} all-to-all(bf16[32,32,512]{2,1,0:T(8,128)(2,1)S(1)} %bitcast.13), channel_id=1, replica_groups=mesh['yh'=2,'yl'=2,'core'=2,'x'=4,'zh'=4,'zl'=2] {'yh','yl','x','zl'}, dimensions={0} | all-to-all | bytes 2097152 | tf_op jit(solution)/shard_map/all_to_all | solution.py:36
  31.4 0.0 copy-start.1
  31.4 0.0 copy-start.3
  31.4 0.1 sum_and_copy.2
  31.6 14.5 %all_to_all.35.terms = bf16[4,32,512]{2,1,0:T(8,128)(2,1)S(1)} all-to-all(bf16[4,32,512]{2,1,0:T(8,128)(2,1)S(1)} %sum_and_copy.2), channel_id=1, replica_groups=mesh['yh'=2,'yl'=2,'core'=2,'x'=4,'zh'=4,'zl'=2] {'zh'}, dimensions={0} | all-to-all | bytes 262144 | tf_op jit(solution)/shard_map/all_to_all | solution.py:36
  46.1 0.9 sum_and_copy.3
  47.0 3.6 %all-to-all-start.2 = ((bf16[16,32,512]{2,1,0:T(8,128)(2,1)}), bf16[16,32,512]{2,1,0:T(8,128)(2,1)S(1)}, u32[]{:S(2)}, u32[]{:S(2)}) async-start(bf16[16,32,512]{2,1,0:T(8,128)(2,1)} %sum_and_copy.3), calls=%async_computation.2 | async-start | bytes 1048576 | tf_op jit(solution)/shard_map/all_to_all | solution.py:36
  50.6 0.0 copy-done.4
  50.6 0.0 copy-done.1
  50.6 1.7 %gather_fusion = s32[256]{0:T(256)S(1)} fusion(s32[65536]{0:T(1024)S(1)} %copy-done.1, s32[1024]{0:T(1024)S(1)} %pad_clamp_fusion), kind=kCustom, calls=%fused_computation | custom fusion | bytes 3072 | tf_op jit(solution)/shard_map/gather | solution.py:42
  52.3 0.2 convert_reduce_fusion
  52.5 0.0 copy-done.3
  52.5 1.4 %convolution_convert_fusion = bf16[512,1024]{1,0:T(8,128)(2,1)} fusion(bf16[256,1024]{1,0:T(8,128)(2,1)S(1)} %copy-done.3, s32[256]{0:T(256)S(1)} %multiply_add_fusion), kind=kOutput, calls=%fused_computation.2 | convolution fusion | flops 269090816 | bytes 1573888 | tf_op jit(solution)/shard_map/dot_general | solution.py:28
  54.0 4.9 %all-to-all-done.2 = bf16[16,32,512]{2,1,0:T(8,128)(2,1)S(1)} async-done(((bf16[16,32,512]{2,1,0:T(8,128)(2,1)}), bf16[16,32,512]{2,1,0:T(8,128)(2,1)S(1)}, u32[]{:S(2)}, u32[]{:S(2)}) %all-to-all-start.2) | async-done | bytes 524320 | tf_op jit(solution)/shard_map/all_to_all | solution.py:36
  58.8 0.0 copy-start.2
  58.9 5.0 %all-to-all-start.3 = ((bf16[32,16,1024]{2,1,0:T(8,128)(2,1)}), bf16[32,16,1024]{2,1,0:T(8,128)(2,1)}, u32[]{:S(2)}, u32[]{:S(2)}) async-start(bf16[32,16,1024]{2,1,0:T(8,128)(2,1)} %bitcast.3), calls=%async_computation.3 | async-start | bytes 2097152 | tf_op jit(solution)/shard_map/all_to_all | solution.py:36
  63.9 4.3 %collective-permute-start.4 = (bf16[512,512]{1,0:T(8,128)(2,1)S(1)}, bf16[512,512]{1,0:T(8,128)(2,1)S(1)}, u32[]{:S(2)}, u32[]{:S(2)}) collective-permute-start(bf16[512,512]{1,0:T(8,128)(2,1)S(1)} %bitcast.14), channel_id=1, source_target_pairs={{0,32},{32,0},{1,33},{33,1},{2,34},{34,2},{3,35},{35,3},{4,36},{36... | collective-permute-start | bytes 1572872 | tf_op jit(solution)/shard_map/ppermute | solution.py:32
  68.2 0.7 collective-permute-start.3
  68.9 0.9 collective-permute-start.2
  69.8 6.6 %collective-permute-done.3.got_high = bf16[256,512]{1,0:T(8,128)(2,1)S(1)} collective-permute-done((bf16[256,512]{1,0:T(8,128)(2,1)S(1)}, bf16[256,512]{1,0:T(8,128)(2,1)S(1)}, u32[]{:S(2)}, u32[]{:S(2)}) %collective-permute-start.3) | collective-permute-done | bytes 262176 | tf_op jit(solution)/shard_map/ppermute | solution.py:249
  76.3 0.0 copy-start.6
  76.4 0.7 collective-permute-start.6
  77.0 0.8 collective-permute-done.2.got_low
  77.8 0.0 copy-start.7
  77.8 1.0 %collective-permute-start.5 = (bf16[256,512]{1,0:T(8,128)(2,1)S(1)}, bf16[256,512]{1,0:T(8,128)(2,1)}, u32[]{:S(2)}, u32[]{:S(2)}) collective-permute-start(bf16[256,512]{1,0:T(8,128)(2,1)S(1)} %collective-permute-done.2.got_low), channel_id=1, source_target_pairs={{0,32},{32,0},{1,33},{33,1},{2,34},{34,2},{3,35},{35,3},{4,36},{36... | collective-permute-start | bytes 786440 | tf_op jit(solution)/shard_map/ppermute | solution.py:32
  78.8 0.1 pad_add_fusion.place
  78.9 0.0 collective-permute-done.4.mine_other
  78.9 0.0 copy-start.5
  78.9 0.0 collective-permute-done.6.high_other
  78.9 0.0 copy-done.7
  78.9 0.8 copy-done.5
  79.7 0.0 copy-start.8
  79.7 0.7 copy-done.8
  80.4 0.0 collective-permute-done.5.low_other
  80.4 0.0 copy-done.2
  80.4 0.0 copy-done.6
  80.4 13.9 %polar.1 = (bf16[1024,1024]{1,0:T(8,128)(2,1)S(1)}, bf16[32,1024]{1,0:T(8,128)(2,1)}) custom-call(s32[3]{0:T(128)S(1)} %pad_add_fusion.place, bf16[512,512]{1,0:T(8,128)(2,1)} %bitcast.16, bf16[256,512]{1,0:T(8,128)(2,1)} %copy-done.7, bf16[256,512]{1,0:T(8,128)(2,1)} %copy-done.6, bf16[512,512]{1,0:T(8,128)(2,1)} %copy-done.5, ...), custom_call_target="tpu_custom_call" | custom-call | flops 9663676416 | bytes 4194304 | tf_op jit(solution)/shard_map/polar/pallas_call | solution.py:172
  94.3 0.0 all-to-all-done.3
  94.3 3.6 %rotate.1 = f32[512,1024]{1,0:T(8,128)} custom-call(bf16[512,1024]{1,0:T(8,128)(2,1)} %bitcast.4.rows, bf16[1024,1024]{1,0:T(8,128)(2,1)S(1)} %get-tuple-element.8.factor), custom_call_target="tpu_custom_call" | custom-call | flops 1073741824 | bytes 5242880 | tf_op jit(solution)/shard_map/rotate/pallas_call | solution.py:219
  (5 shorter events, 0.1 us)
Async XLA Ops:
  0.6 3.3 %copy-start = (bf16[256,1024]{1,0:T(8,128)(2,1)S(1)}, bf16[256,1024]{1,0:T(8,128)(2,1)}, u32[]{:S(2)}) copy-start(bf16[256,1024]{1,0:T(8,128)(2,1)} %param.5) | copy-start | bytes 1572868
  0.6 5.9 %collective-permute-start.1 = (bf16[256,1024]{1,0:T(8,128)(2,1)}, bf16[256,1024]{1,0:T(8,128)(2,1)S(1)}, u32[]{:S(2)}, u32[]{:S(2)}) collective-permute-start(bf16[256,1024]{1,0:T(8,128)(2,1)} %param.4), channel_id=1, source_target_pairs={{0,32},{32,0},{1,33},{33,1},{2,34},{34,2},{3,35},{35,3},{4,36},{36... | collective-permute-start | bytes 1572872 | tf_op jit(solution)/shard_map/ppermute | solution.py:32
  4.0 2.5 %collective-permute-start = (bf16[256,512]{1,0:T(8,128)(2,1)S(1)}, bf16[256,512]{1,0:T(8,128)(2,1)S(1)}, u32[]{:S(2)}, u32[]{:S(2)}) collective-permute-start(bf16[256,512]{1,0:T(8,128)(2,1)S(1)} %constant_dynamic-slice_fusion), channel_id=1, source_target_pairs={{0,32},{32,0},{1,33},{33,1},{2,34},{34,2},{3,35},{35,3},{4,36},{36... | collective-permute-start | bytes 786440 | tf_op jit(solution)/shard_map/ppermute | solution.py:32
  7.6 43.0 %copy-start.4 = (s32[256]{0:T(256)S(1)}, s32[256]{0:T(256)}, u32[]{:S(2)}) copy-start(s32[256]{0:T(256)} %param.6) | copy-start | bytes 3076
  31.4 19.2 %copy-start.1 = (s32[65536]{0:T(1024)S(1)}, s32[65536]{0:T(1024)}, u32[]{:S(2)}) copy-start(s32[65536]{0:T(1024)} %param.7) | copy-start | bytes 786436
  31.4 21.1 %copy-start.3 = (bf16[256,1024]{1,0:T(8,128)(2,1)S(1)}, bf16[256,1024]{1,0:T(8,128)(2,1)}, u32[]{:S(2)}) copy-start(bf16[256,1024]{1,0:T(8,128)(2,1)} %param.4) | copy-start | bytes 1572868
  47.0 11.9 %all-to-all-start.2 = ((bf16[16,32,512]{2,1,0:T(8,128)(2,1)}), bf16[16,32,512]{2,1,0:T(8,128)(2,1)S(1)}, u32[]{:S(2)}, u32[]{:S(2)}) async-start(bf16[16,32,512]{2,1,0:T(8,128)(2,1)} %sum_and_copy.3), calls=%async_computation.2 | async-start | bytes 1048576 | tf_op jit(solution)/shard_map/all_to_all | solution.py:36
  58.8 21.6 %copy-start.2 = (bf16[16,32,512]{2,1,0:T(8,128)(2,1)}, bf16[16,32,512]{2,1,0:T(8,128)(2,1)S(1)}, u32[]{:S(2)}) copy-start(bf16[16,32,512]{2,1,0:T(8,128)(2,1)S(1)} %all-to-all-done.2) | copy-start | bytes 1572868
  58.9 35.5 %all-to-all-start.3 = ((bf16[32,16,1024]{2,1,0:T(8,128)(2,1)}), bf16[32,16,1024]{2,1,0:T(8,128)(2,1)}, u32[]{:S(2)}, u32[]{:S(2)}) async-start(bf16[32,16,1024]{2,1,0:T(8,128)(2,1)} %bitcast.3), calls=%async_computation.3 | async-start | bytes 2097152 | tf_op jit(solution)/shard_map/all_to_all | solution.py:36
  63.9 15.0 %collective-permute-start.4 = (bf16[512,512]{1,0:T(8,128)(2,1)S(1)}, bf16[512,512]{1,0:T(8,128)(2,1)S(1)}, u32[]{:S(2)}, u32[]{:S(2)}) collective-permute-start(bf16[512,512]{1,0:T(8,128)(2,1)S(1)} %bitcast.14), channel_id=1, source_target_pairs={{0,32},{32,0},{1,33},{33,1},{2,34},{34,2},{3,35},{35,3},{4,36},{36... | collective-permute-start | bytes 1572872 | tf_op jit(solution)/shard_map/ppermute | solution.py:32
  68.2 8.1 %collective-permute-start.3 = (bf16[256,512]{1,0:T(8,128)(2,1)S(1)}, bf16[256,512]{1,0:T(8,128)(2,1)S(1)}, u32[]{:S(2)}, u32[]{:S(2)}) collective-permute-start(bf16[256,512]{1,0:T(8,128)(2,1)S(1)} %get-tuple-element.10), channel_id=1, source_target_pairs={{0,192},{64,0},{128,64},{192,128},{1,193},{65,1},{129,65},{193,129... | collective-permute-start | bytes 786440 | tf_op jit(solution)/shard_map/ppermute | solution.py:249
  68.9 8.9 %collective-permute-start.2 = (bf16[256,512]{1,0:T(8,128)(2,1)S(1)}, bf16[256,512]{1,0:T(8,128)(2,1)S(1)}, u32[]{:S(2)}, u32[]{:S(2)}) collective-permute-start(bf16[256,512]{1,0:T(8,128)(2,1)S(1)} %get-tuple-element.11), channel_id=1, source_target_pairs={{0,64},{64,128},{128,192},{192,0},{1,65},{65,129},{129,193},{193,1... | collective-permute-start | bytes 786440 | tf_op jit(solution)/shard_map/ppermute | solution.py:249
  76.3 4.1 %copy-start.6 = (bf16[256,512]{1,0:T(8,128)(2,1)}, bf16[256,512]{1,0:T(8,128)(2,1)S(1)}, u32[]{:S(2)}) copy-start(bf16[256,512]{1,0:T(8,128)(2,1)S(1)} %collective-permute-done.3.got_high) | copy-start | bytes 786436
  76.4 2.6 %collective-permute-start.6 = (bf16[256,512]{1,0:T(8,128)(2,1)S(1)}, bf16[256,512]{1,0:T(8,128)(2,1)S(1)}, u32[]{:S(2)}, u32[]{:S(2)}) collective-permute-start(bf16[256,512]{1,0:T(8,128)(2,1)S(1)} %collective-permute-done.3.got_high), channel_id=1, source_target_pairs={{0,32},{32,0},{1,33},{33,1},{2,34},{34,2},{3,35},{35,3},{4,36},{36... | collective-permute-start | bytes 786440 | tf_op jit(solution)/shard_map/ppermute | solution.py:32
  77.8 1.1 %copy-start.7 = (bf16[256,512]{1,0:T(8,128)(2,1)}, bf16[256,512]{1,0:T(8,128)(2,1)S(1)}, u32[]{:S(2)}) copy-start(bf16[256,512]{1,0:T(8,128)(2,1)S(1)} %collective-permute-done.2.got_low) | copy-start | bytes 786436
  77.8 2.6 %collective-permute-start.5 = (bf16[256,512]{1,0:T(8,128)(2,1)S(1)}, bf16[256,512]{1,0:T(8,128)(2,1)}, u32[]{:S(2)}, u32[]{:S(2)}) collective-permute-start(bf16[256,512]{1,0:T(8,128)(2,1)S(1)} %collective-permute-done.2.got_low), channel_id=1, source_target_pairs={{0,32},{32,0},{1,33},{33,1},{2,34},{34,2},{3,35},{35,3},{4,36},{36... | collective-permute-start | bytes 786440 | tf_op jit(solution)/shard_map/ppermute | solution.py:32
  78.9 0.8 copy-start.5
  79.7 0.7 copy-start.8

commit v7 on v6

--- a/solution.py
+++ b/solution.py
@@ -187,7 +187,7 @@
             pltpu.SemaphoreType.DMA((len(parts),)),
         ],
         compiler_params=pltpu.CompilerParams(vmem_limit_bytes=24 * 1024 * 1024),
-        cost_estimate=pl.CostEstimate(flops=9 * features**3, bytes_accessed=2**22, transcendentals=0),
+        cost_estimate=pl.CostEstimate(flops=16 * features**3, bytes_accessed=2**22, transcendentals=0),
         name="polar",
     )(place, *parts)
 

time: 98.7 us -> 102 us (1.033)
  the two profiles are of different devices: /device:TPU:1 before, /device:TPU:32 now
where the time goes in v7:
time: 102 us; the launch traced here: 101 us
  blocking collectives  42.2 us (41%)
  waiting for transfers between devices  19.1 us (19%)
  Pallas kernels  18.5 us (18%)
  starting transfers between devices  11.8 us (12%)
  local copies, waits for them, and re-layouts  4.76 us (5%)
  matrix products  3.39 us (3%)
    all_to_all x2, blocking collectives, exchange(): return lax.all_to_all(value, axes, split_axis=0, concat_axis=0, tiled=True)  42.2 us
    all_to_all x2, waiting for transfers between devices, exchange(): return lax.all_to_all(value, axes, split_axis=0, concat_axis=0, tiled=True)  16 us
    pallas_call x1, Pallas kernels, polar(): pl.pallas_call(polar_kernel, out_shape=(jax.ShapeDtypeStruct(whole, BF16)...  13.9 us
    all_to_all x2, starting transfers between devices, exchange(): return lax.all_to_all(value, axes, split_axis=0, concat_axis=0, tiled=True)  9.46 us
    pallas_call x1, Pallas kernels, rotate(): pl.pallas_call(rotate_kernel, out_shape=jax.ShapeDtypeStruct((count, feat...  3.63 us
    dot_general x3, matrix products, dot(): return jnp.dot(a, b, preferred_element_type=F32)  3.39 us
    unnamed x18, local copies, waits for them, and re-layouts  2.44 us
  transfers between devices with their start and end apart: 9, of which 5 were waited for; matrix products, arithmetic and copies ran while one was open for 5% of the time, Pallas kernels for 14%

profile of v7, /device:TPU:32, one launch (start us, length us, event | category | flops | bytes accessed | tf_op | source)
XLA Modules:
  0.0 101.1 jit_solution(3134820463085285631)
XLA Ops:
  0.6 0.0 copy-start
  0.6 0.1 collective-permute-start.1
  0.8 0.9 copy-done
  1.7 0.1 collective-permute-start
  1.8 1.5 %fusion.2 = f32[512,1024]{1,0:T(8,128)S(1)} fusion(bf16[256,1024]{1,0:T(8,128)(2,1)} %param.4, bf16[256,1024]{1,0:T(8,128)(2,1)S(1)} %copy-done, s32[]{:T(128)S(6)} %select_n.9), kind=kOutput, calls=%fused_computation.8 | convolution fusion | flops 268435456 | bytes 2883588 | tf_op jit(solution)/shard_map/dot_general | solution.py:28
  3.3 0.0 collective-permute-done
  3.3 0.0 collective-permute-done.1
  3.3 0.5 fusion
  3.8 0.5 copy.8
  4.4 0.0 copy-start.4
  4.4 25.7 %all_to_all.34.terms = bf16[32,32,512]{2,1,0:T(8,128)(2,1)S(1)} all-to-all(bf16[32,32,512]{2,1,0:T(8,128)(2,1)S(1)} %bitcast.13), channel_id=1, replica_groups=mesh['yh'=2,'yl'=2,'core'=2,'x'=4,'zh'=4,'zl'=2] {'yh','yl','x','zl'}, dimensions={0} | all-to-all | bytes 2097152 | tf_op jit(solution)/shard_map/all_to_all | solution.py:36
  30.1 0.0 copy-start.1
  30.1 0.0 copy-start.3
  30.1 0.1 sum_and_copy.2
  30.2 16.5 %all_to_all.35.terms = bf16[4,32,512]{2,1,0:T(8,128)(2,1)S(1)} all-to-all(bf16[4,32,512]{2,1,0:T(8,128)(2,1)S(1)} %sum_and_copy.2), channel_id=1, replica_groups=mesh['yh'=2,'yl'=2,'core'=2,'x'=4,'zh'=4,'zl'=2] {'zh'}, dimensions={0} | all-to-all | bytes 262144 | tf_op jit(solution)/shard_map/all_to_all | solution.py:36
  46.7 0.9 sum_and_copy.3
  47.6 4.5 %all-to-all-start.2 = ((bf16[16,32,512]{2,1,0:T(8,128)(2,1)}), bf16[16,32,512]{2,1,0:T(8,128)(2,1)S(1)}, u32[]{:S(2)}, u32[]{:S(2)}) async-start(bf16[16,32,512]{2,1,0:T(8,128)(2,1)} %sum_and_copy.3), calls=%async_computation.2 | async-start | bytes 1048576 | tf_op jit(solution)/shard_map/all_to_all | solution.py:36
  52.0 0.0 copy-done.4
  52.1 0.0 copy-done.1
  52.1 1.7 %gather_fusion = s32[256]{0:T(256)S(1)} fusion(s32[65536]{0:T(1024)S(1)} %copy-done.1, s32[1024]{0:T(1024)S(1)} %pad_clamp_fusion), kind=kCustom, calls=%fused_computation | custom fusion | bytes 3072 | tf_op jit(solution)/shard_map/gather | solution.py:42
  53.8 0.2 convert_reduce_fusion
  54.0 0.0 copy-done.3
  54.0 1.4 %convolution_convert_fusion = bf16[512,1024]{1,0:T(8,128)(2,1)} fusion(bf16[256,1024]{1,0:T(8,128)(2,1)S(1)} %copy-done.3, s32[256]{0:T(256)S(1)} %multiply_add_fusion), kind=kOutput, calls=%fused_computation.2 | convolution fusion | flops 269090816 | bytes 1573888 | tf_op jit(solution)/shard_map/dot_general | solution.py:28
  55.4 6.0 %all-to-all-done.2 = bf16[16,32,512]{2,1,0:T(8,128)(2,1)S(1)} async-done(((bf16[16,32,512]{2,1,0:T(8,128)(2,1)}), bf16[16,32,512]{2,1,0:T(8,128)(2,1)S(1)}, u32[]{:S(2)}, u32[]{:S(2)}) %all-to-all-start.2) | async-done | bytes 524320 | tf_op jit(solution)/shard_map/all_to_all | solution.py:36
  61.4 0.0 copy-start.2
  61.4 0.1 collective-permute-start.4
  61.5 0.6 collective-permute-start.3
  62.1 1.5 %collective-permute-start.2 = (bf16[256,512]{1,0:T(8,128)(2,1)S(1)}, bf16[256,512]{1,0:T(8,128)(2,1)S(1)}, u32[]{:S(2)}, u32[]{:S(2)}) collective-permute-start(bf16[256,512]{1,0:T(8,128)(2,1)S(1)} %get-tuple-element.11), channel_id=1, source_target_pairs={{0,64},{64,128},{128,192},{192,0},{1,65},{65,129},{129,193},{193,1... | collective-permute-start | bytes 786440 | tf_op jit(solution)/shard_map/ppermute | solution.py:249
  63.6 5.0 %all-to-all-start.3 = ((bf16[32,16,1024]{2,1,0:T(8,128)(2,1)}), bf16[32,16,1024]{2,1,0:T(8,128)(2,1)}, u32[]{:S(2)}, u32[]{:S(2)}) async-start(bf16[32,16,1024]{2,1,0:T(8,128)(2,1)} %bitcast.3), calls=%async_computation.3 | async-start | bytes 2097152 | tf_op jit(solution)/shard_map/all_to_all | solution.py:36
  68.7 1.6 %collective-permute-done.3.got_high = bf16[256,512]{1,0:T(8,128)(2,1)S(1)} collective-permute-done((bf16[256,512]{1,0:T(8,128)(2,1)S(1)}, bf16[256,512]{1,0:T(8,128)(2,1)S(1)}, u32[]{:S(2)}, u32[]{:S(2)}) %collective-permute-start.3) | collective-permute-done | bytes 262176 | tf_op jit(solution)/shard_map/ppermute | solution.py:249
  70.3 0.0 copy-start.6
  70.3 0.0 collective-permute-start.6
  70.3 1.4 %collective-permute-done.2.got_low = bf16[256,512]{1,0:T(8,128)(2,1)S(1)} collective-permute-done((bf16[256,512]{1,0:T(8,128)(2,1)S(1)}, bf16[256,512]{1,0:T(8,128)(2,1)S(1)}, u32[]{:S(2)}, u32[]{:S(2)}) %collective-permute-start.2) | collective-permute-done | bytes 262176 | tf_op jit(solution)/shard_map/ppermute | solution.py:249
  71.7 0.0 copy-start.7
  71.7 0.0 collective-permute-start.5
  71.7 0.1 pad_add_fusion.place
  71.8 0.0 collective-permute-done.4.mine_other
  71.8 0.0 copy-start.5
  71.8 0.0 collective-permute-done.6.high_other
  71.8 0.6 copy-done.7
  72.4 0.2 copy-done.5
  72.6 0.0 copy-start.8
  72.6 0.7 copy-done.8
  73.3 0.1 collective-permute-done.5.low_other
  73.4 0.0 copy-done.2
  73.4 0.0 copy-done.6
  73.4 13.9 %polar.1 = (bf16[1024,1024]{1,0:T(8,128)(2,1)S(1)}, bf16[32,1024]{1,0:T(8,128)(2,1)}) custom-call(s32[3]{0:T(128)S(1)} %pad_add_fusion.place, bf16[512,512]{1,0:T(8,128)(2,1)} %bitcast.16, bf16[256,512]{1,0:T(8,128)(2,1)} %copy-done.7, bf16[256,512]{1,0:T(8,128)(2,1)} %copy-done.6, bf16[512,512]{1,0:T(8,128)(2,1)} %copy-done.5, ...), custom_call_target="tpu_custom_call" | custom-call | flops 17179869184 | bytes 4194304 | tf_op jit(solution)/shard_map/polar/pallas_call | solution.py:172
  87.3 10.0 %all-to-all-done.3 = bf16[32,16,1024]{2,1,0:T(8,128)(2,1)} async-done(((bf16[32,16,1024]{2,1,0:T(8,128)(2,1)}), bf16[32,16,1024]{2,1,0:T(8,128)(2,1)}, u32[]{:S(2)}, u32[]{:S(2)}) %all-to-all-start.3) | async-done | bytes 1048608 | tf_op jit(solution)/shard_map/all_to_all | solution.py:36
  97.3 3.6 %rotate.1 = f32[512,1024]{1,0:T(8,128)} custom-call(bf16[512,1024]{1,0:T(8,128)(2,1)} %bitcast.4.rows, bf16[1024,1024]{1,0:T(8,128)(2,1)S(1)} %get-tuple-element.8.factor), custom_call_target="tpu_custom_call" | custom-call | flops 1073741824 | bytes 5242880 | tf_op jit(solution)/shard_map/rotate/pallas_call | solution.py:219
  (5 shorter events, 0.1 us)
Async XLA Ops:
  0.6 1.0 %copy-start = (bf16[256,1024]{1,0:T(8,128)(2,1)S(1)}, bf16[256,1024]{1,0:T(8,128)(2,1)}, u32[]{:S(2)}) copy-start(bf16[256,1024]{1,0:T(8,128)(2,1)} %param.5) | copy-start | bytes 1572868
  0.6 2.7 %collective-permute-start.1 = (bf16[256,1024]{1,0:T(8,128)(2,1)}, bf16[256,1024]{1,0:T(8,128)(2,1)S(1)}, u32[]{:S(2)}, u32[]{:S(2)}) collective-permute-start(bf16[256,1024]{1,0:T(8,128)(2,1)} %param.4), channel_id=1, source_target_pairs={{0,32},{32,0},{1,33},{33,1},{2,34},{34,2},{3,35},{35,3},{4,36},{36... | collective-permute-start | bytes 1572872 | tf_op jit(solution)/shard_map/ppermute | solution.py:32
  1.7 1.6 %collective-permute-start = (bf16[256,512]{1,0:T(8,128)(2,1)S(1)}, bf16[256,512]{1,0:T(8,128)(2,1)S(1)}, u32[]{:S(2)}, u32[]{:S(2)}) collective-permute-start(bf16[256,512]{1,0:T(8,128)(2,1)S(1)} %constant_dynamic-slice_fusion), channel_id=1, source_target_pairs={{0,32},{32,0},{1,33},{33,1},{2,34},{34,2},{3,35},{35,3},{4,36},{36... | collective-permute-start | bytes 786440 | tf_op jit(solution)/shard_map/ppermute | solution.py:32
  4.4 47.7 %copy-start.4 = (s32[256]{0:T(256)S(1)}, s32[256]{0:T(256)}, u32[]{:S(2)}) copy-start(s32[256]{0:T(256)} %param.6) | copy-start | bytes 3076
  30.1 22.0 %copy-start.1 = (s32[65536]{0:T(1024)S(1)}, s32[65536]{0:T(1024)}, u32[]{:S(2)}) copy-start(s32[65536]{0:T(1024)} %param.7) | copy-start | bytes 786436
  30.1 23.9 %copy-start.3 = (bf16[256,1024]{1,0:T(8,128)(2,1)S(1)}, bf16[256,1024]{1,0:T(8,128)(2,1)}, u32[]{:S(2)}) copy-start(bf16[256,1024]{1,0:T(8,128)(2,1)} %param.4) | copy-start | bytes 1572868
  47.6 13.8 %all-to-all-start.2 = ((bf16[16,32,512]{2,1,0:T(8,128)(2,1)}), bf16[16,32,512]{2,1,0:T(8,128)(2,1)S(1)}, u32[]{:S(2)}, u32[]{:S(2)}) async-start(bf16[16,32,512]{2,1,0:T(8,128)(2,1)} %sum_and_copy.3), calls=%async_computation.2 | async-start | bytes 1048576 | tf_op jit(solution)/shard_map/all_to_all | solution.py:36
  61.4 12.0 %copy-start.2 = (bf16[16,32,512]{2,1,0:T(8,128)(2,1)}, bf16[16,32,512]{2,1,0:T(8,128)(2,1)S(1)}, u32[]{:S(2)}) copy-start(bf16[16,32,512]{2,1,0:T(8,128)(2,1)S(1)} %all-to-all-done.2) | copy-start | bytes 1572868
  61.4 10.3 %collective-permute-start.4 = (bf16[512,512]{1,0:T(8,128)(2,1)S(1)}, bf16[512,512]{1,0:T(8,128)(2,1)S(1)}, u32[]{:S(2)}, u32[]{:S(2)}) collective-permute-start(bf16[512,512]{1,0:T(8,128)(2,1)S(1)} %bitcast.15), channel_id=1, source_target_pairs={{0,32},{32,0},{1,33},{33,1},{2,34},{34,2},{3,35},{35,3},{4,36},{36... | collective-permute-start | bytes 1572872 | tf_op jit(solution)/shard_map/ppermute | solution.py:32
  61.5 8.7 %collective-permute-start.3 = (bf16[256,512]{1,0:T(8,128)(2,1)S(1)}, bf16[256,512]{1,0:T(8,128)(2,1)S(1)}, u32[]{:S(2)}, u32[]{:S(2)}) collective-permute-start(bf16[256,512]{1,0:T(8,128)(2,1)S(1)} %get-tuple-element.10), channel_id=1, source_target_pairs={{0,192},{64,0},{128,64},{192,128},{1,193},{65,1},{129,65},{193,129... | collective-permute-start | bytes 786440 | tf_op jit(solution)/shard_map/ppermute | solution.py:249
  62.1 9.6 %collective-permute-start.2 = (bf16[256,512]{1,0:T(8,128)(2,1)S(1)}, bf16[256,512]{1,0:T(8,128)(2,1)S(1)}, u32[]{:S(2)}, u32[]{:S(2)}) collective-permute-start(bf16[256,512]{1,0:T(8,128)(2,1)S(1)} %get-tuple-element.11), channel_id=1, source_target_pairs={{0,64},{64,128},{128,192},{192,0},{1,65},{65,129},{129,193},{193,1... | collective-permute-start | bytes 786440 | tf_op jit(solution)/shard_map/ppermute | solution.py:249
  63.6 33.6 %all-to-all-start.3 = ((bf16[32,16,1024]{2,1,0:T(8,128)(2,1)}), bf16[32,16,1024]{2,1,0:T(8,128)(2,1)}, u32[]{:S(2)}, u32[]{:S(2)}) async-start(bf16[32,16,1024]{2,1,0:T(8,128)(2,1)} %bitcast.3), calls=%async_computation.3 | async-start | bytes 2097152 | tf_op jit(solution)/shard_map/all_to_all | solution.py:36
  70.3 3.1 %copy-start.6 = (bf16[256,512]{1,0:T(8,128)(2,1)}, bf16[256,512]{1,0:T(8,128)(2,1)S(1)}, u32[]{:S(2)}) copy-start(bf16[256,512]{1,0:T(8,128)(2,1)S(1)} %collective-permute-done.3.got_high) | copy-start | bytes 786436
  70.3 1.5 %collective-permute-start.6 = (bf16[256,512]{1,0:T(8,128)(2,1)S(1)}, bf16[256,512]{1,0:T(8,128)(2,1)S(1)}, u32[]{:S(2)}, u32[]{:S(2)}) collective-permute-start(bf16[256,512]{1,0:T(8,128)(2,1)S(1)} %collective-permute-done.3.got_high), channel_id=1, source_target_pairs={{0,32},{32,0},{1,33},{33,1},{2,34},{34,2},{3,35},{35,3},{4,36},{36... | collective-permute-start | bytes 786440 | tf_op jit(solution)/shard_map/ppermute | solution.py:32
  71.7 0.7 copy-start.7
  71.7 1.7 %collective-permute-start.5 = (bf16[256,512]{1,0:T(8,128)(2,1)S(1)}, bf16[256,512]{1,0:T(8,128)(2,1)}, u32[]{:S(2)}, u32[]{:S(2)}) collective-permute-start(bf16[256,512]{1,0:T(8,128)(2,1)S(1)} %collective-permute-done.2.got_low), channel_id=1, source_target_pairs={{0,32},{32,0},{1,33},{33,1},{2,34},{34,2},{3,35},{35,3},{4,36},{36... | collective-permute-start | bytes 786440 | tf_op jit(solution)/shard_map/ppermute | solution.py:32
  71.8 0.8 copy-start.5
  72.6 0.7 copy-start.8

commit v8 on v4

--- a/solution.py
+++ b/solution.py
@@ -18,6 +18,7 @@
 ALL = ("y", "core", "x", "zh", "zl")
 MEM = ("x", "zh", "zl")
 SPREAD = ("y", "x", "zl")
+Z = ("zh", "zl")
 F32 = jnp.float32
 BF16 = jnp.bfloat16
 
@@ -46,38 +47,6 @@
     return dot(place, old_rows).astype(BF16)
 
 
-def product_kernel(place, old_own, new_own, old_pair, new_pair, out):
-    features, half = out.shape
-    block = features // 4
-    mine = new_own[:, pl.ds(pl.multiple_of(place[1] * half, half), half)]
-    for k in range(4):
-        columns = slice(k * block, (k + 1) * block)
-        total = None
-        for old, new in ((old_own, mine), (old_pair, new_pair[...])):
-            term = lax.dot_general(
-                old[:, columns], new, (((0,), (0,)), ((), ())), preferred_element_type=F32
-            )
-            total = term if total is None else total + term
-        out[columns, :] = total.astype(BF16)
-
-
-def pair_product(place, old_own, new_own, old_pair, new_pair):
-    rows, features = old_own.shape
-    half = features // 2
-    vmem = pl.BlockSpec(memory_space=pltpu.VMEM)
-    return pl.pallas_call(
-        product_kernel,
-        out_shape=jax.ShapeDtypeStruct((features, half), BF16),
-        in_specs=[pl.BlockSpec(memory_space=pltpu.SMEM)] + [vmem] * 4,
-        out_specs=vmem,
-        compiler_params=pltpu.CompilerParams(vmem_limit_bytes=12 * 1024 * 1024),
-        cost_estimate=pl.CostEstimate(
-            flops=4 * rows * features * half, bytes_accessed=3 * 2**20, transcendentals=0
-        ),
-        name="pair_product",
-    )(place, old_own, new_own, old_pair, new_pair)
-
-
 def sum_kernel(terms, out):
     total = terms[0].astype(F32)
     for k in range(1, terms.shape[0]):
@@ -100,20 +69,49 @@
     )(terms)
 
 
-def covariance_slab(place, old_rows, new_rows):
+def sum_pair_kernel(terms, out):
+    rows = terms.shape[1]
+    for low in range(2):
+        total = terms[low].astype(F32)
+        for k in range(low + 2, terms.shape[0], 2):
+            total += terms[k].astype(F32)
+        out[low * rows : (low + 1) * rows, :] = total.astype(BF16)
+
+
+def sum_pairs(terms):
+    _, rows, columns = terms.shape
+    vmem = pl.BlockSpec(memory_space=pltpu.VMEM)
+    return pl.pallas_call(
+        sum_pair_kernel,
+        out_shape=jax.ShapeDtypeStruct((2 * rows, columns), BF16),
+        in_specs=[vmem],
+        out_specs=vmem,
+        compiler_params=pltpu.CompilerParams(vmem_limit_bytes=8 * 1024 * 1024),
+        cost_estimate=pl.CostEstimate(flops=terms.size, bytes_accessed=2**19, transcendentals=0),
+        name="sum_pairs",
+    )(terms)
+
+
+def covariance_block(old_rows, new_rows):
     features = old_rows.shape[1]
     half = features // 2
     core = lax.axis_index("core")
+    mine = lax.dynamic_slice_in_dim(new_rows, core * half, half, 1)
     theirs = lax.dynamic_slice_in_dim(new_rows, (1 - core) * half, half, 1)
-    part = pair_product(place, old_rows, new_rows, swap_core(old_rows), swap_core(theirs))
+    old_pair = swap_core(old_rows)
+    new_pair = swap_core(theirs)
+    part = (dot(old_rows.T, mine) + dot(old_pair.T, new_pair)).astype(BF16)
     planes = lax.axis_size(SPREAD)
-    depth = lax.axis_size("zh")
+    depth = lax.axis_size(Z)
     block = features // planes
     arrived = exchange(part, SPREAD).reshape(planes, block, half)
     copies = sum_and_copy(arrived, depth)
-    arrived = exchange(copies, "zh").reshape(depth, block, half)
-    copies = sum_and_copy(arrived, planes // WIDTH)
-    return exchange(copies.reshape(features // WIDTH, half), ("x", "zl"))
+    return sum_pairs(exchange(copies, Z).reshape(depth, block, half))
+
+
+def gather_shifts(value, axis):
+    steps = {s: [(i, (i + s) % WIDTH) for i in range(WIDTH)] for s in range(1, WIDTH)}
+    return [value] + [lax.ppermute(value, axis, steps[s]) for s in range(1, WIDTH)]
 
 
 def polar_kernel(place, *refs):
@@ -168,12 +166,16 @@
     for s, t in pairs:
         mirrored(gram, s, t, product(middle[span[s], :], middle[span[t], :]))
     polynomial()
-    y, core, member = place[0], place[1], place[2]
+    y, core, member, x = place[0], place[1], place[2], place[3]
+    block = rows // WIDTH
+    sides = [pl.ds(pl.multiple_of(side * half, half), half) for side in (core, 1 - core)]
     for s in range(WIDTH):
-        first = pl.multiple_of(lax.rem(y - s + WIDTH, WIDTH) * rows, rows)
         value = advance(middle, s).astype(BF16)
-        result[pl.ds(first, rows), pl.ds(pl.multiple_of(core * half, half), half)] = value[:, :half]
-        result[pl.ds(first, rows), pl.ds(pl.multiple_of((1 - core) * half, half), half)] = value[:, half:]
+        for j in range(WIDTH):
+            first = lax.rem(y - s + WIDTH, WIDTH) * rows + lax.rem(x - j + WIDTH, WIDTH) * block
+            held = value[j * block : (j + 1) * block]
+            result[pl.ds(pl.multiple_of(first, block), block), sides[0]] = held[:, :half]
+            result[pl.ds(pl.multiple_of(first, block), block), sides[1]] = held[:, half:]
     kept = rotation.shape[0]
     rotation[...] = result[pl.ds(pl.multiple_of(member * kept, kept), kept), :]
 
@@ -253,15 +255,13 @@
 def local(old_rows, new_rows, list_ids, owner_map):
     features = old_rows.shape[1]
     members = lax.axis_size(MEM)
-    place = jnp.stack([lax.axis_index("y"), lax.axis_index("core"), lax.axis_index(MEM)])
-    place = place.astype(jnp.int32)
+    place = jnp.stack([lax.axis_index(axis) for axis in ("y", "core", MEM, "x")]).astype(jnp.int32)
     sent = outgoing_rows(old_rows, list_ids, owner_map, members)
-    slab = covariance_slab(place, old_rows, new_rows)
-    slab, sent = lax.optimization_barrier((slab, sent))
+    block = covariance_block(old_rows, new_rows)
+    block, sent = lax.optimization_barrier((block, sent))
     received = exchange(sent, MEM)
-    owns = [slab]
-    for shift in range(1, WIDTH):
-        owns.append(lax.ppermute(slab, "y", [(i, (i + shift) % WIDTH) for i in range(WIDTH)]))
+    slab = jnp.concatenate(gather_shifts(block, "x"), axis=0)
+    owns = gather_shifts(slab, "y")
     others = [swap_core(own) for own in owns]
     factor, own_rows = polar(place, owns, others, features // members)
     return (rotate(received, factor), own_rows)

time: 98.4 us -> 103 us (1.047); the launches traced: 97.8 us -> 101 us
  Pallas kernels: 18.5 us -> 16 us
  matrix products: 1.42 us -> 3.42 us
  starting transfers between devices: 41.2 us -> 43 us
  waiting for transfers between devices: 29.7 us -> 31.2 us
    ppermute x3 -> x6, waiting for transfers between devices: 0.01 us -> 6.24 us  [gather_shifts(): lax.ppermute(value, axis, steps[s])]
    ppermute x3 -> x6, starting transfers between devices: 1.55 us -> 5.75 us  [gather_shifts(): lax.ppermute(value, axis, steps[s])]
    all_to_all x4 -> x3, waiting for transfers between devices: 27.1 us -> 23.7 us  [exchange(): return lax.all_to_all(value, axes, split_axis=0, concat_axis=0, tiled=True)]
    all_to_all x4 -> x3, starting transfers between devices: 21.3 us -> 18 us  [exchange(): return lax.all_to_all(value, axes, split_axis=0, concat_axis=0, tiled=True)]
    pallas_call x1, Pallas kernels: 2.27 us -> 0.04 us  [sum_pairs(): pl.pallas_call(sum_pair_kernel, out_shape=jax.ShapeDtypeStruct((2 * rows,...]
    dot_general x1 -> x3, matrix products: 1.42 us -> 3.42 us  [dot(): return jnp.dot(a, b, preferred_element_type=F32)]
    ppermute x6, waiting for transfers between devices: 2.58 us -> 1.22 us  [swap_core(): return lax.ppermute(value, 'core', [(0, 1), (1, 0)])]
    convert_element_type x0 -> x1, local copies, waits for them, and re-layouts: none -> 1.32 us  [covariance_block(): part = (dot(old_rows.T, mine) + dot(old_pair.T, new_pair)).astype(BF16)]
  transfers between devices with their start and end apart: 13 -> 15, of which waited for: 5 -> 4; matrix products, arithmetic and copies ran while one was open for 4% -> 5% of each run, Pallas kernels for 12% -> 12%
where the time goes in v8:
time: 103 us; the launch traced here: 101 us
  starting transfers between devices  43 us (42%)
  waiting for transfers between devices  31.2 us (30%)
  Pallas kernels  16 us (16%)
  local copies, waits for them, and re-layouts  6.02 us (6%)
  matrix products  3.42 us (3%)
    all_to_all x3, waiting for transfers between devices, exchange(): return lax.all_to_all(value, axes, split_axis=0, concat_axis=0, tiled=True)  23.7 us
    ppermute x6, starting transfers between devices, swap_core(): return lax.ppermute(value, 'core', [(0, 1), (1, 0)])  19.3 us
    all_to_all x3, starting transfers between devices, exchange(): return lax.all_to_all(value, axes, split_axis=0, concat_axis=0, tiled=True)  18 us
    pallas_call x1, Pallas kernels, polar(): pl.pallas_call(polar_kernel, out_shape=(jax.ShapeDtypeStruct(whole, BF16)...  12.3 us
    ppermute x6, waiting for transfers between devices, gather_shifts(): lax.ppermute(value, axis, steps[s])  6.24 us
    ppermute x6, starting transfers between devices, gather_shifts(): lax.ppermute(value, axis, steps[s])  5.75 us
    dot_general x3, matrix products, dot(): return jnp.dot(a, b, preferred_element_type=F32)  3.42 us
    unnamed x15, local copies, waits for them, and re-layouts  2.95 us
  transfers between devices with their start and end apart: 15, of which 4 were waited for; matrix products, arithmetic and copies ran while one was open for 5% of the time, Pallas kernels for 12%

profile of v8, /device:TPU:1, one launch (start us, length us, event | category | flops | bytes accessed | tf_op | source)
XLA Modules:
  0.0 100.8 jit_solution(4184769871071325646)
XLA Ops:
  0.6 0.0 copy-start
  0.6 3.3 %collective-permute-start.1 = (bf16[256,1024]{1,0:T(8,128)(2,1)}, bf16[256,1024]{1,0:T(8,128)(2,1)S(1)}, u32[]{:S(2)}, u32[]{:S(2)}) collective-permute-start(bf16[256,1024]{1,0:T(8,128)(2,1)} %param.4), channel_id=1, source_target_pairs={{0,32},{32,0},{1,33},{33,1},{2,34},{34,2},{3,35},{35,3},{4,36},{36... | collective-permute-start | bytes 1572872 | tf_op jit(solution)/shard_map/ppermute | solution.py:31
  4.0 0.0 copy-done
  4.0 1.0 %collective-permute-start = (bf16[256,512]{1,0:T(8,128)(2,1)S(1)}, bf16[256,512]{1,0:T(8,128)(2,1)S(1)}, u32[]{:S(2)}, u32[]{:S(2)}) collective-permute-start(bf16[256,512]{1,0:T(8,128)(2,1)S(1)} %constant_dynamic-slice_fusion), channel_id=1, source_target_pairs={{0,32},{32,0},{1,33},{33,1},{2,34},{34,2},{3,35},{35,3},{4,36},{36... | collective-permute-start | bytes 786440 | tf_op jit(solution)/shard_map/ppermute | solution.py:31
  5.0 1.5 %fusion.2 = f32[512,1024]{1,0:T(8,128)S(1)} fusion(bf16[256,1024]{1,0:T(8,128)(2,1)} %param.4, bf16[256,1024]{1,0:T(8,128)(2,1)S(1)} %copy-done, s32[]{:T(128)S(6)} %select_n.9), kind=kOutput, calls=%fused_computation.8 | convolution fusion | flops 268435456 | bytes 2883588 | tf_op jit(solution)/shard_map/dot_general | solution.py:27
  6.5 0.0 collective-permute-done
  6.6 0.0 collective-permute-done.1
  6.6 0.5 fusion
  7.0 0.0 copy-start.5
  7.0 0.0 copy-start.3
  7.0 1.3 %copy.8 = bf16[1024,512]{1,0:T(8,128)(2,1)} copy(bf16[1024,512]{0,1:T(8,128)(2,1)S(1)} %fusion) | data formatting | bytes 2097152 | tf_op jit(solution)/shard_map/convert_element_type | solution.py:103
  8.4 0.0 copy-start.4
  8.4 6.8 %all-to-all-start = ((bf16[32,32,512]{2,1,0:T(8,128)(2,1)}), bf16[32,32,512]{2,1,0:T(8,128)(2,1)S(1)}, u32[]{:S(2)}, u32[]{:S(2)}) async-start(bf16[32,32,512]{2,1,0:T(8,128)(2,1)} %bitcast.1), calls=%async_computation | async-start | bytes 2097152 | tf_op jit(solution)/shard_map/all_to_all | solution.py:35
  15.2 0.0 copy-done.5
  15.2 0.0 copy-done.3
  15.2 1.7 %gather_fusion = s32[256]{0:T(256)S(1)} fusion(s32[65536]{0:T(1024)S(1)} %copy-done.3, s32[1024]{0:T(1024)S(1)} %pad_clamp_fusion), kind=kCustom, calls=%fused_computation | custom fusion | bytes 3072 | tf_op jit(solution)/shard_map/gather | solution.py:41
  17.0 0.2 convert_reduce_fusion
  17.1 15.4 %all-to-all-done.terms = bf16[32,32,512]{2,1,0:T(8,128)(2,1)S(1)} async-done(((bf16[32,32,512]{2,1,0:T(8,128)(2,1)}), bf16[32,32,512]{2,1,0:T(8,128)(2,1)S(1)}, u32[]{:S(2)}, u32[]{:S(2)}) %all-to-all-start) | async-done | bytes 1048608 | tf_op jit(solution)/shard_map/all_to_all | solution.py:35
  32.6 0.9 sum_and_copy.1
  33.4 7.3 %all-to-all-start.1 = ((bf16[8,32,512]{2,1,0:T(8,128)(2,1)}), bf16[8,32,512]{2,1,0:T(8,128)(2,1)S(1)}, u32[]{:S(2)}, u32[]{:S(2)}) async-start(bf16[8,32,512]{2,1,0:T(8,128)(2,1)} %sum_and_copy.1), calls=%async_computation.1 | async-start | bytes 524288 | tf_op jit(solution)/shard_map/all_to_all | solution.py:35
  40.7 0.0 copy-done.4
  40.7 1.5 %convolution_convert_fusion = bf16[512,1024]{1,0:T(8,128)(2,1)} fusion(bf16[256,1024]{1,0:T(8,128)(2,1)S(1)} %copy-done.4, s32[256]{0:T(256)S(1)} %multiply_add_fusion), kind=kOutput, calls=%fused_computation.2 | convolution fusion | flops 269090816 | bytes 1573888 | tf_op jit(solution)/shard_map/dot_general | solution.py:27
  42.2 8.3 %all-to-all-done.1.terms = bf16[8,32,512]{2,1,0:T(8,128)(2,1)S(1)} async-done(((bf16[8,32,512]{2,1,0:T(8,128)(2,1)}), bf16[8,32,512]{2,1,0:T(8,128)(2,1)S(1)}, u32[]{:S(2)}, u32[]{:S(2)}) %all-to-all-start.1) | async-done | bytes 262176 | tf_op jit(solution)/shard_map/all_to_all | solution.py:35
  50.5 3.9 %all-to-all-start.2 = ((bf16[32,16,1024]{2,1,0:T(8,128)(2,1)}), bf16[32,16,1024]{2,1,0:T(8,128)(2,1)S(1)}, u32[]{:S(2)}, u32[]{:S(2)}) async-start(bf16[32,16,1024]{2,1,0:T(8,128)(2,1)} %bitcast.2), calls=%async_computation.2 | async-start | bytes 2097152 | tf_op jit(solution)/shard_map/all_to_all | solution.py:35
  54.4 2.6 %collective-permute-start.4 = (bf16[64,512]{1,0:T(8,128)(2,1)S(1)}, bf16[64,512]{1,0:T(8,128)(2,1)S(1)}, u32[]{:S(2)}, u32[]{:S(2)}) collective-permute-start(bf16[64,512]{1,0:T(8,128)(2,1)S(1)} %sum_pairs.1), channel_id=1, source_target_pairs={{0,24},{8,0},{16,8},{24,16},{1,25},{9,1},{17,9},{25,17},{2,26},{10... | collective-permute-start | bytes 196616 | tf_op jit(solution)/shard_map/ppermute | solution.py:114
  57.0 0.5 collective-permute-start.3
  57.5 0.6 collective-permute-start.2
  58.1 6.2 %collective-permute-done.2 = bf16[64,512]{1,0:T(8,128)(2,1)S(1)} collective-permute-done((bf16[64,512]{1,0:T(8,128)(2,1)S(1)}, bf16[64,512]{1,0:T(8,128)(2,1)S(1)}, u32[]{:S(2)}, u32[]{:S(2)}) %collective-permute-start.2) | collective-permute-done | bytes 65568 | tf_op jit(solution)/shard_map/ppermute | solution.py:114
  64.3 0.0 collective-permute-done.3
  64.4 0.0 collective-permute-done.4
  64.4 1.2 %collective-permute-start.7 = (bf16[256,512]{1,0:T(8,128)(2,1)S(1)}, bf16[256,512]{1,0:T(8,128)(2,1)S(1)}, u32[]{:S(2)}, u32[]{:S(2)}) collective-permute-start(bf16[256,512]{1,0:T(8,128)(2,1)S(1)} %constant_dynamic-update-slice_fusion.refs_0_), channel_id=1, source_target_pairs={{0,192},{64,0},{128,64},{192,128},{1,193},{65,1},{129,65},{193,129... | collective-permute-start | bytes 786440 | tf_op jit(solution)/shard_map/ppermute | solution.py:114
  65.5 0.5 collective-permute-start.6
  66.0 0.4 collective-permute-start.5
  66.5 5.2 %collective-permute-start.8 = (bf16[256,512]{1,0:T(8,128)(2,1)S(1)}, bf16[256,512]{1,0:T(8,128)(2,1)S(1)}, u32[]{:S(2)}, u32[]{:S(2)}) collective-permute-start(bf16[256,512]{1,0:T(8,128)(2,1)S(1)} %constant_dynamic-update-slice_fusion.refs_0_), channel_id=1, source_target_pairs={{0,32},{32,0},{1,33},{33,1},{2,34},{34,2},{3,35},{35,3},{4,36},{36... | collective-permute-start | bytes 786440 | tf_op jit(solution)/shard_map/ppermute | solution.py:31
  71.7 0.0 collective-permute-done.7.refs_3_
  71.7 4.3 %collective-permute-start.11 = (bf16[256,512]{1,0:T(8,128)(2,1)S(1)}, bf16[256,512]{1,0:T(8,128)(2,1)S(1)}, u32[]{:S(2)}, u32[]{:S(2)}) collective-permute-start(bf16[256,512]{1,0:T(8,128)(2,1)S(1)} %collective-permute-done.7.refs_3_), channel_id=1, source_target_pairs={{0,32},{32,0},{1,33},{33,1},{2,34},{34,2},{3,35},{35,3},{4,36},{36... | collective-permute-start | bytes 786440 | tf_op jit(solution)/shard_map/ppermute | solution.py:31
  76.0 0.0 collective-permute-done.6.refs_2_
  76.0 2.7 %collective-permute-start.10 = (bf16[256,512]{1,0:T(8,128)(2,1)S(1)}, bf16[256,512]{1,0:T(8,128)(2,1)S(1)}, u32[]{:S(2)}, u32[]{:S(2)}) collective-permute-start(bf16[256,512]{1,0:T(8,128)(2,1)S(1)} %collective-permute-done.6.refs_2_), channel_id=1, source_target_pairs={{0,32},{32,0},{1,33},{33,1},{2,34},{34,2},{3,35},{35,3},{4,36},{36... | collective-permute-start | bytes 786440 | tf_op jit(solution)/shard_map/ppermute | solution.py:31
  78.7 0.0 collective-permute-done.5.refs_1_
  78.7 2.7 %collective-permute-start.9 = (bf16[256,512]{1,0:T(8,128)(2,1)S(1)}, bf16[256,512]{1,0:T(8,128)(2,1)}, u32[]{:S(2)}, u32[]{:S(2)}) collective-permute-start(bf16[256,512]{1,0:T(8,128)(2,1)S(1)} %collective-permute-done.5.refs_1_), channel_id=1, source_target_pairs={{0,32},{32,0},{1,33},{33,1},{2,34},{34,2},{3,35},{35,3},{4,36},{36... | collective-permute-start | bytes 786440 | tf_op jit(solution)/shard_map/ppermute | solution.py:31
  81.4 0.1 pad_add_fusion.place
  81.5 0.0 collective-permute-done.8.refs_4_
  81.5 0.0 collective-permute-done.11.refs_7_
  81.5 0.0 collective-permute-done.10.refs_6_
  81.5 1.2 %collective-permute-done.9.refs_5_ = bf16[256,512]{1,0:T(8,128)(2,1)} collective-permute-done((bf16[256,512]{1,0:T(8,128)(2,1)S(1)}, bf16[256,512]{1,0:T(8,128)(2,1)}, u32[]{:S(2)}, u32[]{:S(2)}) %collective-permute-start.9) | collective-permute-done | bytes 262176 | tf_op jit(solution)/shard_map/ppermute | solution.py:31
  82.7 12.3 %polar.1 = (bf16[1024,1024]{1,0:T(8,128)(2,1)S(1)}, bf16[32,1024]{1,0:T(8,128)(2,1)}) custom-call(s32[4]{0:T(128)S(1)} %pad_add_fusion.place, bf16[256,512]{1,0:T(8,128)(2,1)S(1)} %constant_dynamic-update-slice_fusion.refs_0_, bf16[256,512]{1,0:T(8,128)(2,1)S(1)} %collective-permute-done.5.refs_1_, bf16[256,512]{1,0:T(8,128)(2,1)S(1)} %collective-permute-done.6.refs_2_, ...), custom_call_target="tpu_custom_call" | custom-call | flops 9663676416 | bytes 4194304 | tf_op jit(solution)/shard_map/polar/pallas_call | solution.py:189
  95.0 0.0 copy-start.1
  95.0 1.3 %copy-done.1 = bf16[1024,1024]{1,0:T(8,128)(2,1)} copy-done((bf16[1024,1024]{1,0:T(8,128)(2,1)}, bf16[1024,1024]{1,0:T(8,128)(2,1)S(1)}, u32[]{:S(2)}) %copy-start.1) | copy-done | bytes 2097176
  96.3 0.0 all-to-all-done.2
  96.3 0.0 copy-start.2
  96.3 1.6 %copy-done.2 = bf16[1024,1024]{1,0:T(8,128)(2,1)S(1)} copy-done((bf16[1024,1024]{1,0:T(8,128)(2,1)S(1)}, bf16[1024,1024]{1,0:T(8,128)(2,1)}, u32[]{:S(2)}) %copy-start.2) | copy-done | bytes 2097176
  97.9 2.8 %rotate.1 = f32[512,1024]{1,0:T(8,128)} custom-call(bf16[512,1024]{1,0:T(8,128)(2,1)S(1)} %bitcast.13, bf16[1024,1024]{1,0:T(8,128)(2,1)S(1)} %copy-done.2), custom_call_target="tpu_custom_call" | custom-call | flops 1073741824 | bytes 5242880 | tf_op jit(solution)/shard_map/rotate/pallas_call | solution.py:236
  (9 shorter events, 0.1 us)
Async XLA Ops:
  0.6 3.3 %copy-start = (bf16[256,1024]{1,0:T(8,128)(2,1)S(1)}, bf16[256,1024]{1,0:T(8,128)(2,1)}, u32[]{:S(2)}) copy-start(bf16[256,1024]{1,0:T(8,128)(2,1)} %param.5) | copy-start | bytes 1572868
  0.6 5.9 %collective-permute-start.1 = (bf16[256,1024]{1,0:T(8,128)(2,1)}, bf16[256,1024]{1,0:T(8,128)(2,1)S(1)}, u32[]{:S(2)}, u32[]{:S(2)}) collective-permute-start(bf16[256,1024]{1,0:T(8,128)(2,1)} %param.4), channel_id=1, source_target_pairs={{0,32},{32,0},{1,33},{33,1},{2,34},{34,2},{3,35},{35,3},{4,36},{36... | collective-permute-start | bytes 1572872 | tf_op jit(solution)/shard_map/ppermute | solution.py:31
  4.0 2.5 %collective-permute-start = (bf16[256,512]{1,0:T(8,128)(2,1)S(1)}, bf16[256,512]{1,0:T(8,128)(2,1)S(1)}, u32[]{:S(2)}, u32[]{:S(2)}) collective-permute-start(bf16[256,512]{1,0:T(8,128)(2,1)S(1)} %constant_dynamic-slice_fusion), channel_id=1, source_target_pairs={{0,32},{32,0},{1,33},{33,1},{2,34},{34,2},{3,35},{35,3},{4,36},{36... | collective-permute-start | bytes 786440 | tf_op jit(solution)/shard_map/ppermute | solution.py:31
  7.0 8.2 %copy-start.5 = (s32[256]{0:T(256)S(1)}, s32[256]{0:T(256)}, u32[]{:S(2)}) copy-start(s32[256]{0:T(256)} %param.6) | copy-start | bytes 3076
  7.0 8.2 %copy-start.3 = (s32[65536]{0:T(1024)S(1)}, s32[65536]{0:T(1024)}, u32[]{:S(2)}) copy-start(s32[65536]{0:T(1024)} %param.7) | copy-start | bytes 786436
  8.4 32.3 %copy-start.4 = (bf16[256,1024]{1,0:T(8,128)(2,1)S(1)}, bf16[256,1024]{1,0:T(8,128)(2,1)}, u32[]{:S(2)}) copy-start(bf16[256,1024]{1,0:T(8,128)(2,1)} %param.4) | copy-start | bytes 1572868
  8.4 24.2 %all-to-all-start = ((bf16[32,32,512]{2,1,0:T(8,128)(2,1)}), bf16[32,32,512]{2,1,0:T(8,128)(2,1)S(1)}, u32[]{:S(2)}, u32[]{:S(2)}) async-start(bf16[32,32,512]{2,1,0:T(8,128)(2,1)} %bitcast.1), calls=%async_computation | async-start | bytes 2097152 | tf_op jit(solution)/shard_map/all_to_all | solution.py:35
  33.4 17.0 %all-to-all-start.1 = ((bf16[8,32,512]{2,1,0:T(8,128)(2,1)}), bf16[8,32,512]{2,1,0:T(8,128)(2,1)S(1)}, u32[]{:S(2)}, u32[]{:S(2)}) async-start(bf16[8,32,512]{2,1,0:T(8,128)(2,1)} %sum_and_copy.1), calls=%async_computation.1 | async-start | bytes 524288 | tf_op jit(solution)/shard_map/all_to_all | solution.py:35
  50.5 45.9 %all-to-all-start.2 = ((bf16[32,16,1024]{2,1,0:T(8,128)(2,1)}), bf16[32,16,1024]{2,1,0:T(8,128)(2,1)S(1)}, u32[]{:S(2)}, u32[]{:S(2)}) async-start(bf16[32,16,1024]{2,1,0:T(8,128)(2,1)} %bitcast.2), calls=%async_computation.2 | async-start | bytes 2097152 | tf_op jit(solution)/shard_map/all_to_all | solution.py:35
  54.4 9.9 %collective-permute-start.4 = (bf16[64,512]{1,0:T(8,128)(2,1)S(1)}, bf16[64,512]{1,0:T(8,128)(2,1)S(1)}, u32[]{:S(2)}, u32[]{:S(2)}) collective-permute-start(bf16[64,512]{1,0:T(8,128)(2,1)S(1)} %sum_pairs.1), channel_id=1, source_target_pairs={{0,24},{8,0},{16,8},{24,16},{1,25},{9,1},{17,9},{25,17},{2,26},{10... | collective-permute-start | bytes 196616 | tf_op jit(solution)/shard_map/ppermute | solution.py:114
  57.0 7.3 %collective-permute-start.3 = (bf16[64,512]{1,0:T(8,128)(2,1)S(1)}, bf16[64,512]{1,0:T(8,128)(2,1)S(1)}, u32[]{:S(2)}, u32[]{:S(2)}) collective-permute-start(bf16[64,512]{1,0:T(8,128)(2,1)S(1)} %sum_pairs.1), channel_id=1, source_target_pairs={{0,16},{8,24},{16,0},{24,8},{1,17},{9,25},{17,1},{25,9},{2,18},{10... | collective-permute-start | bytes 196616 | tf_op jit(solution)/shard_map/ppermute | solution.py:114
  57.5 6.9 %collective-permute-start.2 = (bf16[64,512]{1,0:T(8,128)(2,1)S(1)}, bf16[64,512]{1,0:T(8,128)(2,1)S(1)}, u32[]{:S(2)}, u32[]{:S(2)}) collective-permute-start(bf16[64,512]{1,0:T(8,128)(2,1)S(1)} %sum_pairs.1), channel_id=1, source_target_pairs={{0,8},{8,16},{16,24},{24,0},{1,9},{9,17},{17,25},{25,1},{2,10},{10... | collective-permute-start | bytes 196616 | tf_op jit(solution)/shard_map/ppermute | solution.py:114
  64.4 7.3 %collective-permute-start.7 = (bf16[256,512]{1,0:T(8,128)(2,1)S(1)}, bf16[256,512]{1,0:T(8,128)(2,1)S(1)}, u32[]{:S(2)}, u32[]{:S(2)}) collective-permute-start(bf16[256,512]{1,0:T(8,128)(2,1)S(1)} %constant_dynamic-update-slice_fusion.refs_0_), channel_id=1, source_target_pairs={{0,192},{64,0},{128,64},{192,128},{1,193},{65,1},{129,65},{193,129... | collective-permute-start | bytes 786440 | tf_op jit(solution)/shard_map/ppermute | solution.py:114
  65.5 10.5 %collective-permute-start.6 = (bf16[256,512]{1,0:T(8,128)(2,1)S(1)}, bf16[256,512]{1,0:T(8,128)(2,1)S(1)}, u32[]{:S(2)}, u32[]{:S(2)}) collective-permute-start(bf16[256,512]{1,0:T(8,128)(2,1)S(1)} %constant_dynamic-update-slice_fusion.refs_0_), channel_id=1, source_target_pairs={{0,128},{64,192},{128,0},{192,64},{1,129},{65,193},{129,1},{193,65... | collective-permute-start | bytes 786440 | tf_op jit(solution)/shard_map/ppermute | solution.py:114
  66.0 12.7 %collective-permute-start.5 = (bf16[256,512]{1,0:T(8,128)(2,1)S(1)}, bf16[256,512]{1,0:T(8,128)(2,1)S(1)}, u32[]{:S(2)}, u32[]{:S(2)}) collective-permute-start(bf16[256,512]{1,0:T(8,128)(2,1)S(1)} %constant_dynamic-update-slice_fusion.refs_0_), channel_id=1, source_target_pairs={{0,64},{64,128},{128,192},{192,0},{1,65},{65,129},{129,193},{193,1... | collective-permute-start | bytes 786440 | tf_op jit(solution)/shard_map/ppermute | solution.py:114
  66.5 15.0 %collective-permute-start.8 = (bf16[256,512]{1,0:T(8,128)(2,1)S(1)}, bf16[256,512]{1,0:T(8,128)(2,1)S(1)}, u32[]{:S(2)}, u32[]{:S(2)}) collective-permute-start(bf16[256,512]{1,0:T(8,128)(2,1)S(1)} %constant_dynamic-update-slice_fusion.refs_0_), channel_id=1, source_target_pairs={{0,32},{32,0},{1,33},{33,1},{2,34},{34,2},{3,35},{35,3},{4,36},{36... | collective-permute-start | bytes 786440 | tf_op jit(solution)/shard_map/ppermute | solution.py:31
  71.7 9.8 %collective-permute-start.11 = (bf16[256,512]{1,0:T(8,128)(2,1)S(1)}, bf16[256,512]{1,0:T(8,128)(2,1)S(1)}, u32[]{:S(2)}, u32[]{:S(2)}) collective-permute-start(bf16[256,512]{1,0:T(8,128)(2,1)S(1)} %collective-permute-done.7.refs_3_), channel_id=1, source_target_pairs={{0,32},{32,0},{1,33},{33,1},{2,34},{34,2},{3,35},{35,3},{4,36},{36... | collective-permute-start | bytes 786440 | tf_op jit(solution)/shard_map/ppermute | solution.py:31
  76.0 5.5 %collective-permute-start.10 = (bf16[256,512]{1,0:T(8,128)(2,1)S(1)}, bf16[256,512]{1,0:T(8,128)(2,1)S(1)}, u32[]{:S(2)}, u32[]{:S(2)}) collective-permute-start(bf16[256,512]{1,0:T(8,128)(2,1)S(1)} %collective-permute-done.6.refs_2_), channel_id=1, source_target_pairs={{0,32},{32,0},{1,33},{33,1},{2,34},{34,2},{3,35},{35,3},{4,36},{36... | collective-permute-start | bytes 786440 | tf_op jit(solution)/shard_map/ppermute | solution.py:31
  78.7 4.0 %collective-permute-start.9 = (bf16[256,512]{1,0:T(8,128)(2,1)S(1)}, bf16[256,512]{1,0:T(8,128)(2,1)}, u32[]{:S(2)}, u32[]{:S(2)}) collective-permute-start(bf16[256,512]{1,0:T(8,128)(2,1)S(1)} %collective-permute-done.5.refs_1_), channel_id=1, source_target_pairs={{0,32},{32,0},{1,33},{33,1},{2,34},{34,2},{3,35},{35,3},{4,36},{36... | collective-permute-start | bytes 786440 | tf_op jit(solution)/shard_map/ppermute | solution.py:31
  95.0 1.3 %copy-start.1 = (bf16[1024,1024]{1,0:T(8,128)(2,1)}, bf16[1024,1024]{1,0:T(8,128)(2,1)S(1)}, u32[]{:S(2)}) copy-start(bf16[1024,1024]{1,0:T(8,128)(2,1)S(1)} %get-tuple-element.8.factor) | copy-start | bytes 6291460
  96.3 1.6 %copy-start.2 = (bf16[1024,1024]{1,0:T(8,128)(2,1)S(1)}, bf16[1024,1024]{1,0:T(8,128)(2,1)}, u32[]{:S(2)}) copy-start(bf16[1024,1024]{1,0:T(8,128)(2,1)} %copy-done.1) | copy-start | bytes 6291460

commit v9 on v8

--- a/solution.py
+++ b/solution.py
@@ -204,7 +204,7 @@
             pltpu.SemaphoreType.DMA,
         ],
         compiler_params=pltpu.CompilerParams(vmem_limit_bytes=24 * 1024 * 1024),
-        cost_estimate=pl.CostEstimate(flops=9 * features**3, bytes_accessed=2**22, transcendentals=0),
+        cost_estimate=pl.CostEstimate(flops=13 * features**3, bytes_accessed=2**22, transcendentals=0),
         name="polar",
     )(place, *owns, *others)
 

time: 103 us -> 95.4 us (0.926); the launches traced: 101 us -> 94.8 us
  waiting for transfers between devices: 31.2 us -> 25.9 us
    ppermute x6, waiting for transfers between devices: 6.24 us -> 0.95 us  [gather_shifts(): lax.ppermute(value, axis, steps[s])]
    all_to_all x3, starting transfers between devices: 18 us -> 20 us  [exchange(): return lax.all_to_all(value, axes, split_axis=0, concat_axis=0, tiled=True)]
    ppermute x6, starting transfers between devices: 5.75 us -> 3.82 us  [gather_shifts(): lax.ppermute(value, axis, steps[s])]
  transfers between devices with their start and end apart: 15 -> 15, of which waited for: 4 -> 4; matrix products, arithmetic and copies ran while one was open for 5% -> 5% of each run, Pallas kernels for 12% -> 13%
where the time goes in v9:
time: 95.4 us; the launch traced here: 94.8 us
  starting transfers between devices  42.3 us (44%)
  waiting for transfers between devices  25.9 us (27%)
  Pallas kernels  16 us (17%)
  local copies, waits for them, and re-layouts  6.02 us (6%)
  matrix products  3.42 us (4%)
  between operations  1 us (1%)
    all_to_all x3, waiting for transfers between devices, exchange(): return lax.all_to_all(value, axes, split_axis=0, concat_axis=0, tiled=True)  23.7 us
    all_to_all x3, starting transfers between devices, exchange(): return lax.all_to_all(value, axes, split_axis=0, concat_axis=0, tiled=True)  20 us
    ppermute x6, starting transfers between devices, swap_core(): return lax.ppermute(value, 'core', [(0, 1), (1, 0)])  18.4 us
    pallas_call x1, Pallas kernels, polar(): pl.pallas_call(polar_kernel, out_shape=(jax.ShapeDtypeStruct(whole, BF16)...  12.3 us
    ppermute x6, starting transfers between devices, gather_shifts(): lax.ppermute(value, axis, steps[s])  3.82 us
    dot_general x3, matrix products, dot(): return jnp.dot(a, b, preferred_element_type=F32)  3.42 us
    unnamed x15, local copies, waits for them, and re-layouts  2.95 us
    pallas_call x1, Pallas kernels, rotate(): pl.pallas_call(rotate_kernel, out_shape=jax.ShapeDtypeStruct((count, feat...  2.75 us
  transfers between devices with their start and end apart: 15, of which 4 were waited for; matrix products, arithmetic and copies ran while one was open for 5% of the time, Pallas kernels for 13%

profile of v9, /device:TPU:1, one launch (start us, length us, event | category | flops | bytes accessed | tf_op | source)
XLA Modules:
  0.0 94.8 jit_solution(15824823927833459913)
XLA Ops:
  0.6 0.0 copy-start
  0.6 3.3 %collective-permute-start.1 = (bf16[256,1024]{1,0:T(8,128)(2,1)}, bf16[256,1024]{1,0:T(8,128)(2,1)S(1)}, u32[]{:S(2)}, u32[]{:S(2)}) collective-permute-start(bf16[256,1024]{1,0:T(8,128)(2,1)} %param.4), channel_id=1, source_target_pairs={{0,32},{32,0},{1,33},{33,1},{2,34},{34,2},{3,35},{35,3},{4,36},{36... | collective-permute-start | bytes 1572872 | tf_op jit(solution)/shard_map/ppermute | solution.py:31
  4.0 0.0 copy-done
  4.0 1.0 %collective-permute-start = (bf16[256,512]{1,0:T(8,128)(2,1)S(1)}, bf16[256,512]{1,0:T(8,128)(2,1)S(1)}, u32[]{:S(2)}, u32[]{:S(2)}) collective-permute-start(bf16[256,512]{1,0:T(8,128)(2,1)S(1)} %constant_dynamic-slice_fusion), channel_id=1, source_target_pairs={{0,32},{32,0},{1,33},{33,1},{2,34},{34,2},{3,35},{35,3},{4,36},{36... | collective-permute-start | bytes 786440 | tf_op jit(solution)/shard_map/ppermute | solution.py:31
  5.0 1.5 %fusion.2 = f32[512,1024]{1,0:T(8,128)S(1)} fusion(bf16[256,1024]{1,0:T(8,128)(2,1)} %param.4, bf16[256,1024]{1,0:T(8,128)(2,1)S(1)} %copy-done, s32[]{:T(128)S(6)} %select_n.9), kind=kOutput, calls=%fused_computation.8 | convolution fusion | flops 268435456 | bytes 2883588 | tf_op jit(solution)/shard_map/dot_general | solution.py:27
  6.5 0.0 collective-permute-done
  6.6 0.0 collective-permute-done.1
  6.6 0.5 fusion
  7.0 0.0 copy-start.5
  7.0 0.0 copy-start.3
  7.0 1.3 %copy.8 = bf16[1024,512]{1,0:T(8,128)(2,1)} copy(bf16[1024,512]{0,1:T(8,128)(2,1)S(1)} %fusion) | data formatting | bytes 2097152 | tf_op jit(solution)/shard_map/convert_element_type | solution.py:103
  8.4 0.0 copy-start.4
  8.4 6.8 %all-to-all-start = ((bf16[32,32,512]{2,1,0:T(8,128)(2,1)}), bf16[32,32,512]{2,1,0:T(8,128)(2,1)S(1)}, u32[]{:S(2)}, u32[]{:S(2)}) async-start(bf16[32,32,512]{2,1,0:T(8,128)(2,1)} %bitcast.1), calls=%async_computation | async-start | bytes 2097152 | tf_op jit(solution)/shard_map/all_to_all | solution.py:35
  15.2 0.0 copy-done.5
  15.2 0.0 copy-done.3
  15.2 1.7 %gather_fusion = s32[256]{0:T(256)S(1)} fusion(s32[65536]{0:T(1024)S(1)} %copy-done.3, s32[1024]{0:T(1024)S(1)} %pad_clamp_fusion), kind=kCustom, calls=%fused_computation | custom fusion | bytes 3072 | tf_op jit(solution)/shard_map/gather | solution.py:41
  17.0 0.2 convert_reduce_fusion
  17.1 15.4 %all-to-all-done.terms = bf16[32,32,512]{2,1,0:T(8,128)(2,1)S(1)} async-done(((bf16[32,32,512]{2,1,0:T(8,128)(2,1)}), bf16[32,32,512]{2,1,0:T(8,128)(2,1)S(1)}, u32[]{:S(2)}, u32[]{:S(2)}) %all-to-all-start) | async-done | bytes 1048608 | tf_op jit(solution)/shard_map/all_to_all | solution.py:35
  32.6 0.9 sum_and_copy.1
  33.4 7.3 %all-to-all-start.1 = ((bf16[8,32,512]{2,1,0:T(8,128)(2,1)}), bf16[8,32,512]{2,1,0:T(8,128)(2,1)S(1)}, u32[]{:S(2)}, u32[]{:S(2)}) async-start(bf16[8,32,512]{2,1,0:T(8,128)(2,1)} %sum_and_copy.1), calls=%async_computation.1 | async-start | bytes 524288 | tf_op jit(solution)/shard_map/all_to_all | solution.py:35
  40.7 0.0 copy-done.4
  40.7 1.5 %convolution_convert_fusion = bf16[512,1024]{1,0:T(8,128)(2,1)} fusion(bf16[256,1024]{1,0:T(8,128)(2,1)S(1)} %copy-done.4, s32[256]{0:T(256)S(1)} %multiply_add_fusion), kind=kOutput, calls=%fused_computation.2 | convolution fusion | flops 269090816 | bytes 1573888 | tf_op jit(solution)/shard_map/dot_general | solution.py:27
  42.2 8.3 %all-to-all-done.1.terms = bf16[8,32,512]{2,1,0:T(8,128)(2,1)S(1)} async-done(((bf16[8,32,512]{2,1,0:T(8,128)(2,1)}), bf16[8,32,512]{2,1,0:T(8,128)(2,1)S(1)}, u32[]{:S(2)}, u32[]{:S(2)}) %all-to-all-start.1) | async-done | bytes 262176 | tf_op jit(solution)/shard_map/all_to_all | solution.py:35
  50.5 0.7 collective-permute-start.4
  51.2 1.5 %collective-permute-start.3 = (bf16[64,512]{1,0:T(8,128)(2,1)S(1)}, bf16[64,512]{1,0:T(8,128)(2,1)S(1)}, u32[]{:S(2)}, u32[]{:S(2)}) collective-permute-start(bf16[64,512]{1,0:T(8,128)(2,1)S(1)} %sum_pairs.1), channel_id=1, source_target_pairs={{0,16},{8,24},{16,0},{24,8},{1,17},{9,25},{17,1},{25,9},{2,18},{10... | collective-permute-start | bytes 196616 | tf_op jit(solution)/shard_map/ppermute | solution.py:114
  52.8 0.0 collective-permute-start.2
  52.8 6.0 %all-to-all-start.2 = ((bf16[32,16,1024]{2,1,0:T(8,128)(2,1)}), bf16[32,16,1024]{2,1,0:T(8,128)(2,1)S(1)}, u32[]{:S(2)}, u32[]{:S(2)}) async-start(bf16[32,16,1024]{2,1,0:T(8,128)(2,1)} %bitcast.2), calls=%async_computation.2 | async-start | bytes 2097152 | tf_op jit(solution)/shard_map/all_to_all | solution.py:35
  58.7 0.0 collective-permute-done.2
  58.8 0.0 collective-permute-done.3
  58.8 0.0 collective-permute-done.4
  58.8 0.7 collective-permute-start.7
  59.5 0.0 collective-permute-start.6
  59.5 0.8 collective-permute-start.5
  60.4 3.8 %collective-permute-start.8 = (bf16[256,512]{1,0:T(8,128)(2,1)S(1)}, bf16[256,512]{1,0:T(8,128)(2,1)S(1)}, u32[]{:S(2)}, u32[]{:S(2)}) collective-permute-start(bf16[256,512]{1,0:T(8,128)(2,1)S(1)} %constant_dynamic-update-slice_fusion.refs_0_), channel_id=1, source_target_pairs={{0,32},{32,0},{1,33},{33,1},{2,34},{34,2},{3,35},{35,3},{4,36},{36... | collective-permute-start | bytes 786440 | tf_op jit(solution)/shard_map/ppermute | solution.py:31
  64.2 0.0 collective-permute-done.7.refs_3_
  64.2 6.2 %collective-permute-start.11 = (bf16[256,512]{1,0:T(8,128)(2,1)S(1)}, bf16[256,512]{1,0:T(8,128)(2,1)S(1)}, u32[]{:S(2)}, u32[]{:S(2)}) collective-permute-start(bf16[256,512]{1,0:T(8,128)(2,1)S(1)} %collective-permute-done.7.refs_3_), channel_id=1, source_target_pairs={{0,32},{32,0},{1,33},{33,1},{2,34},{34,2},{3,35},{35,3},{4,36},{36... | collective-permute-start | bytes 786440 | tf_op jit(solution)/shard_map/ppermute | solution.py:31
  70.4 0.0 collective-permute-done.6.refs_2_
  70.4 2.3 %collective-permute-start.10 = (bf16[256,512]{1,0:T(8,128)(2,1)S(1)}, bf16[256,512]{1,0:T(8,128)(2,1)S(1)}, u32[]{:S(2)}, u32[]{:S(2)}) collective-permute-start(bf16[256,512]{1,0:T(8,128)(2,1)S(1)} %collective-permute-done.6.refs_2_), channel_id=1, source_target_pairs={{0,32},{32,0},{1,33},{33,1},{2,34},{34,2},{3,35},{35,3},{4,36},{36... | collective-permute-start | bytes 786440 | tf_op jit(solution)/shard_map/ppermute | solution.py:31
  72.7 0.9 collective-permute-done.5.refs_1_
  73.6 1.7 %collective-permute-start.9 = (bf16[256,512]{1,0:T(8,128)(2,1)S(1)}, bf16[256,512]{1,0:T(8,128)(2,1)}, u32[]{:S(2)}, u32[]{:S(2)}) collective-permute-start(bf16[256,512]{1,0:T(8,128)(2,1)S(1)} %collective-permute-done.5.refs_1_), channel_id=1, source_target_pairs={{0,32},{32,0},{1,33},{33,1},{2,34},{34,2},{3,35},{35,3},{4,36},{36... | collective-permute-start | bytes 786440 | tf_op jit(solution)/shard_map/ppermute | solution.py:31
  75.4 0.1 pad_add_fusion.place
  75.4 0.0 collective-permute-done.8.refs_4_
  75.4 0.0 collective-permute-done.11.refs_7_
  75.4 0.0 collective-permute-done.10.refs_6_
  75.5 1.2 %collective-permute-done.9.refs_5_ = bf16[256,512]{1,0:T(8,128)(2,1)} collective-permute-done((bf16[256,512]{1,0:T(8,128)(2,1)S(1)}, bf16[256,512]{1,0:T(8,128)(2,1)}, u32[]{:S(2)}, u32[]{:S(2)}) %collective-permute-start.9) | collective-permute-done | bytes 262176 | tf_op jit(solution)/shard_map/ppermute | solution.py:31
  76.7 12.3 %polar.1 = (bf16[1024,1024]{1,0:T(8,128)(2,1)S(1)}, bf16[32,1024]{1,0:T(8,128)(2,1)}) custom-call(s32[4]{0:T(128)S(1)} %pad_add_fusion.place, bf16[256,512]{1,0:T(8,128)(2,1)S(1)} %constant_dynamic-update-slice_fusion.refs_0_, bf16[256,512]{1,0:T(8,128)(2,1)S(1)} %collective-permute-done.5.refs_1_, bf16[256,512]{1,0:T(8,128)(2,1)S(1)} %collective-permute-done.6.refs_2_, ...), custom_call_target="tpu_custom_call" | custom-call | flops 13958643712 | bytes 4194304 | tf_op jit(solution)/shard_map/polar/pallas_call | solution.py:189
  89.0 0.0 copy-start.1
  89.0 1.3 %copy-done.1 = bf16[1024,1024]{1,0:T(8,128)(2,1)} copy-done((bf16[1024,1024]{1,0:T(8,128)(2,1)}, bf16[1024,1024]{1,0:T(8,128)(2,1)S(1)}, u32[]{:S(2)}) %copy-start.1) | copy-done | bytes 2097176
  90.3 0.0 all-to-all-done.2
  90.3 0.0 copy-start.2
  90.3 1.6 %copy-done.2 = bf16[1024,1024]{1,0:T(8,128)(2,1)S(1)} copy-done((bf16[1024,1024]{1,0:T(8,128)(2,1)S(1)}, bf16[1024,1024]{1,0:T(8,128)(2,1)}, u32[]{:S(2)}) %copy-start.2) | copy-done | bytes 2097176
  91.9 2.8 %rotate.1 = f32[512,1024]{1,0:T(8,128)} custom-call(bf16[512,1024]{1,0:T(8,128)(2,1)S(1)} %bitcast.13, bf16[1024,1024]{1,0:T(8,128)(2,1)S(1)} %copy-done.2), custom_call_target="tpu_custom_call" | custom-call | flops 1073741824 | bytes 5242880 | tf_op jit(solution)/shard_map/rotate/pallas_call | solution.py:236
  (9 shorter events, 0.1 us)
Async XLA Ops:
  0.6 3.3 %copy-start = (bf16[256,1024]{1,0:T(8,128)(2,1)S(1)}, bf16[256,1024]{1,0:T(8,128)(2,1)}, u32[]{:S(2)}) copy-start(bf16[256,1024]{1,0:T(8,128)(2,1)} %param.5) | copy-start | bytes 1572868
  0.6 5.9 %collective-permute-start.1 = (bf16[256,1024]{1,0:T(8,128)(2,1)}, bf16[256,1024]{1,0:T(8,128)(2,1)S(1)}, u32[]{:S(2)}, u32[]{:S(2)}) collective-permute-start(bf16[256,1024]{1,0:T(8,128)(2,1)} %param.4), channel_id=1, source_target_pairs={{0,32},{32,0},{1,33},{33,1},{2,34},{34,2},{3,35},{35,3},{4,36},{36... | collective-permute-start | bytes 1572872 | tf_op jit(solution)/shard_map/ppermute | solution.py:31
  4.0 2.5 %collective-permute-start = (bf16[256,512]{1,0:T(8,128)(2,1)S(1)}, bf16[256,512]{1,0:T(8,128)(2,1)S(1)}, u32[]{:S(2)}, u32[]{:S(2)}) collective-permute-start(bf16[256,512]{1,0:T(8,128)(2,1)S(1)} %constant_dynamic-slice_fusion), channel_id=1, source_target_pairs={{0,32},{32,0},{1,33},{33,1},{2,34},{34,2},{3,35},{35,3},{4,36},{36... | collective-permute-start | bytes 786440 | tf_op jit(solution)/shard_map/ppermute | solution.py:31
  7.0 8.2 %copy-start.5 = (s32[256]{0:T(256)S(1)}, s32[256]{0:T(256)}, u32[]{:S(2)}) copy-start(s32[256]{0:T(256)} %param.6) | copy-start | bytes 3076
  7.0 8.2 %copy-start.3 = (s32[65536]{0:T(1024)S(1)}, s32[65536]{0:T(1024)}, u32[]{:S(2)}) copy-start(s32[65536]{0:T(1024)} %param.7) | copy-start | bytes 786436
  8.4 32.3 %copy-start.4 = (bf16[256,1024]{1,0:T(8,128)(2,1)S(1)}, bf16[256,1024]{1,0:T(8,128)(2,1)}, u32[]{:S(2)}) copy-start(bf16[256,1024]{1,0:T(8,128)(2,1)} %param.4) | copy-start | bytes 1572868
  8.4 24.2 %all-to-all-start = ((bf16[32,32,512]{2,1,0:T(8,128)(2,1)}), bf16[32,32,512]{2,1,0:T(8,128)(2,1)S(1)}, u32[]{:S(2)}, u32[]{:S(2)}) async-start(bf16[32,32,512]{2,1,0:T(8,128)(2,1)} %bitcast.1), calls=%async_computation | async-start | bytes 2097152 | tf_op jit(solution)/shard_map/all_to_all | solution.py:35
  33.4 17.0 %all-to-all-start.1 = ((bf16[8,32,512]{2,1,0:T(8,128)(2,1)}), bf16[8,32,512]{2,1,0:T(8,128)(2,1)S(1)}, u32[]{:S(2)}, u32[]{:S(2)}) async-start(bf16[8,32,512]{2,1,0:T(8,128)(2,1)} %sum_and_copy.1), calls=%async_computation.1 | async-start | bytes 524288 | tf_op jit(solution)/shard_map/all_to_all | solution.py:35
  50.5 8.3 %collective-permute-start.4 = (bf16[64,512]{1,0:T(8,128)(2,1)S(1)}, bf16[64,512]{1,0:T(8,128)(2,1)S(1)}, u32[]{:S(2)}, u32[]{:S(2)}) collective-permute-start(bf16[64,512]{1,0:T(8,128)(2,1)S(1)} %sum_pairs.1), channel_id=1, source_target_pairs={{0,24},{8,0},{16,8},{24,16},{1,25},{9,1},{17,9},{25,17},{2,26},{10... | collective-permute-start | bytes 196616 | tf_op jit(solution)/shard_map/ppermute | solution.py:114
  51.2 7.5 %collective-permute-start.3 = (bf16[64,512]{1,0:T(8,128)(2,1)S(1)}, bf16[64,512]{1,0:T(8,128)(2,1)S(1)}, u32[]{:S(2)}, u32[]{:S(2)}) collective-permute-start(bf16[64,512]{1,0:T(8,128)(2,1)S(1)} %sum_pairs.1), channel_id=1, source_target_pairs={{0,16},{8,24},{16,0},{24,8},{1,17},{9,25},{17,1},{25,9},{2,18},{10... | collective-permute-start | bytes 196616 | tf_op jit(solution)/shard_map/ppermute | solution.py:114
  52.8 6.0 %collective-permute-start.2 = (bf16[64,512]{1,0:T(8,128)(2,1)S(1)}, bf16[64,512]{1,0:T(8,128)(2,1)S(1)}, u32[]{:S(2)}, u32[]{:S(2)}) collective-permute-start(bf16[64,512]{1,0:T(8,128)(2,1)S(1)} %sum_pairs.1), channel_id=1, source_target_pairs={{0,8},{8,16},{16,24},{24,0},{1,9},{9,17},{17,25},{25,1},{2,10},{10... | collective-permute-start | bytes 196616 | tf_op jit(solution)/shard_map/ppermute | solution.py:114
  52.8 37.6 %all-to-all-start.2 = ((bf16[32,16,1024]{2,1,0:T(8,128)(2,1)}), bf16[32,16,1024]{2,1,0:T(8,128)(2,1)S(1)}, u32[]{:S(2)}, u32[]{:S(2)}) async-start(bf16[32,16,1024]{2,1,0:T(8,128)(2,1)} %bitcast.2), calls=%async_computation.2 | async-start | bytes 2097152 | tf_op jit(solution)/shard_map/all_to_all | solution.py:35
  58.8 5.4 %collective-permute-start.7 = (bf16[256,512]{1,0:T(8,128)(2,1)S(1)}, bf16[256,512]{1,0:T(8,128)(2,1)S(1)}, u32[]{:S(2)}, u32[]{:S(2)}) collective-permute-start(bf16[256,512]{1,0:T(8,128)(2,1)S(1)} %constant_dynamic-update-slice_fusion.refs_0_), channel_id=1, source_target_pairs={{0,192},{64,0},{128,64},{192,128},{1,193},{65,1},{129,65},{193,129... | collective-permute-start | bytes 786440 | tf_op jit(solution)/shard_map/ppermute | solution.py:114
  59.5 10.9 %collective-permute-start.6 = (bf16[256,512]{1,0:T(8,128)(2,1)S(1)}, bf16[256,512]{1,0:T(8,128)(2,1)S(1)}, u32[]{:S(2)}, u32[]{:S(2)}) collective-permute-start(bf16[256,512]{1,0:T(8,128)(2,1)S(1)} %constant_dynamic-update-slice_fusion.refs_0_), channel_id=1, source_target_pairs={{0,128},{64,192},{128,0},{192,64},{1,129},{65,193},{129,1},{193,65... | collective-permute-start | bytes 786440 | tf_op jit(solution)/shard_map/ppermute | solution.py:114
  59.5 14.1 %collective-permute-start.5 = (bf16[256,512]{1,0:T(8,128)(2,1)S(1)}, bf16[256,512]{1,0:T(8,128)(2,1)S(1)}, u32[]{:S(2)}, u32[]{:S(2)}) collective-permute-start(bf16[256,512]{1,0:T(8,128)(2,1)S(1)} %constant_dynamic-update-slice_fusion.refs_0_), channel_id=1, source_target_pairs={{0,64},{64,128},{128,192},{192,0},{1,65},{65,129},{129,193},{193,1... | collective-permute-start | bytes 786440 | tf_op jit(solution)/shard_map/ppermute | solution.py:114
  60.4 15.1 %collective-permute-start.8 = (bf16[256,512]{1,0:T(8,128)(2,1)S(1)}, bf16[256,512]{1,0:T(8,128)(2,1)S(1)}, u32[]{:S(2)}, u32[]{:S(2)}) collective-permute-start(bf16[256,512]{1,0:T(8,128)(2,1)S(1)} %constant_dynamic-update-slice_fusion.refs_0_), channel_id=1, source_target_pairs={{0,32},{32,0},{1,33},{33,1},{2,34},{34,2},{3,35},{35,3},{4,36},{36... | collective-permute-start | bytes 786440 | tf_op jit(solution)/shard_map/ppermute | solution.py:31
  64.2 11.3 %collective-permute-start.11 = (bf16[256,512]{1,0:T(8,128)(2,1)S(1)}, bf16[256,512]{1,0:T(8,128)(2,1)S(1)}, u32[]{:S(2)}, u32[]{:S(2)}) collective-permute-start(bf16[256,512]{1,0:T(8,128)(2,1)S(1)} %collective-permute-done.7.refs_3_), channel_id=1, source_target_pairs={{0,32},{32,0},{1,33},{33,1},{2,34},{34,2},{3,35},{35,3},{4,36},{36... | collective-permute-start | bytes 786440 | tf_op jit(solution)/shard_map/ppermute | solution.py:31
  70.4 5.0 %collective-permute-start.10 = (bf16[256,512]{1,0:T(8,128)(2,1)S(1)}, bf16[256,512]{1,0:T(8,128)(2,1)S(1)}, u32[]{:S(2)}, u32[]{:S(2)}) collective-permute-start(bf16[256,512]{1,0:T(8,128)(2,1)S(1)} %collective-permute-done.6.refs_2_), channel_id=1, source_target_pairs={{0,32},{32,0},{1,33},{33,1},{2,34},{34,2},{3,35},{35,3},{4,36},{36... | collective-permute-start | bytes 786440 | tf_op jit(solution)/shard_map/ppermute | solution.py:31
  73.6 3.0 %collective-permute-start.9 = (bf16[256,512]{1,0:T(8,128)(2,1)S(1)}, bf16[256,512]{1,0:T(8,128)(2,1)}, u32[]{:S(2)}, u32[]{:S(2)}) collective-permute-start(bf16[256,512]{1,0:T(8,128)(2,1)S(1)} %collective-permute-done.5.refs_1_), channel_id=1, source_target_pairs={{0,32},{32,0},{1,33},{33,1},{2,34},{34,2},{3,35},{35,3},{4,36},{36... | collective-permute-start | bytes 786440 | tf_op jit(solution)/shard_map/ppermute | solution.py:31
  89.0 1.3 %copy-start.1 = (bf16[1024,1024]{1,0:T(8,128)(2,1)}, bf16[1024,1024]{1,0:T(8,128)(2,1)S(1)}, u32[]{:S(2)}) copy-start(bf16[1024,1024]{1,0:T(8,128)(2,1)S(1)} %get-tuple-element.8.factor) | copy-start | bytes 6291460
  90.3 1.6 %copy-start.2 = (bf16[1024,1024]{1,0:T(8,128)(2,1)S(1)}, bf16[1024,1024]{1,0:T(8,128)(2,1)}, u32[]{:S(2)}) copy-start(bf16[1024,1024]{1,0:T(8,128)(2,1)} %copy-done.1) | copy-start | bytes 6291460

commit v10 on v9

--- a/solution.py
+++ b/solution.py
@@ -117,7 +117,7 @@
 def polar_kernel(place, *refs):
     owns, others = refs[0:WIDTH], refs[WIDTH : 2 * WIDTH]
     result, rotation = refs[2 * WIDTH : 2 * WIDTH + 2]
-    start, middle, gram32, gram, poly, slab_sem = refs[2 * WIDTH + 2 :]
+    start, middle, gram32, gram, poly, slab_sem, out_sems = refs[2 * WIDTH + 2 :]
     rows, half = owns[0].shape
     features = 2 * half
     span = [slice(s * rows, (s + 1) * rows) for s in range(WIDTH)]
@@ -169,15 +169,22 @@
     y, core, member, x = place[0], place[1], place[2], place[3]
     block = rows // WIDTH
     sides = [pl.ds(pl.multiple_of(side * half, half), half) for side in (core, 1 - core)]
+    stores = []
     for s in range(WIDTH):
         value = advance(middle, s).astype(BF16)
+        base = lax.rem(y - s + WIDTH, WIDTH) * rows
         for j in range(WIDTH):
-            first = lax.rem(y - s + WIDTH, WIDTH) * rows + lax.rem(x - j + WIDTH, WIDTH) * block
+            first = base + lax.rem(x - j + WIDTH, WIDTH) * block
             held = value[j * block : (j + 1) * block]
-            result[pl.ds(pl.multiple_of(first, block), block), sides[0]] = held[:, :half]
-            result[pl.ds(pl.multiple_of(first, block), block), sides[1]] = held[:, half:]
+            start[pl.ds(pl.multiple_of(first, block), block), sides[0]] = held[:, :half]
+            start[pl.ds(pl.multiple_of(first, block), block), sides[1]] = held[:, half:]
+        slab = pl.ds(pl.multiple_of(base, rows), rows)
+        stores.append(pltpu.make_async_copy(start.at[slab, :], result.at[slab, :], out_sems.at[s]))
+        stores[s].start()
     kept = rotation.shape[0]
-    rotation[...] = result[pl.ds(pl.multiple_of(member * kept, kept), kept), :]
+    rotation[...] = start[pl.ds(pl.multiple_of(member * kept, kept), kept), :]
+    for store in stores:
+        store.wait()
 
 
 def polar(place, owns, others, block_rows):
@@ -189,12 +196,12 @@
     return pl.pallas_call(
         polar_kernel,
         out_shape=(
-            jax.ShapeDtypeStruct(whole, BF16),
+            pltpu.HBM(whole, BF16),
             jax.ShapeDtypeStruct((block_rows, features), BF16),
         ),
         in_specs=[pl.BlockSpec(memory_space=pltpu.SMEM), pl.BlockSpec(memory_space=pl.ANY)]
         + [vmem] * (2 * WIDTH - 1),
-        out_specs=(vmem, vmem),
+        out_specs=(pl.BlockSpec(memory_space=pl.ANY), vmem),
         scratch_shapes=[
             pltpu.VMEM(whole, BF16),
             pltpu.VMEM(whole, BF16),
@@ -202,6 +209,7 @@
             pltpu.VMEM(whole, BF16),
             pltpu.VMEM(whole, BF16),
             pltpu.SemaphoreType.DMA,
+            pltpu.SemaphoreType.DMA((WIDTH,)),
         ],
         compiler_params=pltpu.CompilerParams(vmem_limit_bytes=24 * 1024 * 1024),
         cost_estimate=pl.CostEstimate(flops=13 * features**3, bytes_accessed=2**22, transcendentals=0),
@@ -209,21 +217,22 @@
     )(place, *owns, *others)
 
 
-def rotate_kernel(rows, factor, out, held, product, in_sems, out_sems):
-    block = held.shape[1]
-    parts = range(held.shape[0])
+def rotate_kernel(rows, factor, out, weights, product, in_sems, out_sems):
+    block = rows.shape[1] // in_sems.shape[0]
+    parts = range(in_sems.shape[0])
+    columns = [pl.ds(k * block, block) for k in parts]
 
     def fetch(k):
-        return pltpu.make_async_copy(rows.at[pl.ds(k * block, block), :], held.at[k], in_sems.at[k])
+        return pltpu.make_async_copy(factor.at[:, columns[k]], weights.at[:, columns[k]], in_sems.at[k])
 
     def store(k):
-        return pltpu.make_async_copy(product.at[k], out.at[pl.ds(k * block, block), :], out_sems.at[k])
+        return pltpu.make_async_copy(product.at[:, columns[k]], out.at[:, columns[k]], out_sems.at[k])
 
     for k in parts:
         fetch(k).start()
     for k in parts:
         fetch(k).wait()
-        product[k] = jnp.dot(held[k], factor[...], preferred_element_type=F32)
+        product[:, columns[k]] = jnp.dot(rows[...], weights[:, columns[k]], preferred_element_type=F32)
         store(k).start()
     for k in parts:
         store(k).wait()
@@ -232,15 +241,15 @@
 def rotate(rows, factor):
     count, features = rows.shape
     parts = 4
-    block = count // parts
+    anywhere = pl.BlockSpec(memory_space=pl.ANY)
     return pl.pallas_call(
         rotate_kernel,
         out_shape=jax.ShapeDtypeStruct((count, features), F32),
-        in_specs=[pl.BlockSpec(memory_space=pltpu.HBM), pl.BlockSpec(memory_space=pltpu.VMEM)],
-        out_specs=pl.BlockSpec(memory_space=pltpu.HBM),
+        in_specs=[pl.BlockSpec(memory_space=pltpu.VMEM), anywhere],
+        out_specs=anywhere,
         scratch_shapes=[
-            pltpu.VMEM((parts, block, features), BF16),
-            pltpu.VMEM((parts, block, features), F32),
+            pltpu.VMEM((features, features), BF16),
+            pltpu.VMEM((count, features), F32),
             pltpu.SemaphoreType.DMA((parts,)),
             pltpu.SemaphoreType.DMA((parts,)),
         ],
@@ -264,6 +273,7 @@
     owns = gather_shifts(slab, "y")
     others = [swap_core(own) for own in owns]
     factor, own_rows = polar(place, owns, others, features // members)
+    factor = pltpu.with_memory_space_constraint(factor, pltpu.HBM)
     return (rotate(received, factor), own_rows)
 
 

time: 95.4 us -> 95.3 us (level)
  local copies, waits for them, and re-layouts: 6.02 us -> 3.12 us
  Pallas kernels: 16 us -> 18.8 us
    unnamed x15 -> x11, local copies, waits for them, and re-layouts: 2.95 us -> 0.05 us
    pallas_call x1, Pallas kernels: 2.75 us -> 4.67 us  [rotate(): pl.pallas_call(rotate_kernel, out_shape=jax.ShapeDtypeStruct((count, feat...]
  transfers between devices with their start and end apart: 15 -> 15, of which waited for: 4 -> 4; matrix products, arithmetic and copies ran while one was open for 5% -> 5% of each run, Pallas kernels for 13% -> 14%
where the time goes in v10:
time: 95.3 us; the launch traced here: 94.7 us
  starting transfers between devices  42.3 us (44%)
  waiting for transfers between devices  25.9 us (27%)
  Pallas kernels  18.8 us (20%)
  matrix products  3.39 us (4%)
  local copies, waits for them, and re-layouts  3.12 us (3%)
  between operations  1 us (1%)
    all_to_all x3, waiting for transfers between devices, exchange(): return lax.all_to_all(value, axes, split_axis=0, concat_axis=0, tiled=True)  23.7 us
    all_to_all x3, starting transfers between devices, exchange(): return lax.all_to_all(value, axes, split_axis=0, concat_axis=0, tiled=True)  20 us
    ppermute x6, starting transfers between devices, swap_core(): return lax.ppermute(value, 'core', [(0, 1), (1, 0)])  18.4 us
    pallas_call x1, Pallas kernels, polar(): pl.pallas_call(polar_kernel, out_shape=(pltpu.HBM(whole, BF16), jax.Shape...  13.2 us
    pallas_call x1, Pallas kernels, rotate(): pl.pallas_call(rotate_kernel, out_shape=jax.ShapeDtypeStruct((count, feat...  4.67 us
    ppermute x6, starting transfers between devices, gather_shifts(): lax.ppermute(value, axis, steps[s])  3.82 us
    dot_general x3, matrix products, dot(): return jnp.dot(a, b, preferred_element_type=F32)  3.39 us
  transfers between devices with their start and end apart: 15, of which 4 were waited for; matrix products, arithmetic and copies ran while one was open for 5% of the time, Pallas kernels for 14%

profile of v10, /device:TPU:1, one launch (start us, length us, event | category | flops | bytes accessed | tf_op | source)
XLA Modules:
  0.0 94.7 jit_solution(17330841361472475174)
XLA Ops:
  0.6 0.0 copy-start
  0.6 3.3 %collective-permute-start.1 = (bf16[256,1024]{1,0:T(8,128)(2,1)}, bf16[256,1024]{1,0:T(8,128)(2,1)S(1)}, u32[]{:S(2)}, u32[]{:S(2)}) collective-permute-start(bf16[256,1024]{1,0:T(8,128)(2,1)} %param.4), channel_id=1, source_target_pairs={{0,32},{32,0},{1,33},{33,1},{2,34},{34,2},{3,35},{35,3},{4,36},{36... | collective-permute-start | bytes 1572872 | tf_op jit(solution)/shard_map/ppermute | solution.py:31
  4.0 0.0 copy-done
  4.0 1.0 %collective-permute-start = (bf16[256,512]{1,0:T(8,128)(2,1)S(1)}, bf16[256,512]{1,0:T(8,128)(2,1)S(1)}, u32[]{:S(2)}, u32[]{:S(2)}) collective-permute-start(bf16[256,512]{1,0:T(8,128)(2,1)S(1)} %constant_dynamic-slice_fusion), channel_id=1, source_target_pairs={{0,32},{32,0},{1,33},{33,1},{2,34},{34,2},{3,35},{35,3},{4,36},{36... | collective-permute-start | bytes 786440 | tf_op jit(solution)/shard_map/ppermute | solution.py:31
  5.0 1.5 %fusion.2 = f32[512,1024]{1,0:T(8,128)S(1)} fusion(bf16[256,1024]{1,0:T(8,128)(2,1)} %param.4, bf16[256,1024]{1,0:T(8,128)(2,1)S(1)} %copy-done, s32[]{:T(128)S(6)} %select_n.9), kind=kOutput, calls=%fused_computation.8 | convolution fusion | flops 268435456 | bytes 2883588 | tf_op jit(solution)/shard_map/dot_general | solution.py:27
  6.5 0.0 collective-permute-done
  6.6 0.0 collective-permute-done.1
  6.6 0.5 fusion
  7.0 0.0 copy-start.3
  7.0 0.0 copy-start.1
  7.0 1.3 %copy.8 = bf16[1024,512]{1,0:T(8,128)(2,1)} copy(bf16[1024,512]{0,1:T(8,128)(2,1)S(1)} %fusion) | data formatting | bytes 2097152 | tf_op jit(solution)/shard_map/convert_element_type | solution.py:103
  8.4 0.0 copy-start.2
  8.4 6.8 %all-to-all-start = ((bf16[32,32,512]{2,1,0:T(8,128)(2,1)}), bf16[32,32,512]{2,1,0:T(8,128)(2,1)S(1)}, u32[]{:S(2)}, u32[]{:S(2)}) async-start(bf16[32,32,512]{2,1,0:T(8,128)(2,1)} %bitcast.1), calls=%async_computation | async-start | bytes 2097152 | tf_op jit(solution)/shard_map/all_to_all | solution.py:35
  15.2 0.0 copy-done.3
  15.2 0.0 copy-done.1
  15.2 1.7 %gather_fusion = s32[256]{0:T(256)S(1)} fusion(s32[65536]{0:T(1024)S(1)} %copy-done.1, s32[1024]{0:T(1024)S(1)} %pad_clamp_fusion), kind=kCustom, calls=%fused_computation | custom fusion | bytes 3072 | tf_op jit(solution)/shard_map/gather | solution.py:41
  17.0 0.2 convert_reduce_fusion
  17.1 15.4 %all-to-all-done.terms = bf16[32,32,512]{2,1,0:T(8,128)(2,1)S(1)} async-done(((bf16[32,32,512]{2,1,0:T(8,128)(2,1)}), bf16[32,32,512]{2,1,0:T(8,128)(2,1)S(1)}, u32[]{:S(2)}, u32[]{:S(2)}) %all-to-all-start) | async-done | bytes 1048608 | tf_op jit(solution)/shard_map/all_to_all | solution.py:35
  32.6 0.8 sum_and_copy.1
  33.4 7.3 %all-to-all-start.1 = ((bf16[8,32,512]{2,1,0:T(8,128)(2,1)}), bf16[8,32,512]{2,1,0:T(8,128)(2,1)S(1)}, u32[]{:S(2)}, u32[]{:S(2)}) async-start(bf16[8,32,512]{2,1,0:T(8,128)(2,1)} %sum_and_copy.1), calls=%async_computation.1 | async-start | bytes 524288 | tf_op jit(solution)/shard_map/all_to_all | solution.py:35
  40.7 0.0 copy-done.2
  40.7 1.4 %convolution_convert_fusion = bf16[512,1024]{1,0:T(8,128)(2,1)} fusion(bf16[256,1024]{1,0:T(8,128)(2,1)S(1)} %copy-done.2, s32[256]{0:T(256)S(1)} %multiply_add_fusion), kind=kOutput, calls=%fused_computation.2 | convolution fusion | flops 269090816 | bytes 1573888 | tf_op jit(solution)/shard_map/dot_general | solution.py:27
  42.1 8.3 %all-to-all-done.1.terms = bf16[8,32,512]{2,1,0:T(8,128)(2,1)S(1)} async-done(((bf16[8,32,512]{2,1,0:T(8,128)(2,1)}), bf16[8,32,512]{2,1,0:T(8,128)(2,1)S(1)}, u32[]{:S(2)}, u32[]{:S(2)}) %all-to-all-start.1) | async-done | bytes 262176 | tf_op jit(solution)/shard_map/all_to_all | solution.py:35
  50.5 0.7 collective-permute-start.4
  51.2 1.5 %collective-permute-start.3 = (bf16[64,512]{1,0:T(8,128)(2,1)S(1)}, bf16[64,512]{1,0:T(8,128)(2,1)S(1)}, u32[]{:S(2)}, u32[]{:S(2)}) collective-permute-start(bf16[64,512]{1,0:T(8,128)(2,1)S(1)} %sum_pairs.1), channel_id=1, source_target_pairs={{0,16},{8,24},{16,0},{24,8},{1,17},{9,25},{17,1},{25,9},{2,18},{10... | collective-permute-start | bytes 196616 | tf_op jit(solution)/shard_map/ppermute | solution.py:114
  52.8 0.0 collective-permute-start.2
  52.8 6.0 %all-to-all-start.2 = ((bf16[32,16,1024]{2,1,0:T(8,128)(2,1)}), bf16[32,16,1024]{2,1,0:T(8,128)(2,1)S(1)}, u32[]{:S(2)}, u32[]{:S(2)}) async-start(bf16[32,16,1024]{2,1,0:T(8,128)(2,1)} %bitcast.2), calls=%async_computation.2 | async-start | bytes 2097152 | tf_op jit(solution)/shard_map/all_to_all | solution.py:35
  58.7 0.0 collective-permute-done.2
  58.8 0.0 collective-permute-done.3
  58.8 0.0 collective-permute-done.4
  58.8 0.7 collective-permute-start.7
  59.5 0.0 collective-permute-start.6
  59.5 0.8 collective-permute-start.5
  60.4 3.8 %collective-permute-start.8 = (bf16[256,512]{1,0:T(8,128)(2,1)S(1)}, bf16[256,512]{1,0:T(8,128)(2,1)S(1)}, u32[]{:S(2)}, u32[]{:S(2)}) collective-permute-start(bf16[256,512]{1,0:T(8,128)(2,1)S(1)} %constant_dynamic-update-slice_fusion.refs_0_), channel_id=1, source_target_pairs={{0,32},{32,0},{1,33},{33,1},{2,34},{34,2},{3,35},{35,3},{4,36},{36... | collective-permute-start | bytes 786440 | tf_op jit(solution)/shard_map/ppermute | solution.py:31
  64.2 0.0 collective-permute-done.7.refs_3_
  64.2 6.2 %collective-permute-start.11 = (bf16[256,512]{1,0:T(8,128)(2,1)S(1)}, bf16[256,512]{1,0:T(8,128)(2,1)S(1)}, u32[]{:S(2)}, u32[]{:S(2)}) collective-permute-start(bf16[256,512]{1,0:T(8,128)(2,1)S(1)} %collective-permute-done.7.refs_3_), channel_id=1, source_target_pairs={{0,32},{32,0},{1,33},{33,1},{2,34},{34,2},{3,35},{35,3},{4,36},{36... | collective-permute-start | bytes 786440 | tf_op jit(solution)/shard_map/ppermute | solution.py:31
  70.4 0.0 collective-permute-done.6.refs_2_
  70.4 2.3 %collective-permute-start.10 = (bf16[256,512]{1,0:T(8,128)(2,1)S(1)}, bf16[256,512]{1,0:T(8,128)(2,1)S(1)}, u32[]{:S(2)}, u32[]{:S(2)}) collective-permute-start(bf16[256,512]{1,0:T(8,128)(2,1)S(1)} %collective-permute-done.6.refs_2_), channel_id=1, source_target_pairs={{0,32},{32,0},{1,33},{33,1},{2,34},{34,2},{3,35},{35,3},{4,36},{36... | collective-permute-start | bytes 786440 | tf_op jit(solution)/shard_map/ppermute | solution.py:31
  72.7 0.9 collective-permute-done.5.refs_1_
  73.6 1.7 %collective-permute-start.9 = (bf16[256,512]{1,0:T(8,128)(2,1)S(1)}, bf16[256,512]{1,0:T(8,128)(2,1)}, u32[]{:S(2)}, u32[]{:S(2)}) collective-permute-start(bf16[256,512]{1,0:T(8,128)(2,1)S(1)} %collective-permute-done.5.refs_1_), channel_id=1, source_target_pairs={{0,32},{32,0},{1,33},{33,1},{2,34},{34,2},{3,35},{35,3},{4,36},{36... | collective-permute-start | bytes 786440 | tf_op jit(solution)/shard_map/ppermute | solution.py:31
  75.4 0.1 pad_add_fusion.place
  75.4 0.0 collective-permute-done.8.refs_4_
  75.4 0.0 collective-permute-done.11.refs_7_
  75.4 0.0 collective-permute-done.10.refs_6_
  75.5 1.2 %collective-permute-done.9.refs_5_ = bf16[256,512]{1,0:T(8,128)(2,1)} collective-permute-done((bf16[256,512]{1,0:T(8,128)(2,1)S(1)}, bf16[256,512]{1,0:T(8,128)(2,1)}, u32[]{:S(2)}, u32[]{:S(2)}) %collective-permute-start.9) | collective-permute-done | bytes 262176 | tf_op jit(solution)/shard_map/ppermute | solution.py:31
  76.7 13.2 %polar.1 = (bf16[1024,1024]{1,0:T(8,128)(2,1)}, bf16[32,1024]{1,0:T(8,128)(2,1)}) custom-call(s32[4]{0:T(128)S(1)} %pad_add_fusion.place, bf16[256,512]{1,0:T(8,128)(2,1)S(1)} %constant_dynamic-update-slice_fusion.refs_0_, bf16[256,512]{1,0:T(8,128)(2,1)S(1)} %collective-permute-done.5.refs_1_, bf16[256,512]{1,0:T(8,128)(2,1)S(1)} %collective-permute-done.6.refs_2_, ...), custom_call_target="tpu_custom_call" | custom-call | flops 13958643712 | bytes 4194304 | tf_op jit(solution)/shard_map/polar/pallas_call | solution.py:196
  89.9 0.0 all-to-all-done.2
  89.9 4.7 %rotate.1 = f32[512,1024]{1,0:T(8,128)} custom-call(bf16[512,1024]{1,0:T(8,128)(2,1)S(1)} %bitcast.13, bf16[1024,1024]{1,0:T(8,128)(2,1)} %get-tuple-element.8.factor), custom_call_target="tpu_custom_call" | custom-call | flops 1073741824 | bytes 5242880 | tf_op jit(solution)/shard_map/rotate/pallas_call | solution.py:245
  (9 shorter events, 0.1 us)
Async XLA Ops:
  0.6 3.3 %copy-start = (bf16[256,1024]{1,0:T(8,128)(2,1)S(1)}, bf16[256,1024]{1,0:T(8,128)(2,1)}, u32[]{:S(2)}) copy-start(bf16[256,1024]{1,0:T(8,128)(2,1)} %param.5) | copy-start | bytes 1572868
  0.6 5.9 %collective-permute-start.1 = (bf16[256,1024]{1,0:T(8,128)(2,1)}, bf16[256,1024]{1,0:T(8,128)(2,1)S(1)}, u32[]{:S(2)}, u32[]{:S(2)}) collective-permute-start(bf16[256,1024]{1,0:T(8,128)(2,1)} %param.4), channel_id=1, source_target_pairs={{0,32},{32,0},{1,33},{33,1},{2,34},{34,2},{3,35},{35,3},{4,36},{36... | collective-permute-start | bytes 1572872 | tf_op jit(solution)/shard_map/ppermute | solution.py:31
  4.0 2.5 %collective-permute-start = (bf16[256,512]{1,0:T(8,128)(2,1)S(1)}, bf16[256,512]{1,0:T(8,128)(2,1)S(1)}, u32[]{:S(2)}, u32[]{:S(2)}) collective-permute-start(bf16[256,512]{1,0:T(8,128)(2,1)S(1)} %constant_dynamic-slice_fusion), channel_id=1, source_target_pairs={{0,32},{32,0},{1,33},{33,1},{2,34},{34,2},{3,35},{35,3},{4,36},{36... | collective-permute-start | bytes 786440 | tf_op jit(solution)/shard_map/ppermute | solution.py:31
  7.0 8.2 %copy-start.3 = (s32[256]{0:T(256)S(1)}, s32[256]{0:T(256)}, u32[]{:S(2)}) copy-start(s32[256]{0:T(256)} %param.6) | copy-start | bytes 3076
  7.0 8.2 %copy-start.1 = (s32[65536]{0:T(1024)S(1)}, s32[65536]{0:T(1024)}, u32[]{:S(2)}) copy-start(s32[65536]{0:T(1024)} %param.7) | copy-start | bytes 786436
  8.4 32.3 %copy-start.2 = (bf16[256,1024]{1,0:T(8,128)(2,1)S(1)}, bf16[256,1024]{1,0:T(8,128)(2,1)}, u32[]{:S(2)}) copy-start(bf16[256,1024]{1,0:T(8,128)(2,1)} %param.4) | copy-start | bytes 1572868
  8.4 24.2 %all-to-all-start = ((bf16[32,32,512]{2,1,0:T(8,128)(2,1)}), bf16[32,32,512]{2,1,0:T(8,128)(2,1)S(1)}, u32[]{:S(2)}, u32[]{:S(2)}) async-start(bf16[32,32,512]{2,1,0:T(8,128)(2,1)} %bitcast.1), calls=%async_computation | async-start | bytes 2097152 | tf_op jit(solution)/shard_map/all_to_all | solution.py:35
  33.4 17.0 %all-to-all-start.1 = ((bf16[8,32,512]{2,1,0:T(8,128)(2,1)}), bf16[8,32,512]{2,1,0:T(8,128)(2,1)S(1)}, u32[]{:S(2)}, u32[]{:S(2)}) async-start(bf16[8,32,512]{2,1,0:T(8,128)(2,1)} %sum_and_copy.1), calls=%async_computation.1 | async-start | bytes 524288 | tf_op jit(solution)/shard_map/all_to_all | solution.py:35
  50.5 8.3 %collective-permute-start.4 = (bf16[64,512]{1,0:T(8,128)(2,1)S(1)}, bf16[64,512]{1,0:T(8,128)(2,1)S(1)}, u32[]{:S(2)}, u32[]{:S(2)}) collective-permute-start(bf16[64,512]{1,0:T(8,128)(2,1)S(1)} %sum_pairs.1), channel_id=1, source_target_pairs={{0,24},{8,0},{16,8},{24,16},{1,25},{9,1},{17,9},{25,17},{2,26},{10... | collective-permute-start | bytes 196616 | tf_op jit(solution)/shard_map/ppermute | solution.py:114
  51.2 7.5 %collective-permute-start.3 = (bf16[64,512]{1,0:T(8,128)(2,1)S(1)}, bf16[64,512]{1,0:T(8,128)(2,1)S(1)}, u32[]{:S(2)}, u32[]{:S(2)}) collective-permute-start(bf16[64,512]{1,0:T(8,128)(2,1)S(1)} %sum_pairs.1), channel_id=1, source_target_pairs={{0,16},{8,24},{16,0},{24,8},{1,17},{9,25},{17,1},{25,9},{2,18},{10... | collective-permute-start | bytes 196616 | tf_op jit(solution)/shard_map/ppermute | solution.py:114
  52.8 6.0 %collective-permute-start.2 = (bf16[64,512]{1,0:T(8,128)(2,1)S(1)}, bf16[64,512]{1,0:T(8,128)(2,1)S(1)}, u32[]{:S(2)}, u32[]{:S(2)}) collective-permute-start(bf16[64,512]{1,0:T(8,128)(2,1)S(1)} %sum_pairs.1), channel_id=1, source_target_pairs={{0,8},{8,16},{16,24},{24,0},{1,9},{9,17},{17,25},{25,1},{2,10},{10... | collective-permute-start | bytes 196616 | tf_op jit(solution)/shard_map/ppermute | solution.py:114
  52.8 37.1 %all-to-all-start.2 = ((bf16[32,16,1024]{2,1,0:T(8,128)(2,1)}), bf16[32,16,1024]{2,1,0:T(8,128)(2,1)S(1)}, u32[]{:S(2)}, u32[]{:S(2)}) async-start(bf16[32,16,1024]{2,1,0:T(8,128)(2,1)} %bitcast.2), calls=%async_computation.2 | async-start | bytes 2097152 | tf_op jit(solution)/shard_map/all_to_all | solution.py:35
  58.8 5.4 %collective-permute-start.7 = (bf16[256,512]{1,0:T(8,128)(2,1)S(1)}, bf16[256,512]{1,0:T(8,128)(2,1)S(1)}, u32[]{:S(2)}, u32[]{:S(2)}) collective-permute-start(bf16[256,512]{1,0:T(8,128)(2,1)S(1)} %constant_dynamic-update-slice_fusion.refs_0_), channel_id=1, source_target_pairs={{0,192},{64,0},{128,64},{192,128},{1,193},{65,1},{129,65},{193,129... | collective-permute-start | bytes 786440 | tf_op jit(solution)/shard_map/ppermute | solution.py:114
  59.5 10.9 %collective-permute-start.6 = (bf16[256,512]{1,0:T(8,128)(2,1)S(1)}, bf16[256,512]{1,0:T(8,128)(2,1)S(1)}, u32[]{:S(2)}, u32[]{:S(2)}) collective-permute-start(bf16[256,512]{1,0:T(8,128)(2,1)S(1)} %constant_dynamic-update-slice_fusion.refs_0_), channel_id=1, source_target_pairs={{0,128},{64,192},{128,0},{192,64},{1,129},{65,193},{129,1},{193,65... | collective-permute-start | bytes 786440 | tf_op jit(solution)/shard_map/ppermute | solution.py:114
  59.5 14.1 %collective-permute-start.5 = (bf16[256,512]{1,0:T(8,128)(2,1)S(1)}, bf16[256,512]{1,0:T(8,128)(2,1)S(1)}, u32[]{:S(2)}, u32[]{:S(2)}) collective-permute-start(bf16[256,512]{1,0:T(8,128)(2,1)S(1)} %constant_dynamic-update-slice_fusion.refs_0_), channel_id=1, source_target_pairs={{0,64},{64,128},{128,192},{192,0},{1,65},{65,129},{129,193},{193,1... | collective-permute-start | bytes 786440 | tf_op jit(solution)/shard_map/ppermute | solution.py:114
  60.4 15.1 %collective-permute-start.8 = (bf16[256,512]{1,0:T(8,128)(2,1)S(1)}, bf16[256,512]{1,0:T(8,128)(2,1)S(1)}, u32[]{:S(2)}, u32[]{:S(2)}) collective-permute-start(bf16[256,512]{1,0:T(8,128)(2,1)S(1)} %constant_dynamic-update-slice_fusion.refs_0_), channel_id=1, source_target_pairs={{0,32},{32,0},{1,33},{33,1},{2,34},{34,2},{3,35},{35,3},{4,36},{36... | collective-permute-start | bytes 786440 | tf_op jit(solution)/shard_map/ppermute | solution.py:31
  64.2 11.3 %collective-permute-start.11 = (bf16[256,512]{1,0:T(8,128)(2,1)S(1)}, bf16[256,512]{1,0:T(8,128)(2,1)S(1)}, u32[]{:S(2)}, u32[]{:S(2)}) collective-permute-start(bf16[256,512]{1,0:T(8,128)(2,1)S(1)} %collective-permute-done.7.refs_3_), channel_id=1, source_target_pairs={{0,32},{32,0},{1,33},{33,1},{2,34},{34,2},{3,35},{35,3},{4,36},{36... | collective-permute-start | bytes 786440 | tf_op jit(solution)/shard_map/ppermute | solution.py:31
  70.4 5.0 %collective-permute-start.10 = (bf16[256,512]{1,0:T(8,128)(2,1)S(1)}, bf16[256,512]{1,0:T(8,128)(2,1)S(1)}, u32[]{:S(2)}, u32[]{:S(2)}) collective-permute-start(bf16[256,512]{1,0:T(8,128)(2,1)S(1)} %collective-permute-done.6.refs_2_), channel_id=1, source_target_pairs={{0,32},{32,0},{1,33},{33,1},{2,34},{34,2},{3,35},{35,3},{4,36},{36... | collective-permute-start | bytes 786440 | tf_op jit(solution)/shard_map/ppermute | solution.py:31
  73.6 3.0 %collective-permute-start.9 = (bf16[256,512]{1,0:T(8,128)(2,1)S(1)}, bf16[256,512]{1,0:T(8,128)(2,1)}, u32[]{:S(2)}, u32[]{:S(2)}) collective-permute-start(bf16[256,512]{1,0:T(8,128)(2,1)S(1)} %collective-permute-done.5.refs_1_), channel_id=1, source_target_pairs={{0,32},{32,0},{1,33},{33,1},{2,34},{34,2},{3,35},{35,3},{4,36},{36... | collective-permute-start | bytes 786440 | tf_op jit(solution)/shard_map/ppermute | solution.py:31
